TPU v7x, 32 devices: a whole 2x2x4 slice. The times are simulated.
32 devices in a mesh: shard: 4 (over x, core), context: 2 (over y), tensor: 4 (over z).
Axes of the slice: x: 2, y: 2, z: 4, core: 2. Of those that a mesh axis runs over, the one named last changes fastest.
Arguments:
- tokens: bfloat16 [4, 1152, 2048], P('shard', ('context', 'tensor')), may hold values from -6 to 6
- cotangent: bfloat16 [4, 1152, 2048], P('shard', ('context', 'tensor')), may hold values from -6 to 6
- segments: int32 [4, 1152], P('shard'), may hold values from 0 to 4, as said below
- first_gain: bfloat16 [2048], P('shard'), may hold values from 0.099609375 to 1.8984375
- second_gain: bfloat16 [2048], P('shard'), may hold values from 0.099609375 to 1.8984375
- query_weight: bfloat16 [2048, 2048], P('shard', 'tensor'), may hold values from -0.25 to 0.25
- key_weight: bfloat16 [2048, 512], P('shard', 'tensor'), may hold values from -0.125 to 0.125
- value_weight: bfloat16 [2048, 512], P('shard', 'tensor'), may hold values from -0.125 to 0.125
- output_weight: bfloat16 [2048, 2048], P('shard', 'tensor'), may hold values from -1 to 1
- gate_weight: bfloat16 [2048, 8192], P('shard', 'tensor'), may hold values from -0.125 to 0.125
- up_matrix: bfloat16 [2048, 8192], P('shard', 'tensor'), may hold values from -0.125 to 0.125
- down_weight: bfloat16 [2048, 8192], P('shard', 'tensor'), may hold values from -0.125 to 0.125
Outputs:
- layer_output: bfloat16 [4, 1152, 2048], P('shard', ('context', 'tensor'))
- tokens_grad: bfloat16 [4, 1152, 2048], P('shard', ('context', 'tensor'))
- first_gain_grad: float32 [2048], P('shard')
- second_gain_grad: float32 [2048], P('shard')
- query_weight_grad: float32 [2048, 2048], P('shard', 'tensor')
- key_weight_grad: float32 [2048, 512], P('shard', 'tensor')
- value_weight_grad: float32 [2048, 512], P('shard', 'tensor')
- output_weight_grad: float32 [2048, 2048], P('shard', 'tensor')
- gate_weight_grad: float32 [2048, 8192], P('shard', 'tensor')
- up_weight_grad: float32 [2048, 8192], P('shard', 'tensor')
- down_weight_grad: float32 [2048, 8192], P('shard', 'tensor')
Inputs may be any that keep to these rules, and one draw needn't show every extreme that they name: segments[b, i] counts the document starts among positions 1 to i of sequence b (several may share a position), so it never falls along a sequence, is 0 at position 0 and 4 at the last position; no document starts after position 287 and before position 865.
All inputs are finite; a program needn't handle non-finite values.
Results may differ from a plain program's by a relative error of at most 0.025.
Values may be sent and summed in bfloat16 or wider, within the bound.
No kernel may reach another device: no remote copies, remote signals or barrier semaphores. Data moves between devices by JAX's collectives and lax.ppermute only.
A program may use at most 256 MiB of HBM per device.

v0:
```python
import jax
import jax.numpy as jnp
from jax import lax
from jax.sharding import PartitionSpec as P

H = 32
KV = 8
HD = 64


EPS = 1e-05
THETA = 500000.0
MASKED = -1e30


def positions_of(segments):
    index_row = jnp.arange(segments.shape[1], dtype=jnp.int32)
    changed = jnp.concatenate(
        [jnp.ones((segments.shape[0], 1), bool), segments[:, 1:] != segments[:, :-1]], axis=1
    )
    starts = lax.cummax(jnp.where(changed, index_row[None, :], 0), axis=1)
    return index_row[None, :] - starts


def rope_tables(positions):
    freq_index = jnp.arange(HD // 2, dtype=jnp.float32)
    inverse = THETA ** (-2.0 * freq_index / HD)
    angles = positions.astype(jnp.float32)[:, None] * inverse[None, :]
    cosines = jnp.cos(angles)
    sines = jnp.sin(angles)
    return (jnp.concatenate([cosines, cosines], axis=-1), jnp.concatenate([sines, sines], axis=-1))


def rotate(values, cosines, sines):
    middle = values.shape[-1] // 2
    turned = jnp.concatenate([-values[..., middle:], values[..., :middle]], axis=-1)
    return values * cosines + turned * sines


def unrotate(grads, cosines, sines):
    middle = grads.shape[-1] // 2
    rescaled_rows = grads * sines
    return grads * cosines + jnp.concatenate(
        [rescaled_rows[..., middle:], -rescaled_rows[..., :middle]], axis=-1
    )


def rms_scale(values):
    return lax.rsqrt(jnp.mean(values * values, axis=-1, keepdims=True) + EPS)


def project(rows, weight):
    return jnp.einsum("bld,dc->blc", rows, weight, preferred_element_type=jnp.float32)


def project_back(rows, weight):
    return jnp.einsum("blc,dc->bld", rows, weight, preferred_element_type=jnp.float32)


def weight_grad(rows, grads):
    return jnp.einsum("bld,blc->dc", rows, grads, preferred_element_type=jnp.float32)


def gather_weights(shard_pieces):
    return (
        lax.all_gather(shard_pieces[0], "shard", axis=0, tiled=True),
        lax.all_gather(shard_pieces[1], "shard", axis=0, tiled=True),
        lax.all_gather(shard_pieces[2], "shard", axis=0, tiled=True),
        lax.all_gather(shard_pieces[3], "shard", axis=0, tiled=True),
        lax.all_gather(shard_pieces[4], "shard", axis=0, tiled=True),
        lax.all_gather(shard_pieces[5], "shard", axis=0, tiled=True),
        lax.all_gather(shard_pieces[6], "shard", axis=0, tiled=True),
        lax.all_gather(shard_pieces[7], "shard", axis=0, tiled=True),
        lax.all_gather(shard_pieces[8], "shard", axis=0, tiled=True),
    )


def gather_rows(values):
    return lax.all_gather(values, "tensor", axis=1, tiled=True)


def sum_rows(values):
    return lax.psum_scatter(
        values.astype(jnp.bfloat16), "tensor", scatter_dimension=1, tiled=True
    ).astype(jnp.float32)


def prepare_heads(query_seq, keyval_seq, seg_row, pos_row):
    seq_len, groups = (query_seq.shape[0], query_seq.shape[1])
    cosines, sines = rope_tables(pos_row)
    query_f = query_seq.reshape(seq_len, groups, H // KV, HD).astype(jnp.float32)
    query_rot = rotate(query_f, cosines[:, None, None, :], sines[:, None, None, :]).astype(
        jnp.bfloat16
    )
    key_rot = rotate(
        keyval_seq[..., :HD].astype(jnp.float32), cosines[:, None, :], sines[:, None, :]
    ).astype(jnp.bfloat16)
    value_part = keyval_seq[..., HD:]
    scores = jnp.einsum(
        "lkga,mka->kglm", query_rot, key_rot, preferred_element_type=jnp.float32
    ) * HD ** (-0.5)
    index_row = jnp.arange(seq_len, dtype=jnp.int32)
    allowed = (seg_row[:, None] == seg_row[None, :]) & (index_row[None, :] <= index_row[:, None])
    scores = jnp.where(allowed, scores, MASKED)
    return (query_rot, key_rot, value_part, scores, cosines, sines)


def attend_forward(items):
    query_seq, keyval_seq, seg_row, pos_row = items
    seq_len, groups = (query_seq.shape[0], query_seq.shape[1])
    query_rot, key_rot, value_part, scores, cosines, sines = prepare_heads(
        query_seq, keyval_seq, seg_row, pos_row
    )
    top_score = jnp.max(scores, axis=-1, keepdims=True)
    row_total = jnp.sum(jnp.exp(scores - top_score), axis=-1, keepdims=True)
    log_total = top_score + jnp.log(row_total)
    probs = jnp.exp(scores - log_total).astype(jnp.bfloat16)
    attended = jnp.einsum("kglm,mka->lkga", probs, value_part, preferred_element_type=jnp.float32)
    return (attended.astype(jnp.bfloat16).reshape(seq_len, groups, -1), log_total[..., 0])


def attend_backward(items):
    query_seq, keyval_seq, grad_seq, log_total, seg_row, pos_row = items
    seq_len, groups = (query_seq.shape[0], query_seq.shape[1])
    query_rot, key_rot, value_part, scores, cosines, sines = prepare_heads(
        query_seq, keyval_seq, seg_row, pos_row
    )
    probs = jnp.exp(scores - log_total[..., None])
    grad_heads = grad_seq.reshape(seq_len, groups, H // KV, HD)
    grad_probs = jnp.einsum(
        "lkga,mka->kglm", grad_heads, value_part, preferred_element_type=jnp.float32
    )
    delta = jnp.sum(probs * grad_probs, axis=-1, keepdims=True)
    grad_scores = (probs * (grad_probs - delta)).astype(jnp.bfloat16)
    grad_query_rot = jnp.einsum(
        "kglm,mka->lkga", grad_scores, key_rot, preferred_element_type=jnp.float32
    ) * HD ** (-0.5)
    grad_key_rot = jnp.einsum(
        "kglm,lkga->mka", grad_scores, query_rot, preferred_element_type=jnp.float32
    ) * HD ** (-0.5)
    grad_value = jnp.einsum(
        "kglm,lkga->mka", probs.astype(jnp.bfloat16), grad_heads, preferred_element_type=jnp.float32
    )
    grad_query = unrotate(
        grad_query_rot, cosines[:, None, None, :], sines[:, None, None, :]
    ).astype(jnp.bfloat16)
    grad_key = unrotate(grad_key_rot, cosines[:, None, :], sines[:, None, :]).astype(jnp.bfloat16)
    grad_keyval = jnp.concatenate([grad_key, grad_value.astype(jnp.bfloat16)], axis=-1)
    return (grad_query.reshape(seq_len, groups, -1), grad_keyval)


def norm_backward(gradient_of_normed, input_rows, row_scales, gain_full):
    normalized_rows = input_rows * row_scales
    rescaled_rows = gradient_of_normed * gain_full
    gradient_of_input = row_scales * (
        rescaled_rows
        - normalized_rows * jnp.mean(rescaled_rows * normalized_rows, axis=-1, keepdims=True)
    )
    return (gradient_of_input, jnp.sum(gradient_of_normed * normalized_rows, axis=(0, 1)))


def shards(
    tokens,
    cotangent,
    segments,
    first_gain,
    second_gain,
    query_weight,
    key_weight,
    value_weight,
    output_weight,
    gate_weight,
    up_matrix,
    down_weight,
):
    shard_pieces = (
        first_gain,
        second_gain,
        query_weight,
        key_weight,
        value_weight,
        output_weight,
        gate_weight,
        up_matrix,
        down_weight,
    )
    gain_one, gain_two, w_query, w_key, w_value, w_output, w_gate, w_up, w_down = gather_weights(
        shard_pieces
    )
    gain_one_f = gain_one.astype(jnp.float32)
    gain_two_f = gain_two.astype(jnp.float32)
    tokens_f = tokens.astype(jnp.float32)
    scale_one = rms_scale(tokens_f)
    normed_one = (tokens_f * scale_one * gain_one_f).astype(jnp.bfloat16)
    normed_all = gather_rows(normed_one)
    batch, local_len = (normed_all.shape[0], normed_all.shape[1])
    kv_local = w_key.shape[1] // HD
    query_proj = project(normed_all, w_query).astype(jnp.bfloat16)
    key_proj = project(normed_all, w_key).astype(jnp.bfloat16)
    value_proj = project(normed_all, w_value).astype(jnp.bfloat16)
    query_pack = query_proj.reshape(batch, local_len, kv_local, -1)
    keyval_pack = jnp.concatenate(
        [
            key_proj.reshape(batch, local_len, kv_local, HD),
            value_proj.reshape(batch, local_len, kv_local, HD),
        ],
        axis=-1,
    )
    query_heads, keyval_heads = (
        lax.all_to_all(query_pack, "context", split_axis=2, concat_axis=1, tiled=True),
        lax.all_to_all(keyval_pack, "context", split_axis=2, concat_axis=1, tiled=True),
    )
    positions = positions_of(segments)
    context_heads, log_totals = lax.map(
        attend_forward, (query_heads, keyval_heads, segments, positions)
    )
    context_rows = lax.all_to_all(context_heads, "context", split_axis=1, concat_axis=2, tiled=True)
    context_flat = context_rows.reshape(batch, local_len, -1)
    attn_rows = sum_rows(project_back(context_flat, w_output))
    hidden_one = tokens_f + attn_rows
    scale_two = rms_scale(hidden_one)
    normed_two = (hidden_one * scale_two * gain_two_f).astype(jnp.bfloat16)
    normed_two_all = gather_rows(normed_two)
    gate_rows = project(normed_two_all, w_gate)
    up_rows = project(normed_two_all, w_up)
    sig_gate = jax.nn.sigmoid(gate_rows)
    silu_gate = gate_rows * sig_gate
    hidden_mid = (silu_gate * up_rows).astype(jnp.bfloat16)
    ffn_rows = sum_rows(project_back(hidden_mid, w_down))
    layer_output = (hidden_one + ffn_rows).astype(jnp.bfloat16)
    gain_one, gain_two, w_query, w_key, w_value, w_output, w_gate, w_up, w_down = gather_weights(
        shard_pieces
    )
    gain_one_f = gain_one.astype(jnp.float32)
    gain_two_f = gain_two.astype(jnp.float32)
    cot_f = cotangent.astype(jnp.float32)
    down_grad_all = gather_rows(cotangent)
    grad_down_w = weight_grad(down_grad_all, hidden_mid)
    grad_hidden = project(down_grad_all, w_down)
    grad_gate = (grad_hidden * up_rows * sig_gate * (1.0 + gate_rows * (1.0 - sig_gate))).astype(
        jnp.bfloat16
    )
    grad_up = (grad_hidden * silu_gate).astype(jnp.bfloat16)
    grad_gate_w = weight_grad(normed_two_all, grad_gate)
    grad_up_w = weight_grad(normed_two_all, grad_up)
    normed_two_grad = sum_rows(project_back(grad_gate, w_gate) + project_back(grad_up, w_up))
    norm_two_back, gain_two_part = norm_backward(normed_two_grad, hidden_one, scale_two, gain_two_f)
    resid_grad = cot_f + norm_two_back
    attn_grad_all = gather_rows(resid_grad.astype(jnp.bfloat16))
    grad_output_w = weight_grad(attn_grad_all, context_flat)
    context_grad = (
        project(attn_grad_all, w_output)
        .astype(jnp.bfloat16)
        .reshape(batch, local_len, kv_local, -1)
    )
    context_grad_heads = lax.all_to_all(
        context_grad, "context", split_axis=2, concat_axis=1, tiled=True
    )
    query_grad_heads, keyval_grad_heads = lax.map(
        attend_backward,
        (query_heads, keyval_heads, context_grad_heads, log_totals, segments, positions),
    )
    query_grad, keyval_grad = (
        lax.all_to_all(query_grad_heads, "context", split_axis=1, concat_axis=2, tiled=True),
        lax.all_to_all(keyval_grad_heads, "context", split_axis=1, concat_axis=2, tiled=True),
    )
    query_grad = query_grad.reshape(batch, local_len, -1)
    key_grad = keyval_grad[..., :HD].reshape(batch, local_len, -1)
    value_grad = keyval_grad[..., HD:].reshape(batch, local_len, -1)
    grad_query_w = weight_grad(normed_all, query_grad)
    grad_key_w = weight_grad(normed_all, key_grad)
    grad_value_w = weight_grad(normed_all, value_grad)
    normed_one_part = (
        project_back(query_grad, w_query)
        + project_back(key_grad, w_key)
        + project_back(value_grad, w_value)
    )
    normed_one_grad = sum_rows(normed_one_part)
    norm_one_back, gain_one_part = norm_backward(normed_one_grad, tokens_f, scale_one, gain_one_f)
    tokens_grad = (resid_grad + norm_one_back).astype(jnp.bfloat16)
    gain_one_sum, gain_two_sum = lax.psum((gain_one_part, gain_two_part), "tensor")
    grad_terms = (
        gain_one_sum,
        gain_two_sum,
        grad_query_w,
        grad_key_w,
        grad_value_w,
        grad_output_w,
        grad_gate_w,
        grad_up_w,
        grad_down_w,
    )
    owned = (
        lax.psum_scatter(
            grad_terms[0].astype(jnp.bfloat16), "shard", scatter_dimension=0, tiled=True
        ).astype(jnp.float32),
        lax.psum_scatter(
            grad_terms[1].astype(jnp.bfloat16), "shard", scatter_dimension=0, tiled=True
        ).astype(jnp.float32),
        lax.psum_scatter(
            grad_terms[2].astype(jnp.bfloat16), "shard", scatter_dimension=0, tiled=True
        ).astype(jnp.float32),
        lax.psum_scatter(
            grad_terms[3].astype(jnp.bfloat16), "shard", scatter_dimension=0, tiled=True
        ).astype(jnp.float32),
        lax.psum_scatter(
            grad_terms[4].astype(jnp.bfloat16), "shard", scatter_dimension=0, tiled=True
        ).astype(jnp.float32),
        lax.psum_scatter(
            grad_terms[5].astype(jnp.bfloat16), "shard", scatter_dimension=0, tiled=True
        ).astype(jnp.float32),
        lax.psum_scatter(
            grad_terms[6].astype(jnp.bfloat16), "shard", scatter_dimension=0, tiled=True
        ).astype(jnp.float32),
        lax.psum_scatter(
            grad_terms[7].astype(jnp.bfloat16), "shard", scatter_dimension=0, tiled=True
        ).astype(jnp.float32),
        lax.psum_scatter(
            grad_terms[8].astype(jnp.bfloat16), "shard", scatter_dimension=0, tiled=True
        ).astype(jnp.float32),
    )
    owned = (
        lax.psum(owned[0].astype(jnp.bfloat16), "context").astype(jnp.float32),
        lax.psum(owned[1].astype(jnp.bfloat16), "context").astype(jnp.float32),
        lax.psum(owned[2].astype(jnp.bfloat16), "context").astype(jnp.float32),
        lax.psum(owned[3].astype(jnp.bfloat16), "context").astype(jnp.float32),
        lax.psum(owned[4].astype(jnp.bfloat16), "context").astype(jnp.float32),
        lax.psum(owned[5].astype(jnp.bfloat16), "context").astype(jnp.float32),
        lax.psum(owned[6].astype(jnp.bfloat16), "context").astype(jnp.float32),
        lax.psum(owned[7].astype(jnp.bfloat16), "context").astype(jnp.float32),
        lax.psum(owned[8].astype(jnp.bfloat16), "context").astype(jnp.float32),
    )
    return (
        layer_output,
        tokens_grad,
        owned[0],
        owned[1],
        owned[2],
        owned[3],
        owned[4],
        owned[5],
        owned[6],
        owned[7],
        owned[8],
    )


def solution(mesh):
    return jax.shard_map(
        shards,
        mesh=mesh,
        in_specs=(
            P("shard", ("context", "tensor"), None),
            P("shard", ("context", "tensor"), None),
            P("shard", None),
            P("shard"),
            P("shard"),
            P("shard", "tensor"),
            P("shard", "tensor"),
            P("shard", "tensor"),
            P("shard", "tensor"),
            P("shard", "tensor"),
            P("shard", "tensor"),
            P("shard", "tensor"),
        ),
        out_specs=(
            P("shard", ("context", "tensor"), None),
            P("shard", ("context", "tensor"), None),
            P("shard"),
            P("shard"),
            P("shard", "tensor"),
            P("shard", "tensor"),
            P("shard", "tensor"),
            P("shard", "tensor"),
            P("shard", "tensor"),
            P("shard", "tensor"),
            P("shard", "tensor"),
        ),
        check_vma=False,
    )
```

profile of v0, /device:TPU:0, one launch (start us, length us, event | category | flops | bytes accessed | tf_op | source)
XLA Modules:
  0.0 1374.9 jit_solution(5671796065979896181)
XLA Ops:
  42.2 27.7 %all-gather.12.cloned.1.call-done = bf16[1,576,2048]{2,1,0:T(8,128)(2,1)} async-done(((bf16[1,144,2048]{2,1,0:T(8,128)(2,1)}), bf16[1,576,2048]{2,1,0:T(8,128)(2,1)}) %all-gather.12.cloned.1.call-update) | async-done | bytes 2359312 | tf_op jit(solution)/shard_map/all_gather | solution.py:79
  79.1 13.8 %all-gather.14.cloned.1.call-done = bf16[2048,512]{1,0:T(8,128)(2,1)} async-done(((bf16[512,512]{1,0:T(8,128)(2,1)}), bf16[2048,512]{1,0:T(8,128)(2,1)}) %all-gather.14.cloned.1.call-update) | async-done | bytes 2097168 | tf_op jit(solution)/shard_map/all_gather | solution.py:68
  140.4 18.1 %reduce.14 = bf16[1152,256]{1,0:T(8,128)(2,1)S(1)} reduce(bf16[1152,1,1,256]{3,2,1,0:T(2,128)(2,1)S(1)} %bitcast.251, bf16[]{:T(256)} %broadcast.209), dimensions={1,2}, to_apply=%bitcast.203.reduce_sub_computation | reduce | bytes 1179650
  158.7 11.1 all_to_all.87
  182.2 41.5 %reduce-scatter.12.cloned.1.call-done = bf16[1,144,2048]{2,1,0:T(8,128)(2,1)} async-done(((bf16[1,576,2048]{2,1,0:T(8,128)(2,1)}), bf16[1,144,2048]{2,1,0:T(8,128)(2,1)}) %reduce-scatter.12.cloned.1.call-update) | async-done | bytes 589840 | tf_op jit(solution)/shard_map/reduce_scatter | solution.py:83
  230.0 47.3 %all-gather.18.cloned.1.call-done = bf16[1,576,2048]{2,1,0:T(8,128)(2,1)} async-done(((bf16[1,144,2048]{2,1,0:T(8,128)(2,1)}), bf16[1,576,2048]{2,1,0:T(8,128)(2,1)}) %all-gather.18.cloned.1.call-update) | async-done | bytes 2359312 | tf_op jit(solution)/shard_map/all_gather | solution.py:79
  277.3 58.5 %all-gather.22.cloned.1.call-done = bf16[2048,2048]{1,0:T(8,128)(2,1)} async-done(((bf16[512,2048]{1,0:T(8,128)(2,1)}), bf16[2048,2048]{1,0:T(8,128)(2,1)}) %all-gather.22.cloned.1.call-update) | async-done | bytes 8388624 | tf_op jit(solution)/shard_map/all_gather | solution.py:73
  345.4 50.3 %all-gather.20.cloned.1.call-done = bf16[2048,2048]{1,0:T(8,128)(2,1)} async-done(((bf16[512,2048]{1,0:T(8,128)(2,1)}), bf16[2048,2048]{1,0:T(8,128)(2,1)}) %all-gather.20.cloned.1.call-update) | async-done | bytes 8388624 | tf_op jit(solution)/shard_map/all_gather | solution.py:72
  405.2 42.6 %all-gather.26.cloned.1.call-done = bf16[1,576,2048]{2,1,0:T(8,128)(2,1)} async-done(((bf16[1,144,2048]{2,1,0:T(8,128)(2,1)}), bf16[1,576,2048]{2,1,0:T(8,128)(2,1)}) %all-gather.26.cloned.1.call-update) | async-done | bytes 2359312 | tf_op jit(solution)/shard_map/all_gather | solution.py:79
  447.8 58.7 %all-gather.24.cloned.1.call-done = bf16[2048,2048]{1,0:T(8,128)(2,1)} async-done(((bf16[512,2048]{1,0:T(8,128)(2,1)}), bf16[2048,2048]{1,0:T(8,128)(2,1)}) %all-gather.24.cloned.1.call-update) | async-done | bytes 8388624 | tf_op jit(solution)/shard_map/all_gather | solution.py:74
  506.5 13.0 multiply_convert_fusion.1
  534.6 48.1 %reduce-scatter.16.cloned.1.call-done = bf16[1,144,2048]{2,1,0:T(8,128)(2,1)} async-done(((bf16[1,576,2048]{2,1,0:T(8,128)(2,1)}), bf16[1,144,2048]{2,1,0:T(8,128)(2,1)}) %reduce-scatter.16.cloned.1.call-update) | async-done | bytes 589840 | tf_op jit(solution)/shard_map/reduce_scatter | solution.py:83
  586.9 50.1 %all-gather.28.cloned.1.call-done = bf16[1,576,2048]{2,1,0:T(8,128)(2,1)} async-done(((bf16[1,144,2048]{2,1,0:T(8,128)(2,1)}), bf16[1,576,2048]{2,1,0:T(8,128)(2,1)}) %all-gather.28.cloned.1.call-update) | async-done | bytes 2359312 | tf_op jit(solution)/shard_map/all_gather | solution.py:79
  667.7 13.3 multiply_reduce_fusion
  681.1 15.0 %fusion.4 = bf16[4,1152,1152]{1,2,0:T(8,128)(2,1)S(1)} fusion(f32[1,4,1152,1152]{2,3,1,0:T(8,128)} %get-tuple-element.132, f32[1,4,1152,1152]{2,3,1,0:T(8,128)} %copy-done, f32[4,1152]{1,0:T(4,128)S(1)} %get-tuple-element.131, f32[4,1152]{1,0:T(4,128)S(1)} %copy-done.35), kind=kLoop, calls=%fused_computation.10 | loop fusion | flops 21233664 | bytes 53121024 | tf_op jit(solution)/shard_map/reshape.90
  759.8 11.2 all_to_all.89
  779.7 11.5 convolution_convert_fusion
  841.0 74.2 %reduce-scatter.30.cloned.1.call-done = bf16[512,2048]{1,0:T(8,128)(2,1)} async-done(((bf16[2048,2048]{1,0:T(8,128)(2,1)}), bf16[512,2048]{1,0:T(8,128)(2,1)}) %reduce-scatter.30.cloned.1.call-update) | async-done | bytes 2097168 | tf_op jit(solution)/shard_map/reduce_scatter | solution.py:315
  915.2 74.4 %reduce-scatter.28.cloned.1.call-done = bf16[512,2048]{1,0:T(8,128)(2,1)} async-done(((bf16[2048,2048]{1,0:T(8,128)(2,1)}), bf16[512,2048]{1,0:T(8,128)(2,1)}) %reduce-scatter.28.cloned.1.call-update) | async-done | bytes 2097168 | tf_op jit(solution)/shard_map/reduce_scatter | solution.py:312
  989.6 74.2 %reduce-scatter.32.cloned.1.call-done = bf16[512,2048]{0,1:T(8,128)(2,1)} async-done(((bf16[2048,2048]{0,1:T(8,128)(2,1)}), bf16[512,2048]{0,1:T(8,128)(2,1)}) %reduce-scatter.32.cloned.1.call-update) | async-done | bytes 2097168 | tf_op jit(solution)/shard_map/reduce_scatter | solution.py:318
  1065.6 49.2 %reduce-scatter.18.cloned.1.call-done = bf16[1,144,2048]{2,1,0:T(8,128)(2,1)} async-done(((bf16[1,576,2048]{2,1,0:T(8,128)(2,1)}), bf16[1,144,2048]{2,1,0:T(8,128)(2,1)}) %reduce-scatter.18.cloned.1.call-update) | async-done | bytes 589840 | tf_op jit(solution)/shard_map/reduce_scatter | solution.py:83
  1116.4 17.4 %all-reduce.2 = (bf16[2048]{0:T(1024)(128)(2,1)S(1)}, bf16[2048]{0:T(1024)(128)(2,1)S(1)}) all-reduce(f32[2048]{0:T(1024)S(1)} %get-tuple-element.94, f32[2048]{0:T(1024)S(1)} %get-tuple-element.92), channel_id=1, replica_groups=mesh['shard'=4,'context'=2,'tensor'=4] {'tensor'}, use_global_device_ids=true, to_apply=%region_14.15 | all-reduce | flops 4096 | bytes 24576 | tf_op jit(solution)/shard_map/psum | solution.py:281
  1146.2 19.1 %reduce-scatter.14.cloned.1.call-done = bf16[1,144,2048]{2,1,0:T(8,128)(2,1)} async-done(((bf16[1,576,2048]{2,1,0:T(8,128)(2,1)}), bf16[1,144,2048]{2,1,0:T(8,128)(2,1)}) %reduce-scatter.14.cloned.1.call-update) | async-done | bytes 589840 | tf_op jit(solution)/shard_map/reduce_scatter | solution.py:83
  1168.5 183.2 %all-reduce.8.cloned.1.call-done = (bf16[512,2048]{0,1:T(8,128)(2,1)}, bf16[512,512]{1,0:T(8,128)(2,1)}, bf16[512,128]{1,0:T(8,128)(2,1)}, bf16[512,128]{1,0:T(8...) async-done(((bf16[512,2048]{0,1:T(8,128)(2,1)}, bf16[512,512]{1,0:T(8,128)(2,1)}, bf16[512,128]{1,0:T(8,128)(2,1)}, ...) | async-done | bytes 7602192 | tf_op jit(solution)/shard_map/psum | solution.py:331
  (300 shorter events, 335.2 us)
Async XLA Ops:
  7.2 62.7 %all-gather.12.cloned.1.call-start = ((), (), s32[]{:S(2)}) async-start(), calls=%async_computation.17 | async-start | bytes 2949120 | tf_op jit(solution)/shard_map/all_gather | solution.py:79
  17.5 75.4 %all-gather.14.cloned.1.call-start = ((), (), s32[]{:S(2)}) async-start(), calls=%async_computation.18 | async-start | bytes 2621440 | tf_op jit(solution)/shard_map/all_gather | solution.py:68
  18.3 152.9 %all-gather.16.cloned.1.call-start = ((), (), s32[]{:S(2)}) async-start(), calls=%async_computation.19 | async-start | bytes 2621440 | tf_op jit(solution)/shard_map/all_gather | solution.py:71
  75.6 21.3 %all-to-all-start = ((bf16[1,576,2,128]{3,1,0,2:T(8,128)(2,1)}), bf16[1,576,2,128]{3,1,0,2:T(8,128)(2,1)S(1)}, u32[]{:S(2)}, u32[]{:S(2)}) async-start(bf16[1,576,2,128]{3,1,0,2:T(8,128)(2,1)} %copy.56), calls=%async_computation | async-start | bytes 589824 | tf_op jit(solution)/shard_map/all_to_all | solution.py:211
  96.9 12.9 all-to-all-start.1
  100.4 123.3 %reduce-scatter.12.cloned.1.call-start = ((), (), s32[]{:S(2)}) async-start(), calls=%async_computation.20 | async-start | bytes 2949120 | tf_op jit(solution)/shard_map/reduce_scatter | solution.py:83
  176.4 100.9 %all-gather.18.cloned.1.call-start = ((), (), s32[]{:S(2)}) async-start(), calls=%async_computation.21 | async-start | bytes 2949120 | tf_op jit(solution)/shard_map/all_gather | solution.py:79
  227.2 108.7 %all-gather.22.cloned.1.call-start = ((), (), s32[]{:S(2)}) async-start(), calls=%async_computation.23 | async-start | bytes 10485760 | tf_op jit(solution)/shard_map/all_gather | solution.py:73
  227.8 168.0 %all-gather.20.cloned.1.call-start = ((), (), s32[]{:S(2)}) async-start(), calls=%async_computation.22 | async-start | bytes 10485760 | tf_op jit(solution)/shard_map/all_gather | solution.py:72
  228.5 219.3 %all-gather.26.cloned.1.call-start = ((), (), s32[]{:S(2)}) async-start(), calls=%async_computation.26 | async-start | bytes 2949120 | tf_op jit(solution)/shard_map/all_gather | solution.py:79
  229.3 277.3 %all-gather.24.cloned.1.call-start = ((), (), s32[]{:S(2)}) async-start(), calls=%async_computation.24 | async-start | bytes 10485760 | tf_op jit(solution)/shard_map/all_gather | solution.py:74
  230.0 352.7 %reduce-scatter.16.cloned.1.call-start = ((), (), s32[]{:S(2)}) async-start(), calls=%async_computation.27 | async-start | bytes 2949120 | tf_op jit(solution)/shard_map/reduce_scatter | solution.py:83
  534.5 102.5 %all-gather.28.cloned.1.call-start = ((), (), s32[]{:S(2)}) async-start(), calls=%async_computation.28 | async-start | bytes 2949120 | tf_op jit(solution)/shard_map/all_gather | solution.py:79
  644.5 12.4 all-to-all-start.3
  648.0 186.5 %reduce-scatter.24.cloned.1.call-start = ((), (), s32[]{:S(2)}) async-start(), calls=%async_computation.32 | async-start | bytes 655360 | tf_op jit(solution)/shard_map/reduce_scatter | solution.py:306
  728.4 106.1 %reduce-scatter.22.cloned.1.call-start = ((), (), s32[]{:S(2)}) async-start(), calls=%async_computation.31 | async-start | bytes 655360 | tf_op jit(solution)/shard_map/reduce_scatter | solution.py:303
  733.0 101.5 %reduce-scatter.26.cloned.1.call-start = ((), (), s32[]{:S(2)}) async-start(), calls=%async_computation.33 | async-start | bytes 2621440 | tf_op jit(solution)/shard_map/reduce_scatter | solution.py:309
  738.1 102.9 %reduce-scatter.20.cloned.1.call-start = ((), (), s32[]{:S(2)}) async-start(), calls=%async_computation.30 | async-start | bytes 2621440 | tf_op jit(solution)/shard_map/reduce_scatter | solution.py:300
  779.5 135.7 %reduce-scatter.30.cloned.1.call-start = ((), (), s32[]{:S(2)}) async-start(), calls=%async_computation.35 | async-start | bytes 10485760 | tf_op jit(solution)/shard_map/reduce_scatter | solution.py:315
  791.2 198.3 %reduce-scatter.28.cloned.1.call-start = ((), (), s32[]{:S(2)}) async-start(), calls=%async_computation.34 | async-start | bytes 10485760 | tf_op jit(solution)/shard_map/reduce_scatter | solution.py:312
  803.6 260.1 %reduce-scatter.32.cloned.1.call-start = ((), (), s32[]{:S(2)}) async-start(), calls=%async_computation.36 | async-start | bytes 10485760 | tf_op jit(solution)/shard_map/reduce_scatter | solution.py:318
  816.1 298.7 %reduce-scatter.18.cloned.1.call-start = ((), (), s32[]{:S(2)}) async-start(), calls=%async_computation.29 | async-start | bytes 2949120 | tf_op jit(solution)/shard_map/reduce_scatter | solution.py:83
  822.7 342.6 %reduce-scatter.14.cloned.1.call-start = ((), (), s32[]{:S(2)}) async-start(), calls=%async_computation.25 | async-start | bytes 2949120 | tf_op jit(solution)/shard_map/reduce_scatter | solution.py:83
  834.4 517.4 %all-reduce.8.cloned.1.call-start = ((), (), s32[]{:S(2)}) async-start(), calls=%async_computation.37 | async-start | bytes 15204352 | tf_op jit(solution)/shard_map/psum | solution.py:331
  (59 other events, 1488.2 us)
Sparse Core Ops, SparseCore 0:
  17.6 52.2 all-gather.11
  71.5 21.3 all-gather.13
  94.5 22.5 all-gather.15
  176.5 47.1 reduce-scatter.11
  227.3 49.9 all-gather.17
  278.7 57.0 all-gather.21
  337.4 58.2 all-gather.19
  397.3 50.4 all-gather.25
  449.4 57.0 all-gather.23
  534.7 48.0 reduce-scatter.15
  587.0 49.9 all-gather.27
  728.5 19.7 reduce-scatter.23
  751.4 21.6 reduce-scatter.21
  775.5 31.4 reduce-scatter.25
  809.5 31.4 reduce-scatter.19
  843.4 71.7 reduce-scatter.29
  917.8 71.7 reduce-scatter.27
  992.0 71.7 reduce-scatter.31
  1066.7 48.0 reduce-scatter.17
  1117.6 47.6 reduce-scatter.13
  1168.6 183.0 all-reduce.7
where the time goes:
time: 1380 us; the launch traced here: 1370 us
  waiting for transfers between devices  939 us (68%)
  matrix products  164 us (12%)
  other arithmetic  91.9 us (7%)
  blocking collectives  86.9 us (6%)
  local copies, waits for them, and re-layouts  64 us (5%)
  between operations  16.3 us (1%)
    psum x1, waiting for transfers between devices, shards(): lax.psum(owned[8].astype(jnp.bfloat16), 'context').astype(jnp.float32)  183 us
    all_gather x4, waiting for transfers between devices, gather_rows(): return lax.all_gather(values, 'tensor', axis=1, tiled=True)  168 us
    reduce_scatter x4, waiting for transfers between devices, sum_rows(): lax.psum_scatter(values.astype(jnp.bfloat16), 'tensor', scatter_dimension...  158 us
    reduce_scatter x1, waiting for transfers between devices, shards(): lax.psum_scatter(grad_terms[6].astype(jnp.bfloat16), 'shard', scatter_dim...  74.4 us
    reduce_scatter x1, waiting for transfers between devices, shards(): lax.psum_scatter(grad_terms[7].astype(jnp.bfloat16), 'shard', scatter_dim...  74.2 us
    reduce_scatter x1, waiting for transfers between devices, shards(): lax.psum_scatter(grad_terms[8].astype(jnp.bfloat16), 'shard', scatter_dim...  74.2 us
    all_gather x1, waiting for transfers between devices, gather_weights(): lax.all_gather(shard_pieces[8], 'shard', axis=0, tiled=True)  58.7 us
    all_gather x1, waiting for transfers between devices, gather_weights(): lax.all_gather(shard_pieces[7], 'shard', axis=0, tiled=True)  58.5 us
  transfers between devices with their start and end apart: 24, of which 19 were waited for; matrix products, arithmetic and copies ran while one was open for 13% of the time, Pallas kernels for 0%

commit v1 on v0

v1 whole, which is shorter than its diff:
```python
import functools

import jax
import jax.numpy as jnp
from jax import lax
from jax.experimental import pallas as pl
from jax.experimental.pallas import tpu as pltpu
from jax.sharding import PartitionSpec as P

H = 32
KV = 8
HD = 64
GROUP = H // KV
QW = GROUP * HD
PW = QW + 2 * HD

EPS = 1e-05
THETA = 500000.0
MASKED = -1e30
BF = jnp.bfloat16
F32 = jnp.float32


def mm(a, b, dims, out=F32):
    return lax.dot_general(a, b, (dims, ((), ())), preferred_element_type=F32).astype(out)


def shift(values, step):
    return lax.ppermute(values, "tensor", [(i, (i + step) % 4) for i in range(4)])


def flip(values):
    return lax.ppermute(values, "context", [(0, 1), (1, 0)])


def xor_send(values, bit, count):
    return lax.ppermute(values, "shard", [(i, i ^ bit) for i in range(count)])


def shard_bits(count):
    bits = []
    bit = count // 2
    while bit:
        bits.append(bit)
        bit //= 2
    return bits


def xor_order(count):
    order = [0]
    for bit in shard_bits(count):
        order = order + [o | bit for o in order]
    return order


class Order:
    def __init__(self):
        self.mark = jnp.zeros((), F32)

    def after(self, values):
        values, _ = lax.optimization_barrier((values, self.mark))
        return values

    def wait(self, values):
        values, self.mark = lax.optimization_barrier((values, self.mark))
        return values


def add_bf(a, b):
    return (a.astype(F32) + b.astype(F32)).astype(BF)


def reduce_rest(kept, bits, count):
    for bit in bits:
        half = kept.shape[0] // 2
        kept = add_bf(kept[:half], xor_send(kept[half:], bit, count))
    return kept


def split_at(rows):
    return -(-rows // 32) * 16


def gather_rows_start(rows):
    return shift(rows, 1), shift(rows, -1)


def gather_rows_next(near):
    right, left = near
    mid = split_at(left.shape[0])
    return shift(left[:mid], -1), shift(right[mid:], 1)


def gather_rows_end(rows, near, far):
    return jnp.concatenate([rows, near[1], far[0], far[1], near[0]], axis=0)


def sum_rows_start(terms):
    length = terms.shape[0] // 4
    mid = split_at(length)
    far = terms[2 * length : 3 * length]
    return shift(far[:mid], 1), shift(far[mid:], -1)


def sum_rows_next(terms, far):
    length = terms.shape[0] // 4
    mid = split_at(length)
    t1, t3 = terms[length : 2 * length], terms[3 * length :]
    t1 = jnp.concatenate([add_bf(t1[:mid], far[0]), t1[mid:]], axis=0)
    t3 = jnp.concatenate([t3[:mid], add_bf(t3[mid:], far[1])], axis=0)
    return shift(t1, 1), shift(t3, -1)


def sum_rows_end(terms, near):
    own = terms[: terms.shape[0] // 4]
    return own.astype(F32) + near[0].astype(F32) + near[1].astype(F32)


def pick_turn(values):
    lane = lax.broadcasted_iota(jnp.int32, values.shape, 1)
    ahead = pltpu.roll(values, 2 * HD - HD // 2, 1)
    behind = pltpu.roll(values, HD // 2, 1)
    return jnp.where(lane % HD < HD // 2, ahead, behind)


def slot_of(block, z, length):
    return pl.multiple_of(((block - z + 4) % 4) * length, 16)


def causal_width(block, length, total):
    return min(total, -(-((block + 1) * length) // 128) * 128)


def masked_scores(q, k, start, first_row):
    s = mm(q, k, ((1,), (1,)))
    col = lax.broadcasted_iota(jnp.int32, s.shape, 1)
    row = lax.broadcasted_iota(jnp.int32, s.shape, 0) + first_row
    return jnp.where((col <= row) & (col >= start), s, MASKED)


def attn_forward_kernel(meta, own, oth, start, cos, sin, att_own, att_oth, rot, lse, nat):
    y, z = meta[0], meta[1]
    total = rot.shape[0]
    half = total // 2
    length = half // 4
    for src, base in ((own, y * half), (oth, (1 - y) * half)):
        for b in range(4):
            at = pl.ds(pl.multiple_of(base + b * length, 16), length)
            rows = src[pl.ds(slot_of(b, z, length), length), :].astype(BF)
            c, s = cos[at, :], sin[at, :]
            for part in range(PW // 128):
                u = rows[:, part * 128 : (part + 1) * 128].astype(F32)
                turned = u * c + pick_turn(u) * s
                if part == PW // 128 - 1:
                    lane = lax.broadcasted_iota(jnp.int32, u.shape, 1)
                    turned = jnp.where(lane < HD, turned, u)
                rot[at, part * 128 : (part + 1) * 128] = turned.astype(BF).astype(F32)
    for b in range(8):
        at = slice(b * length, (b + 1) * length)
        width = causal_width(b, length, total)
        k = rot[:width, QW : QW + HD].astype(BF)
        v = rot[:width, QW + HD :].astype(BF)
        heads = []
        for h in range(GROUP):
            q = (rot[at, h * HD : (h + 1) * HD] * HD**-0.5).astype(BF)
            s = masked_scores(q, k, start[at, :], b * length)
            top = jnp.max(s, axis=1, keepdims=True)
            p = jnp.exp(s - top)
            norm = jnp.sum(p, axis=1, keepdims=True)
            lse[at, h : h + 1] = top + jnp.log(norm)
            p = (p * (1.0 / norm)).astype(BF)
            heads.append(mm(p, v, ((1,), (0,))))
        nat[at, :] = jnp.concatenate(heads, axis=1)
    for dst, base in ((att_own, y * half), (att_oth, (1 - y) * half)):
        for b in range(4):
            at = pl.ds(pl.multiple_of(base + b * length, 16), length)
            dst[pl.ds(slot_of(b, z, length), length), :] = nat[at, :]


def attn_backward_kernel(
    meta, rot, lse, own, oth, start, cos, sin, d_own, d_oth, nat, d_nat, dk, dv
):
    y, z = meta[0], meta[1]
    total = rot.shape[0]
    half = total // 2
    length = half // 4
    for src, base in ((own, y * half), (oth, (1 - y) * half)):
        for b in range(4):
            at = pl.ds(pl.multiple_of(base + b * length, 16), length)
            nat[at, :] = src[pl.ds(slot_of(b, z, length), length), :]
    dk[...] = jnp.zeros_like(dk)
    dv[...] = jnp.zeros_like(dv)
    for b in range(8):
        at = slice(b * length, (b + 1) * length)
        width = causal_width(b, length, total)
        k = rot[:width, QW : QW + HD].astype(BF)
        v = rot[:width, QW + HD :].astype(BF)
        d_heads = []
        for h in range(GROUP):
            q = (rot[at, h * HD : (h + 1) * HD] * HD**-0.5).astype(BF)
            g = nat[at, h * HD : (h + 1) * HD].astype(BF)
            p = jnp.exp(masked_scores(q, k, start[at, :], b * length) - lse[at, h : h + 1])
            dp = mm(g, v, ((1,), (1,)))
            delta = jnp.sum(p * dp, axis=1, keepdims=True)
            ds = (p * (dp - delta)).astype(BF)
            d_heads.append(mm(ds, k, ((1,), (0,))) * HD**-0.5)
            dk[:width, :] += mm(ds, q, ((0,), (0,)))
            dv[:width, :] += mm(p.astype(BF), g, ((0,), (0,)))
        d_q = jnp.concatenate(d_heads, axis=1)
        for part in range(QW // 128):
            u = d_q[:, part * 128 : (part + 1) * 128]
            u = u * cos[at, :] - pick_turn(u) * sin[at, :]
            d_nat[at, part * 128 : (part + 1) * 128] = u
    for b in range(8):
        at = slice(b * length, (b + 1) * length)
        u = jnp.concatenate([dk[at, :], dv[at, :]], axis=1)
        turned = u * cos[at, :] - pick_turn(u) * sin[at, :]
        lane = lax.broadcasted_iota(jnp.int32, u.shape, 1)
        d_nat[at, QW:] = jnp.where(lane < HD, turned, u)
    for dst, base in ((d_own, y * half), (d_oth, (1 - y) * half)):
        for b in range(4):
            at = pl.ds(pl.multiple_of(base + b * length, 16), length)
            dst[pl.ds(slot_of(b, z, length), length), :] = d_nat[at, :]


VMEM = pl.BlockSpec(memory_space=pltpu.VMEM)
SMEM = pl.BlockSpec(memory_space=pltpu.SMEM)
ATTN_PARAMS = dict(vmem_limit_bytes=24 * 1024 * 1024)


def attn_forward(meta, own, oth, start, cos, sin):
    half = own.shape[0]
    return pl.pallas_call(
        attn_forward_kernel,
        out_shape=(
            jax.ShapeDtypeStruct((half, QW), F32),
            jax.ShapeDtypeStruct((half, QW), F32),
            jax.ShapeDtypeStruct((2 * half, PW), F32),
            jax.ShapeDtypeStruct((2 * half, GROUP), F32),
        ),
        in_specs=[SMEM] + [VMEM] * 5,
        out_specs=[VMEM] * 4,
        scratch_shapes=[pltpu.VMEM((2 * half, QW), F32)],
        compiler_params=pltpu.CompilerParams(**ATTN_PARAMS),
        cost_estimate=pl.CostEstimate(
            flops=8 * half * half * QW, bytes_accessed=8 * half * PW, transcendentals=8 * half * half
        ),
        name="attend_forward",
    )(meta, own, oth, start, cos, sin)


def attn_backward(meta, rot, lse, own, oth, start, cos, sin):
    half = own.shape[0]
    return pl.pallas_call(
        attn_backward_kernel,
        out_shape=(
            jax.ShapeDtypeStruct((half, PW), F32),
            jax.ShapeDtypeStruct((half, PW), F32),
        ),
        in_specs=[SMEM] + [VMEM] * 7,
        out_specs=[VMEM] * 2,
        scratch_shapes=[
            pltpu.VMEM((2 * half, QW), F32),
            pltpu.VMEM((2 * half, PW), F32),
            pltpu.VMEM((2 * half, HD), F32),
            pltpu.VMEM((2 * half, HD), F32),
        ],
        compiler_params=pltpu.CompilerParams(**ATTN_PARAMS),
        cost_estimate=pl.CostEstimate(
            flops=20 * half * half * QW, bytes_accessed=12 * half * PW, transcendentals=8 * half * half
        ),
        name="attend_backward",
    )(meta, rot, lse, own, oth, start, cos, sin)


def positions_of(seg_row):
    index_row = jnp.arange(seg_row.shape[0], dtype=jnp.int32)
    changed = jnp.concatenate([jnp.ones((1,), bool), seg_row[1:] != seg_row[:-1]])
    starts = lax.cummax(jnp.where(changed, index_row, 0), axis=0)
    return index_row - starts, starts


def rope_tables(positions):
    freq_index = jnp.arange(HD // 2, dtype=F32)
    inverse = THETA ** (-2.0 * freq_index / HD)
    angles = positions.astype(F32)[:, None] * inverse[None, :]
    cosines = jnp.cos(angles)
    sines = jnp.sin(angles)
    return (
        jnp.concatenate([cosines] * 4, axis=-1),
        jnp.concatenate([-sines, sines] * 2, axis=-1),
    )


def rms_scale(values):
    return lax.rsqrt(jnp.mean(values * values, axis=-1, keepdims=True) + EPS)


def norm_backward(grad_normed, normalized, scales, gain):
    rescaled = grad_normed * gain
    grad_input = scales * (
        rescaled - normalized * jnp.mean(rescaled * normalized, axis=-1, keepdims=True)
    )
    return grad_input


def shards(
    count,
    tokens,
    cotangent,
    segments,
    first_gain,
    second_gain,
    query_weight,
    key_weight,
    value_weight,
    output_weight,
    gate_weight,
    up_matrix,
    down_weight,
):
    s = lax.axis_index("shard")
    y = lax.axis_index("context")
    z = lax.axis_index("tensor")
    order = xor_order(count)
    deep = first_gain.shape[0]
    width = deep * count

    def to_xor(rows):
        return jnp.concatenate(
            [lax.dynamic_slice_in_dim(rows, (s ^ o) * deep, deep, axis=1) for o in order], axis=1
        )

    inverse_order = [order.index(o) for o in range(count)]

    def from_xor(rows):
        slots = jnp.array(inverse_order, jnp.int32)
        return jnp.concatenate(
            [
                lax.dynamic_slice_in_dim(rows, slots[s ^ b] * deep, deep, axis=1)
                for b in range(count)
            ],
            axis=1,
        )

    def swap(halves):
        middle = halves.shape[1] // 2
        return jnp.concatenate([halves[:, middle:], halves[:, :middle]], axis=1)

    def own_first(halves):
        return jnp.where(y == 0, halves, swap(halves))

    meta = jnp.stack([y, z]).astype(jnp.int32)
    positions, starts = positions_of(segments[0])
    start_col = starts[:, None]
    cos, sin = rope_tables(positions)

    bits = shard_bits(count)
    line = Order()

    def fetch(piece, axis=0):
        return [piece, xor_send(piece, bits[0], count)]

    def fetch_end(blocks, axis=0):
        for bit in bits[1:]:
            if count > 4:
                blocks = [jnp.concatenate(blocks, axis=axis)]
            blocks = blocks + [xor_send(b, bit, count) for b in blocks]
        return jnp.concatenate(blocks, axis=axis)

    pack = own_first(
        jnp.concatenate(
            [
                piece[:, part * piece.shape[1] // 2 : (part + 1) * piece.shape[1] // 2]
                for part in range(2)
                for piece in (query_weight, key_weight, value_weight)
            ],
            axis=1,
        )
    )
    out_piece = own_first(output_weight)

    rows = to_xor(tokens[0])
    near = gather_rows_start(rows)
    pack_blocks = fetch(pack)
    gains = jnp.stack([first_gain.astype(F32), second_gain.astype(F32)])
    gains = fetch_end(fetch(gains, 1), 1)
    gain_one, gain_two = gains[:1], gains[1:]
    cot = to_xor(cotangent[0])

    pack_blocks = line.wait(pack_blocks)
    out_blocks = fetch(line.after(out_piece))
    gate_blocks = fetch(line.after(gate_weight))
    w_pack = fetch_end(pack_blocks)
    near = line.wait(near)
    far = gather_rows_next(near)
    out_blocks = line.wait(out_blocks)
    up_blocks = fetch(line.after(up_matrix))
    w_out = fetch_end(out_blocks)
    far = line.wait(far)
    rows_all = gather_rows_end(rows, near, far)

    rows_f = rows.astype(F32)
    scale_one = rms_scale(rows_f)
    all_f = rows_all.astype(F32)
    hat_all = all_f * rms_scale(all_f)
    normed_all = (hat_all * gain_one).astype(BF)
    proj = mm(normed_all, w_pack, ((1,), (0,)), BF)
    proj = line.wait(proj)
    proj_own = proj[:, :PW]
    proj_oth = flip(proj[:, PW:])
    cot_near = gather_rows_start(line.after(cot))
    proj_oth = line.wait(proj_oth)
    att_own, att_oth, rot, lse = attn_forward(
        meta, proj_own.astype(F32), proj_oth.astype(F32), start_col, cos, sin
    )
    att_oth = flip(line.wait(att_oth.astype(BF)))
    cot_near = line.wait(cot_near)
    cot_far = gather_rows_next(cot_near)
    att_oth = line.wait(att_oth)
    context = jnp.concatenate([att_own.astype(BF), att_oth], axis=1)
    attn_terms = line.wait(mm(context, w_out, ((1,), (1,)), BF))
    far = sum_rows_start(attn_terms)
    cot_far = line.wait(cot_far)
    cot_all = gather_rows_end(cot, cot_near, cot_far)
    far = line.wait(far)
    near = sum_rows_next(attn_terms, far)
    gate_blocks = line.wait(gate_blocks)
    down_blocks = fetch(line.after(down_weight))
    w_gate = fetch_end(gate_blocks)
    near = line.wait(near)
    attn = sum_rows_end(attn_terms, near)

    hidden_one = rows_f + attn
    scale_two = rms_scale(hidden_one)
    hat_two = hidden_one * scale_two
    normed_two = line.wait((hat_two * gain_two).astype(BF))
    near = line.wait(gather_rows_start(normed_two))
    far = gather_rows_next(near)
    up_blocks = line.wait(up_blocks)
    w_up = fetch_end(up_blocks)
    far = line.wait(far)
    normed_two_all = gather_rows_end(normed_two, near, far)
    down_blocks = line.wait(down_blocks)
    w_down = fetch_end(down_blocks)
    gate = mm(normed_two_all, w_gate, ((1,), (0,)))
    up = mm(normed_two_all, w_up, ((1,), (0,)))
    sig = jax.nn.sigmoid(gate)
    silu = gate * sig
    hidden = line.wait((silu * up).astype(BF))

    def grad_start(left, right):
        half = width // 2
        term = mm(left[:, half:], right, ((0,), (0,)), BF)
        sent = xor_send(term, bits[-1], count)
        return mm(left[:, :half], right, ((0,), (0,)), BF), sent

    def grad_next(kept, sent):
        kept = line.wait(add_bf(kept, sent))
        half = kept.shape[0] // 2
        if len(bits) < 2:
            return kept, None
        return kept[:half], xor_send(kept[half:], bits[-2], count)

    def grad_end(kept, sent):
        if sent is not None:
            kept = add_bf(kept, sent)
        kept = line.wait(reduce_rest(kept, bits[:-2][::-1], count))
        return kept, flip(kept)

    def both(pair):
        return pair[0].astype(F32) + pair[1].astype(F32)

    down_pair = grad_start(cot_all, hidden)
    down_half = grad_next(*down_pair)
    grad_hidden = mm(line.after(cot_all), w_down, ((1,), (0,)))
    grad_gate = (grad_hidden * up * sig * (1.0 + gate * (1.0 - sig))).astype(BF)
    grad_up = (grad_hidden * silu).astype(BF)
    grad_gate, grad_up = line.wait((grad_gate, grad_up))
    mid_terms = (mm(grad_gate, w_gate, ((1,), (1,))) + mm(grad_up, w_up, ((1,), (1,)))).astype(BF)
    mid_terms = line.wait(mid_terms)
    far = sum_rows_start(mid_terms)
    normed_left, grad_gate = line.after((normed_two_all, grad_gate))
    gate_pair = grad_start(normed_left, grad_gate)
    far = line.wait(far)
    near = sum_rows_next(mid_terms, far)
    down_half = line.wait(down_half)
    down_full = grad_end(*down_half)
    gate_half = grad_next(*gate_pair)
    normed_left, grad_up = line.after((normed_two_all, grad_up))
    up_pair = grad_start(normed_left, grad_up)
    near = line.wait(near)
    normed_two_grad = sum_rows_end(mid_terms, near)

    resid = cot.astype(F32) + norm_backward(normed_two_grad, hat_two, scale_two, gain_two)
    gain_two_part = jnp.sum(normed_two_grad * hat_two, axis=0)

    resid_low = line.wait(resid.astype(BF))
    near = gather_rows_start(resid_low)
    ffn_terms = mm(line.after(hidden), w_down, ((1,), (1,)), BF)
    near, ffn_terms = line.wait((near, ffn_terms))
    far = gather_rows_next(near)
    far = line.wait(far)
    resid_all = gather_rows_end(resid_low, near, far)
    grad_context = line.wait(mm(resid_all, w_out, ((1,), (0,)), BF))
    g_own = grad_context[:, :QW]
    g_oth = flip(grad_context[:, QW:])
    ffn_far = sum_rows_start(line.after(ffn_terms))
    gate_half = line.wait(gate_half)
    gate_full = grad_end(*gate_half)
    up_half = grad_next(*up_pair)
    resid_left, context = line.after((resid_all, context))
    out_pair = grad_start(resid_left, context)
    g_oth = line.wait(g_oth)
    d_own, d_oth = attn_backward(
        meta, rot, lse, g_own.astype(F32), g_oth.astype(F32), start_col, cos, sin
    )
    d_oth = flip(line.wait(d_oth.astype(BF)))
    ffn_far = line.wait(ffn_far)
    ffn_near = sum_rows_next(ffn_terms, ffn_far)
    down_full = line.wait(down_full)
    down_total = both(down_full)
    out_half = grad_next(*out_pair)
    d_oth = line.wait(d_oth)
    d_pack = jnp.concatenate([d_own.astype(BF), d_oth], axis=1)
    one_terms = mm(d_pack, w_pack, ((1,), (1,)))
    ffn_near = line.wait(ffn_near)
    one_low = line.wait(one_terms.astype(BF))
    far = sum_rows_start(one_low)
    up_half = line.wait(up_half)
    up_full = grad_end(*up_half)
    normed_left, d_pack = line.after((normed_all, d_pack))
    pack_pair = grad_start(normed_left, d_pack)
    layer_output = (hidden_one + sum_rows_end(ffn_terms, ffn_near)).astype(BF)
    gain_one_part = jnp.sum(one_terms * hat_all, axis=0)
    far = line.wait(far)
    near = sum_rows_next(one_low, far)
    out_half = line.wait(out_half)
    out_full = grad_end(*out_half)
    pack_half = grad_next(*pack_pair)
    gate_total = both(line.wait(gate_full))

    part = jnp.stack([gain_one_part, gain_two_part])
    for step in (1, 2):
        part = part + lax.ppermute(part, "tensor", [(i, i ^ step) for i in range(4)])
    size = width
    for bit in bits[::-1]:
        size = size // 2
        part = part[:, :size] + xor_send(part[:, size:], bit, count)
    gain_total = part + flip(part)

    pack_half = line.wait(pack_half)
    pack_full = grad_end(*pack_half)
    near = line.wait(near)
    normed_one_grad = sum_rows_end(one_low, near)
    back = norm_backward(normed_one_grad, rows_f * scale_one, scale_one, gain_one)
    tokens_grad = (resid + back).astype(BF)

    def both_swapped(pair):
        return own_first(pair[0].astype(F32) + swap(pair[1]).astype(F32))

    up_total = both(line.wait(up_full))
    out_total = both_swapped(line.wait(out_full))
    pack_total = both_swapped(pack_full)
    query_parts, key_parts, value_parts = (
        jnp.concatenate([pack_total[:, at : at + size], pack_total[:, PW + at : PW + at + size]], 1)
        for at, size in ((0, QW), (QW, HD), (QW + HD, HD))
    )
    return (
        from_xor(layer_output)[None],
        from_xor(tokens_grad)[None],
        gain_total[0],
        gain_total[1],
        query_parts,
        key_parts,
        value_parts,
        out_total,
        gate_total,
        up_total,
        down_total,
    )


def solution(mesh):
    return jax.shard_map(
        functools.partial(shards, mesh.shape["shard"]),
        mesh=mesh,
        in_specs=(
            P("shard", ("context", "tensor"), None),
            P("shard", ("context", "tensor"), None),
            P("shard", None),
            P("shard"),
            P("shard"),
            P("shard", "tensor"),
            P("shard", "tensor"),
            P("shard", "tensor"),
            P("shard", "tensor"),
            P("shard", "tensor"),
            P("shard", "tensor"),
            P("shard", "tensor"),
        ),
        out_specs=(
            P("shard", ("context", "tensor"), None),
            P("shard", ("context", "tensor"), None),
            P("shard"),
            P("shard"),
            P("shard", "tensor"),
            P("shard", "tensor"),
            P("shard", "tensor"),
            P("shard", "tensor"),
            P("shard", "tensor"),
            P("shard", "tensor"),
            P("shard", "tensor"),
        ),
        check_vma=False,
    )
```

time: 1380 us -> 719 us (0.52)
  waiting for transfers between devices: 939 us -> 419 us
  blocking collectives: 86.9 us -> 0 us
  matrix products: 164 us -> 97.1 us
  starting transfers between devices: 12.4 us -> 76.8 us
  other arithmetic: 91.9 us -> 37.8 us
  Pallas kernels: 0 us -> 37.7 us
  local copies, waits for them, and re-layouts: 64 us -> 37.9 us
    ppermute x0 -> x74, waiting for transfers between devices: none -> 419 us  [the longest x30 181 us: xor_send(): return lax.ppermute(values, 'shard', [(i, i ^ bit) for i in range(count)])]
    reduce_scatter x11 -> x0, waiting for transfers between devices: 387 us -> none  [the longest x4 158 us: sum_rows(): lax.psum_scatter(values.astype(jnp.bfloat16), 'tensor', scatter_dimension...]
    all_gather x9 -> x0, waiting for transfers between devices: 349 us -> none  [the longest x4 168 us: gather_rows(): return lax.all_gather(values, 'tensor', axis=1, tiled=True)]
    psum x1 -> x0, waiting for transfers between devices: 183 us -> none  [shards(): lax.psum(owned[8].astype(jnp.bfloat16), 'context').astype(jnp.float32)]
    ppermute x0 -> x74, starting transfers between devices: none -> 76.8 us  [the longest x32 52.1 us: shift(): lax.ppermute(values, 'tensor', [(i, (i + step) % 4) for i in range(4)])]
    dot_general x27 -> x20, matrix products: 164 us -> 97.1 us  [mm(): lax.dot_general(a, b, (dims, ((), ())), preferred_element_type=F32)]
    pallas_call x0 -> x2, Pallas kernels: none -> 37.7 us  [the longest x1 22.6 us: attn_backward(): pl.pallas_call(attn_backward_kernel, out_shape=(jax.ShapeDtypeStruct((hal...]
    unnamed x4 -> x3, other arithmetic: 33.7 us -> 1.22 us
  transfers between devices with their start and end apart: 24 -> 74, of which waited for: 19 -> 37; matrix products, arithmetic and copies ran while one was open for 13% -> 14% of each run, Pallas kernels for 0% -> 5%
where the time goes in v1:
time: 719 us; the launch traced here: 711 us
  waiting for transfers between devices  419 us (58%)
  matrix products  97.1 us (14%)
  starting transfers between devices  76.8 us (11%)
  local copies, waits for them, and re-layouts  37.9 us (5%)
  other arithmetic  37.8 us (5%)
  Pallas kernels  37.7 us (5%)
    ppermute x30, waiting for transfers between devices, xor_send(): return lax.ppermute(values, 'shard', [(i, i ^ bit) for i in range(count)])  181 us
    ppermute x32, waiting for transfers between devices, shift(): lax.ppermute(values, 'tensor', [(i, (i + step) % 4) for i in range(4)])  127 us
    ppermute x10, waiting for transfers between devices, flip(): return lax.ppermute(values, 'context', [(0, 1), (1, 0)])  103 us
    dot_general x20, matrix products, mm(): lax.dot_general(a, b, (dims, ((), ())), preferred_element_type=F32)  97.1 us
    ppermute x32, starting transfers between devices, shift(): lax.ppermute(values, 'tensor', [(i, (i + step) % 4) for i in range(4)])  52.1 us
    pallas_call x1, Pallas kernels, attn_backward(): pl.pallas_call(attn_backward_kernel, out_shape=(jax.ShapeDtypeStruct((hal...  22.6 us
    unnamed x146, local copies, waits for them, and re-layouts  19.2 us
    pallas_call x1, Pallas kernels, attn_forward(): pl.pallas_call(attn_forward_kernel, out_shape=(jax.ShapeDtypeStruct((half...  15.1 us
  transfers between devices with their start and end apart: 74, of which 37 were waited for; matrix products, arithmetic and copies ran while one was open for 14% of the time, Pallas kernels for 5%

profile of v1, /device:TPU:0, one launch (start us, length us, event | category | flops | bytes accessed | tf_op | source)
XLA Modules:
  0.0 711.0 jit_solution(8256697596792359102)
XLA Ops:
  20.7 11.6 %collective-permute-done.2 = bf16[512,768]{1,0:T(8,128)(2,1)} collective-permute-done((bf16[512,768]{1,0:T(8,128)(2,1)S(1)}, bf16[512,768]{1,0:T(8,128)(2,1)}, u32[]{:S(2)}, u32[]{:S(2)}) %collective-permute-start.2) | collective-permute-done | bytes 786464 | tf_op jit(solution)/shard_map/ppermute | solution.py:37
  74.4 15.1 %attend_forward.1 = (f32[576,256]{1,0:T(8,128)S(1)}, f32[576,256]{1,0:T(8,128)S(1)}, f32[1152,384]{1,0:T(8,128)S(1)}, f32[1152,4]{1,0:T(8,128)S(1)}) custom-call(s32[2]{0:T(128)S(1)} %pad_add_fusion.meta, f32[576,384]{1,0:T(8,128)S(1)} %get-tuple-element.358.own, f32[576,384]{1,0:T(8,128)S(1)} %convert_element_type.347.oth, s32[1152,1]{1,0:T(8,128)S(1)} %bitcast.75, ...), custom_call_target="tpu_custom_call" | custom-call | flops 679477248 | bytes 1769472 | tf_op jit(solution)/shard_map/attend_forward/pallas_call | solution.py:233
  114.1 9.3 %collective-permute-done.18 = bf16[64,2048]{1,0:T(8,128)(2,1)S(1)} collective-permute-done((bf16[64,2048]{1,0:T(8,128)(2,1)S(1)}, bf16[64,2048]{1,0:T(8,128)(2,1)S(1)}, u32[]{:S(2)}, u32[]{:S(2)}) %collective-permute-start.18) | collective-permute-done | bytes 262176 | tf_op jit(solution)/shard_map/ppermute | solution.py:29
  127.6 26.1 %collective-permute-done.23 = bf16[512,2048]{1,0:T(8,128)(2,1)S(1)} collective-permute-done((bf16[512,2048]{1,0:T(8,128)(2,1)S(1)}, bf16[512,2048]{1,0:T(8,128)(2,1)S(1)}, u32[]{:S(2)}, u32[]{:S(2)}) %collective-permute-start.23) | collective-permute-done | bytes 2097184 | tf_op jit(solution)/shard_map/ppermute | solution.py:37
  158.4 10.0 %collective-permute-done.25 = bf16[144,2048]{1,0:T(8,128)(2,1)S(1)} collective-permute-done((bf16[144,2048]{1,0:T(8,128)(2,1)S(1)}, bf16[144,2048]{1,0:T(8,128)(2,1)S(1)}, u32[]{:S(2)}, u32[]{:S(2)}) %collective-permute-start.25) | collective-permute-done | bytes 589856 | tf_op jit(solution)/shard_map/ppermute | solution.py:29
  168.6 11.6 %collective-permute-done.24 = bf16[144,2048]{1,0:T(8,128)(2,1)S(1)} collective-permute-done((bf16[144,2048]{1,0:T(8,128)(2,1)S(1)}, bf16[144,2048]{1,0:T(8,128)(2,1)S(1)}, u32[]{:S(2)}, u32[]{:S(2)}) %collective-permute-start.24) | collective-permute-done | bytes 589856 | tf_op jit(solution)/shard_map/ppermute | solution.py:29
  180.2 18.4 %collective-permute-done.28 = bf16[512,2048]{1,0:T(8,128)(2,1)S(1)} collective-permute-done((bf16[512,2048]{1,0:T(8,128)(2,1)S(1)}, bf16[512,2048]{1,0:T(8,128)(2,1)S(1)}, u32[]{:S(2)}, u32[]{:S(2)}) %collective-permute-start.28) | collective-permute-done | bytes 2097184 | tf_op jit(solution)/shard_map/ppermute | solution.py:37
  209.1 31.9 %collective-permute-done.33 = bf16[512,2048]{1,0:T(8,128)(2,1)S(1)} collective-permute-done((bf16[512,2048]{1,0:T(8,128)(2,1)S(1)}, bf16[512,2048]{1,0:T(8,128)(2,1)S(1)}, u32[]{:S(2)}, u32[]{:S(2)}) %collective-permute-start.33) | collective-permute-done | bytes 2097184 | tf_op jit(solution)/shard_map/ppermute | solution.py:37
  251.2 11.0 %multiply_convert_fusion.2 = (bf16[576,2048]{1,0:T(8,128)(2,1)S(1)}, f32[576,2048]{1,0:T(8,128)}) fusion(f32[576,2048]{1,0:T(8,128)} %fusion.55, bf16[576,2048]{1,0:T(8,128)(2,1)S(1)} %constant_dynamic-update-slice_fusion.18, bf16[2048,2048]{1,0:T(8,128)(2,1)} %constant_dynamic-update-slice_fusion.27), kind=kOutput, calls=%fused_computation.13 | convolution fusion | flops 4838916096 | bytes 22544384 | tf_op jit(solution)/shard_map/dot_general | solution.py:25
  267.0 8.9 %collective-permute-done.35 = bf16[512,2048]{1,0:T(8,128)(2,1)S(1)} collective-permute-done((bf16[512,2048]{1,0:T(8,128)(2,1)S(1)}, bf16[512,2048]{1,0:T(8,128)(2,1)S(1)}, u32[]{:S(2)}, u32[]{:S(2)}) %collective-permute-start.35) | collective-permute-done | bytes 2097184 | tf_op jit(solution)/shard_map/ppermute | solution.py:37
  288.1 12.2 %multiply_convert_fusion = (bf16[576,2048]{1,0:T(8,128)(2,1)S(1)}, bf16[576,2048]{1,0:T(8,128)(2,1)}) fusion(f32[576,2048]{1,0:T(8,128)} %fusion.55, f32[576,2048]{1,0:T(8,128)} %get-tuple-element.403, bf16[576,2048]{1,0:T(8,128)(2,1)S(1)} %constant_dynamic-update-slice_fusion.13, bf16[2048,2048]{1,0:T(8,128)(2,1)} %copy-done.27), kind=kOutput, calls=%fused_computation.11 | convolution fusion | flops 4847173632 | bytes 24903680 | tf_op jit(solution)/shard_map/dot_general | solution.py:25
  301.8 10.7 %fusion.56 = f32[576,2048]{1,0:T(8,128)} fusion(bf16[576,2048]{1,0:T(8,128)(2,1)S(1)} %get-tuple-element.259, bf16[2048,2048]{1,0:T(8,128)(2,1)} %constant_dynamic-update-slice_fusion.27), kind=kOutput, calls=%fused_computation.210 | convolution fusion | flops 4831838208 | bytes 15466496 | tf_op jit(solution)/shard_map/dot_general | solution.py:25
  329.8 11.5 %collective-permute-done.38 = bf16[64,2048]{1,0:T(8,128)(2,1)S(1)} collective-permute-done((bf16[64,2048]{1,0:T(8,128)(2,1)S(1)}, bf16[64,2048]{1,0:T(8,128)(2,1)S(1)}, u32[]{:S(2)}, u32[]{:S(2)}) %collective-permute-start.38) | collective-permute-done | bytes 262176 | tf_op jit(solution)/shard_map/ppermute | solution.py:29
  343.7 29.6 %collective-permute-done.42 = bf16[512,2048]{1,0:T(8,128)(2,1)S(1)} collective-permute-done((bf16[512,2048]{1,0:T(8,128)(2,1)S(1)}, bf16[512,2048]{1,0:T(8,128)(2,1)S(1)}, u32[]{:S(2)}, u32[]{:S(2)}) %collective-permute-start.42) | collective-permute-done | bytes 2097184 | tf_op jit(solution)/shard_map/ppermute | solution.py:37
  398.8 11.1 %collective-permute-done.43 = bf16[144,2048]{1,0:T(8,128)(2,1)S(1)} collective-permute-done((bf16[144,2048]{1,0:T(8,128)(2,1)S(1)}, bf16[144,2048]{1,0:T(8,128)(2,1)S(1)}, u32[]{:S(2)}, u32[]{:S(2)}) %collective-permute-start.43) | collective-permute-done | bytes 589856 | tf_op jit(solution)/shard_map/ppermute | solution.py:29
  427.5 12.2 %collective-permute-done.51 = bf16[512,2048]{1,0:T(8,128)(2,1)S(1)} collective-permute-done((bf16[512,2048]{1,0:T(8,128)(2,1)S(1)}, bf16[512,2048]{1,0:T(8,128)(2,1)S(1)}, u32[]{:S(2)}, u32[]{:S(2)}) %collective-permute-start.51) | collective-permute-done | bytes 2097184 | tf_op jit(solution)/shard_map/ppermute | solution.py:37
  453.1 37.7 %collective-permute-done.72 = bf16[512,2048]{1,0:T(8,128)(2,1)} collective-permute-done((bf16[512,2048]{1,0:T(8,128)(2,1)}, bf16[512,2048]{1,0:T(8,128)(2,1)}, u32[]{:S(2)}, u32[]{:S(2)}) %collective-permute-start.72) | collective-permute-done | bytes 2097184 | tf_op jit(solution)/shard_map/ppermute | solution.py:33
  501.6 37.4 %collective-permute-done.49 = bf16[576,256]{1,0:T(8,128)(2,1)S(1)} collective-permute-done((bf16[576,256]{1,0:T(8,128)(2,1)S(1)}, bf16[576,256]{1,0:T(8,128)(2,1)S(1)}, u32[]{:S(2)}, u32[]{:S(2)}) %collective-permute-start.49) | collective-permute-done | bytes 294944 | tf_op jit(solution)/shard_map/ppermute | solution.py:33
  539.0 22.6 %attend_backward.1 = (f32[576,384]{1,0:T(8,128)S(1)}, f32[576,384]{1,0:T(8,128)S(1)}) custom-call(s32[2]{0:T(128)S(1)} %pad_add_fusion.meta, f32[1152,384]{1,0:T(8,128)S(1)} %copy-done.1, f32[1152,4]{1,0:T(8,128)S(1)} %get-tuple-element.256.lse, f32[576,256]{1,0:T(8,128)S(1)} %get-tuple-element.370.own, f32[576,256]{1,0:T(8,128)S(1)} %convert_element_type.403.oth, ...), custom_call_target="tpu_custom_call" | custom-call | flops 1698693120 | bytes 2654208 | tf_op jit(solution)/shard_map/attend_backward/pallas_call | solution.py:254
  579.8 9.1 %collective-permute-done.52 = bf16[144,2048]{1,0:T(8,128)(2,1)S(1)} collective-permute-done((bf16[144,2048]{1,0:T(8,128)(2,1)S(1)}, bf16[144,2048]{1,0:T(8,128)(2,1)S(1)}, u32[]{:S(2)}, u32[]{:S(2)}) %collective-permute-start.52) | collective-permute-done | bytes 589856 | tf_op jit(solution)/shard_map/ppermute | solution.py:29
  608.3 19.1 %collective-permute-done.65 = f32[2,512]{1,0:T(2,128)S(1)} collective-permute-done((f32[2,512]{1,0:T(2,128)S(1)}, f32[2,512]{1,0:T(2,128)S(1)}, u32[]{:S(2)}, u32[]{:S(2)}) %collective-permute-start.65) | collective-permute-done | bytes 4128 | tf_op jit(solution)/shard_map/ppermute | solution.py:37
  653.8 12.9 %collective-permute-done.60 = bf16[144,2048]{1,0:T(8,128)(2,1)S(1)} collective-permute-done((bf16[144,2048]{1,0:T(8,128)(2,1)S(1)}, bf16[144,2048]{1,0:T(8,128)(2,1)S(1)}, u32[]{:S(2)}, u32[]{:S(2)}) %collective-permute-start.60) | collective-permute-done | bytes 589856 | tf_op jit(solution)/shard_map/ppermute | solution.py:29
  670.1 18.2 %collective-permute-done.68 = bf16[512,768]{1,0:T(8,128)(2,1)S(1)} collective-permute-done((bf16[512,768]{1,0:T(8,128)(2,1)S(1)}, bf16[512,768]{1,0:T(8,128)(2,1)S(1)}, u32[]{:S(2)}, u32[]{:S(2)}) %collective-permute-start.68) | collective-permute-done | bytes 786464 | tf_op jit(solution)/shard_map/ppermute | solution.py:37
  692.9 14.1 %collective-permute-done.69 = bf16[512,768]{1,0:T(8,128)(2,1)S(1)} collective-permute-done((bf16[512,768]{1,0:T(8,128)(2,1)S(1)}, bf16[512,768]{1,0:T(8,128)(2,1)S(1)}, u32[]{:S(2)}, u32[]{:S(2)}) %collective-permute-start.69) | collective-permute-done | bytes 786464 | tf_op jit(solution)/shard_map/ppermute | solution.py:33
  (429 shorter events, 293.4 us)
Async XLA Ops:
  55.7 35.5 %collective-permute-start.15 = (bf16[512,512]{1,0:T(8,128)(2,1)}, bf16[512,512]{1,0:T(8,128)(2,1)}, u32[]{:S(2)}, u32[]{:S(2)}) collective-permute-start(bf16[512,512]{1,0:T(8,128)(2,1)} %maximum_select_fusion.2), channel_id=1, source_target_pairs={{0,8},{8,0},{16,24},{24,16},{1,9},{9,1},{17,25},{25,17},{2,10},{10... | collective-permute-start | bytes 1572872 | tf_op jit(solution)/shard_map/ppermute | solution.py:37
  105.1 48.6 %collective-permute-start.23 = (bf16[512,2048]{1,0:T(8,128)(2,1)S(1)}, bf16[512,2048]{1,0:T(8,128)(2,1)S(1)}, u32[]{:S(2)}, u32[]{:S(2)}) collective-permute-start(bf16[512,2048]{1,0:T(8,128)(2,1)S(1)} %copy-done.13), channel_id=1, source_target_pairs={{0,16},{8,24},{16,0},{24,8},{1,17},{9,25},{17,1},{25,9},{2,18},{10... | collective-permute-start | bytes 6291464 | tf_op jit(solution)/shard_map/ppermute | solution.py:37
  125.9 72.8 %collective-permute-start.28 = (bf16[512,2048]{1,0:T(8,128)(2,1)S(1)}, bf16[512,2048]{1,0:T(8,128)(2,1)S(1)}, u32[]{:S(2)}, u32[]{:S(2)}) collective-permute-start(bf16[512,2048]{1,0:T(8,128)(2,1)S(1)} %copy-done.14), channel_id=1, source_target_pairs={{0,16},{8,24},{16,0},{24,8},{1,17},{9,25},{17,1},{25,9},{2,18},{10... | collective-permute-start | bytes 6291464 | tf_op jit(solution)/shard_map/ppermute | solution.py:37
  156.4 84.6 %collective-permute-start.33 = (bf16[512,2048]{1,0:T(8,128)(2,1)S(1)}, bf16[512,2048]{1,0:T(8,128)(2,1)S(1)}, u32[]{:S(2)}, u32[]{:S(2)}) collective-permute-start(bf16[512,2048]{1,0:T(8,128)(2,1)S(1)} %copy-done.15), channel_id=1, source_target_pairs={{0,16},{8,24},{16,0},{24,8},{1,17},{9,25},{17,1},{25,9},{2,18},{10... | collective-permute-start | bytes 6291464 | tf_op jit(solution)/shard_map/ppermute | solution.py:37
  156.9 84.0 %collective-permute-start.29 = (bf16[512,2048]{1,0:T(8,128)(2,1)S(1)}, bf16[512,2048]{1,0:T(8,128)(2,1)S(1)}, u32[]{:S(2)}, u32[]{:S(2)}) collective-permute-start(bf16[512,2048]{1,0:T(8,128)(2,1)S(1)} %copy-done.13), channel_id=1, source_target_pairs={{0,8},{8,0},{16,24},{24,16},{1,9},{9,1},{17,25},{25,17},{2,10},{10... | collective-permute-start | bytes 6291464 | tf_op jit(solution)/shard_map/ppermute | solution.py:37
  168.4 72.7 %collective-permute-start.30 = (bf16[512,2048]{1,0:T(8,128)(2,1)S(1)}, bf16[512,2048]{1,0:T(8,128)(2,1)S(1)}, u32[]{:S(2)}, u32[]{:S(2)}) collective-permute-start(bf16[512,2048]{1,0:T(8,128)(2,1)S(1)} %collective-permute-done.23), channel_id=1, source_target_pairs={{0,8},{8,0},{16,24},{24,16},{1,9},{9,1},{17,25},{25,17},{2,10},{10... | collective-permute-start | bytes 6291464 | tf_op jit(solution)/shard_map/ppermute | solution.py:37
  207.4 40.8 %collective-permute-start.31 = (bf16[512,2048]{1,0:T(8,128)(2,1)S(1)}, bf16[512,2048]{1,0:T(8,128)(2,1)S(1)}, u32[]{:S(2)}, u32[]{:S(2)}) collective-permute-start(bf16[512,2048]{1,0:T(8,128)(2,1)S(1)} %copy-done.14), channel_id=1, source_target_pairs={{0,8},{8,0},{16,24},{24,16},{1,9},{9,1},{17,25},{25,17},{2,10},{10... | collective-permute-start | bytes 6291464 | tf_op jit(solution)/shard_map/ppermute | solution.py:37
  209.0 40.7 %collective-permute-start.32 = (bf16[512,2048]{1,0:T(8,128)(2,1)S(1)}, bf16[512,2048]{1,0:T(8,128)(2,1)S(1)}, u32[]{:S(2)}, u32[]{:S(2)}) collective-permute-start(bf16[512,2048]{1,0:T(8,128)(2,1)S(1)} %collective-permute-done.28), channel_id=1, source_target_pairs={{0,8},{8,0},{16,24},{24,16},{1,9},{9,1},{17,25},{25,17},{2,10},{10... | collective-permute-start | bytes 6291464 | tf_op jit(solution)/shard_map/ppermute | solution.py:37
  324.5 51.0 %collective-permute-start.41 = (bf16[1024,2048]{1,0:T(8,128)(2,1)}, bf16[1024,2048]{1,0:T(8,128)(2,1)S(1)}, u32[]{:S(2)}, u32[]{:S(2)}) collective-permute-start(bf16[1024,2048]{1,0:T(8,128)(2,1)} %convolution_convert_fusion.1), channel_id=1, source_target_pairs={{0,8},{8,0},{16,24},{24,16},{1,9},{9,1},{17,25},{25,17},{2,10},{10... | collective-permute-start | bytes 12582920 | tf_op jit(solution)/shard_map/ppermute | solution.py:37
  325.3 48.0 %collective-permute-start.42 = (bf16[512,2048]{1,0:T(8,128)(2,1)S(1)}, bf16[512,2048]{1,0:T(8,128)(2,1)S(1)}, u32[]{:S(2)}, u32[]{:S(2)}) collective-permute-start(bf16[512,2048]{1,0:T(8,128)(2,1)S(1)} %get-tuple-element.329), channel_id=1, source_target_pairs={{0,16},{8,24},{16,0},{24,8},{1,17},{9,25},{17,1},{25,9},{2,18},{10... | collective-permute-start | bytes 6291464 | tf_op jit(solution)/shard_map/ppermute | solution.py:37
  341.4 37.9 %collective-permute-start.40 = (bf16[144,2048]{1,0:T(8,128)(2,1)S(1)}, bf16[144,2048]{1,0:T(8,128)(2,1)S(1)}, u32[]{:S(2)}, u32[]{:S(2)}) collective-permute-start(bf16[144,2048]{1,0:T(8,128)(2,1)S(1)} %pad_maximum_fusion.10), channel_id=1, source_target_pairs={{0,3},{1,0},{2,1},{3,2},{4,7},{5,4},{6,5},{7,6},{8,11},{9,8},{10,9... | collective-permute-start | bytes 1769480 | tf_op jit(solution)/shard_map/ppermute | solution.py:29
  342.8 36.6 %collective-permute-start.39 = (bf16[144,2048]{1,0:T(8,128)(2,1)S(1)}, bf16[144,2048]{1,0:T(8,128)(2,1)S(1)}, u32[]{:S(2)}, u32[]{:S(2)}) collective-permute-start(bf16[144,2048]{1,0:T(8,128)(2,1)S(1)} %pad_maximum_fusion.9), channel_id=1, source_target_pairs={{0,1},{1,2},{2,3},{3,0},{4,5},{5,6},{6,7},{7,4},{8,9},{9,10},{10,1... | collective-permute-start | bytes 1769480 | tf_op jit(solution)/shard_map/ppermute | solution.py:29
  393.3 46.5 %collective-permute-start.51 = (bf16[512,2048]{1,0:T(8,128)(2,1)S(1)}, bf16[512,2048]{1,0:T(8,128)(2,1)S(1)}, u32[]{:S(2)}, u32[]{:S(2)}) collective-permute-start(bf16[512,2048]{1,0:T(8,128)(2,1)S(1)} %get-tuple-element.327), channel_id=1, source_target_pairs={{0,16},{8,24},{16,0},{24,8},{1,17},{9,25},{17,1},{25,9},{2,18},{10... | collective-permute-start | bytes 6291464 | tf_op jit(solution)/shard_map/ppermute | solution.py:37
  414.0 81.9 %collective-permute-start.50 = (bf16[1024,2048]{1,0:T(8,128)(2,1)}, bf16[1024,2048]{1,0:T(8,128)(2,1)}, u32[]{:S(2)}, u32[]{:S(2)}) collective-permute-start(bf16[1024,2048]{1,0:T(8,128)(2,1)} %convolution_convert_fusion), channel_id=1, source_target_pairs={{0,8},{8,0},{16,24},{24,16},{1,9},{9,1},{17,25},{25,17},{2,10},{10... | collective-permute-start | bytes 12582920 | tf_op jit(solution)/shard_map/ppermute | solution.py:37
  441.9 48.9 %collective-permute-start.72 = (bf16[512,2048]{1,0:T(8,128)(2,1)}, bf16[512,2048]{1,0:T(8,128)(2,1)}, u32[]{:S(2)}, u32[]{:S(2)}) collective-permute-start(bf16[512,2048]{1,0:T(8,128)(2,1)} %add_convert_fusion.5), channel_id=1, source_target_pairs={{0,4},{4,0},{1,5},{5,1},{2,6},{6,2},{3,7},{7,3},{8,12},{12,8},{9,1... | collective-permute-start | bytes 6291464 | tf_op jit(solution)/shard_map/ppermute | solution.py:33
  447.2 114.7 %collective-permute-start.56 = (bf16[512,2048]{1,0:T(8,128)(2,1)}, bf16[512,2048]{1,0:T(8,128)(2,1)S(1)}, u32[]{:S(2)}, u32[]{:S(2)}) collective-permute-start(bf16[512,2048]{1,0:T(8,128)(2,1)} %add_convert_fusion.6), channel_id=1, source_target_pairs={{0,4},{4,0},{1,5},{5,1},{2,6},{6,2},{3,7},{7,3},{8,12},{12,8},{9,1... | collective-permute-start | bytes 6291464 | tf_op jit(solution)/shard_map/ppermute | solution.py:33
  448.6 113.1 %collective-permute-start.48 = (bf16[64,2048]{1,0:T(8,128)(2,1)S(1)}, bf16[64,2048]{1,0:T(8,128)(2,1)S(1)}, u32[]{:S(2)}, u32[]{:S(2)}) collective-permute-start(bf16[64,2048]{1,0:T(8,128)(2,1)S(1)} %slice.372), channel_id=1, source_target_pairs={{0,3},{1,0},{2,1},{3,2},{4,7},{5,4},{6,5},{7,6},{8,11},{9,8},{10,9... | collective-permute-start | bytes 786440 | tf_op jit(solution)/shard_map/ppermute | solution.py:29
  452.3 86.7 %collective-permute-start.49 = (bf16[576,256]{1,0:T(8,128)(2,1)S(1)}, bf16[576,256]{1,0:T(8,128)(2,1)S(1)}, u32[]{:S(2)}, u32[]{:S(2)}) collective-permute-start(bf16[576,256]{1,0:T(8,128)(2,1)S(1)} %get-tuple-element.369), channel_id=1, source_target_pairs={{0,4},{4,0},{1,5},{5,1},{2,6},{6,2},{3,7},{7,3},{8,12},{12,8},{9,1... | collective-permute-start | bytes 884744 | tf_op jit(solution)/shard_map/ppermute | solution.py:33
  490.8 70.9 %collective-permute-start.47 = (bf16[80,2048]{1,0:T(8,128)(2,1)S(1)}, bf16[80,2048]{1,0:T(8,128)(2,1)S(1)}, u32[]{:S(2)}, u32[]{:S(2)}) collective-permute-start(bf16[80,2048]{1,0:T(8,128)(2,1)S(1)} %slice.371), channel_id=1, source_target_pairs={{0,1},{1,2},{2,3},{3,0},{4,5},{5,6},{6,7},{7,4},{8,9},{9,10},{10,1... | collective-permute-start | bytes 983048 | tf_op jit(solution)/shard_map/ppermute | solution.py:29
  567.9 65.1 %collective-permute-start.59 = (bf16[512,2048]{1,0:T(8,128)(2,1)S(1)}, bf16[512,2048]{1,0:T(8,128)(2,1)S(1)}, u32[]{:S(2)}, u32[]{:S(2)}) collective-permute-start(bf16[512,2048]{1,0:T(8,128)(2,1)S(1)} %get-tuple-element.325), channel_id=1, source_target_pairs={{0,16},{8,24},{16,0},{24,8},{1,17},{9,25},{17,1},{25,9},{2,18},{10... | collective-permute-start | bytes 6291464 | tf_op jit(solution)/shard_map/ppermute | solution.py:37
  593.6 40.2 %collective-permute-start.58 = (bf16[64,2048]{1,0:T(8,128)(2,1)S(1)}, bf16[64,2048]{1,0:T(8,128)(2,1)S(1)}, u32[]{:S(2)}, u32[]{:S(2)}) collective-permute-start(bf16[64,2048]{1,0:T(8,128)(2,1)S(1)} %get-tuple-element.333), channel_id=1, source_target_pairs={{0,3},{1,0},{2,1},{3,2},{4,7},{5,4},{6,5},{7,6},{8,11},{9,8},{10,9... | collective-permute-start | bytes 786440 | tf_op jit(solution)/shard_map/ppermute | solution.py:29
  594.0 37.5 %collective-permute-start.70 = (bf16[512,512]{1,0:T(8,128)(2,1)S(1)}, bf16[512,512]{1,0:T(8,128)(2,1)S(1)}, u32[]{:S(2)}, u32[]{:S(2)}) collective-permute-start(bf16[512,512]{1,0:T(8,128)(2,1)S(1)} %get-tuple-element.355), channel_id=1, source_target_pairs={{0,16},{8,24},{16,0},{24,8},{1,17},{9,25},{17,1},{25,9},{2,18},{10... | collective-permute-start | bytes 1572872 | tf_op jit(solution)/shard_map/ppermute | solution.py:37
  594.5 39.4 %collective-permute-start.57 = (bf16[80,2048]{1,0:T(8,128)(2,1)S(1)}, bf16[80,2048]{1,0:T(8,128)(2,1)S(1)}, u32[]{:S(2)}, u32[]{:S(2)}) collective-permute-start(bf16[80,2048]{1,0:T(8,128)(2,1)S(1)} %get-tuple-element.332), channel_id=1, source_target_pairs={{0,1},{1,2},{2,3},{3,0},{4,5},{5,6},{6,7},{7,4},{8,9},{9,10},{10,1... | collective-permute-start | bytes 983048 | tf_op jit(solution)/shard_map/ppermute | solution.py:29
  640.2 49.9 %collective-permute-start.73 = (bf16[512,2048]{1,0:T(8,128)(2,1)S(1)}, bf16[512,2048]{1,0:T(8,128)(2,1)S(1)}, u32[]{:S(2)}, u32[]{:S(2)}) collective-permute-start(bf16[512,2048]{1,0:T(8,128)(2,1)S(1)} %add_convert_fusion.4), channel_id=1, source_target_pairs={{0,4},{4,0},{1,5},{5,1},{2,6},{6,2},{3,7},{7,3},{8,12},{12,8},{9,1... | collective-permute-start | bytes 6291464 | tf_op jit(solution)/shard_map/ppermute | solution.py:33
  (109 other events, 1806.9 us)

commit v2 on v1

--- a/solution.py
+++ b/solution.py
@@ -58,12 +58,10 @@
         self.mark = jnp.zeros((), F32)
 
     def after(self, values):
-        values, _ = lax.optimization_barrier((values, self.mark))
-        return values
-
-    def wait(self, values):
         values, self.mark = lax.optimization_barrier((values, self.mark))
         return values
+
+    wait = after
 
 
 def add_bf(a, b):
@@ -243,7 +241,7 @@
         scratch_shapes=[pltpu.VMEM((2 * half, QW), F32)],
         compiler_params=pltpu.CompilerParams(**ATTN_PARAMS),
         cost_estimate=pl.CostEstimate(
-            flops=8 * half * half * QW, bytes_accessed=8 * half * PW, transcendentals=8 * half * half
+            flops=half * half * QW, bytes_accessed=half * PW, transcendentals=0
         ),
         name="attend_forward",
     )(meta, own, oth, start, cos, sin)
@@ -267,7 +265,7 @@
         ],
         compiler_params=pltpu.CompilerParams(**ATTN_PARAMS),
         cost_estimate=pl.CostEstimate(
-            flops=20 * half * half * QW, bytes_accessed=12 * half * PW, transcendentals=8 * half * half
+            flops=half * half * QW, bytes_accessed=half * PW, transcendentals=0
         ),
         name="attend_backward",
     )(meta, rot, lse, own, oth, start, cos, sin)
@@ -390,12 +388,11 @@
 
     pack_blocks = line.wait(pack_blocks)
     out_blocks = fetch(line.after(out_piece))
-    gate_blocks = fetch(line.after(gate_weight))
     w_pack = fetch_end(pack_blocks)
     near = line.wait(near)
     far = gather_rows_next(near)
     out_blocks = line.wait(out_blocks)
-    up_blocks = fetch(line.after(up_matrix))
+    gate_blocks = fetch(line.after(gate_weight))
     w_out = fetch_end(out_blocks)
     far = line.wait(far)
     rows_all = gather_rows_end(rows, near, far)
@@ -405,8 +402,7 @@
     all_f = rows_all.astype(F32)
     hat_all = all_f * rms_scale(all_f)
     normed_all = (hat_all * gain_one).astype(BF)
-    proj = mm(normed_all, w_pack, ((1,), (0,)), BF)
-    proj = line.wait(proj)
+    proj = line.wait(mm(normed_all, w_pack, ((1,), (0,)), BF))
     proj_own = proj[:, :PW]
     proj_oth = flip(proj[:, PW:])
     cot_near = gather_rows_start(line.after(cot))
@@ -416,18 +412,18 @@
     )
     att_oth = flip(line.wait(att_oth.astype(BF)))
     cot_near = line.wait(cot_near)
-    cot_far = gather_rows_next(cot_near)
+    gate_blocks = line.wait(gate_blocks)
+    up_blocks = fetch(line.after(up_matrix))
+    w_gate = fetch_end(gate_blocks)
     att_oth = line.wait(att_oth)
     context = jnp.concatenate([att_own.astype(BF), att_oth], axis=1)
     attn_terms = line.wait(mm(context, w_out, ((1,), (1,)), BF))
     far = sum_rows_start(attn_terms)
-    cot_far = line.wait(cot_far)
-    cot_all = gather_rows_end(cot, cot_near, cot_far)
     far = line.wait(far)
     near = sum_rows_next(attn_terms, far)
-    gate_blocks = line.wait(gate_blocks)
+    up_blocks = line.wait(up_blocks)
     down_blocks = fetch(line.after(down_weight))
-    w_gate = fetch_end(gate_blocks)
+    w_up = fetch_end(up_blocks)
     near = line.wait(near)
     attn = sum_rows_end(attn_terms, near)
 
@@ -436,18 +432,17 @@
     hat_two = hidden_one * scale_two
     normed_two = line.wait((hat_two * gain_two).astype(BF))
     near = line.wait(gather_rows_start(normed_two))
-    far = gather_rows_next(near)
-    up_blocks = line.wait(up_blocks)
-    w_up = fetch_end(up_blocks)
-    far = line.wait(far)
+    far = line.wait(gather_rows_next(near))
+    cot_far = gather_rows_next(line.after(cot_near))
     normed_two_all = gather_rows_end(normed_two, near, far)
-    down_blocks = line.wait(down_blocks)
+    gate = mm(normed_two_all, w_gate, ((1,), (0,)))
+    down_blocks, gate = line.wait((down_blocks, gate))
     w_down = fetch_end(down_blocks)
-    gate = mm(normed_two_all, w_gate, ((1,), (0,)))
     up = mm(normed_two_all, w_up, ((1,), (0,)))
     sig = jax.nn.sigmoid(gate)
     silu = gate * sig
-    hidden = line.wait((silu * up).astype(BF))
+    hidden, cot_far = line.wait(((silu * up).astype(BF), cot_far))
+    cot_all = gather_rows_end(cot, cot_near, cot_far)
 
     def grad_start(left, right):
         half = width // 2
@@ -455,40 +450,57 @@
         sent = xor_send(term, bits[-1], count)
         return mm(left[:, :half], right, ((0,), (0,)), BF), sent
 
-    def grad_next(kept, sent):
+    def grad_next(kept, sent, pieces):
         kept = line.wait(add_bf(kept, sent))
-        half = kept.shape[0] // 2
-        if len(bits) < 2:
-            return kept, None
-        return kept[:half], xor_send(kept[half:], bits[-2], count)
-
-    def grad_end(kept, sent):
+        if len(bits) != 2:
+            return [(reduce_rest(kept, bits[:-1][::-1], count), None)]
+        size = kept.shape[0] // 2 // pieces
+        return [
+            (
+                kept[i * size : (i + 1) * size],
+                xor_send(kept[(pieces + i) * size : (pieces + i + 1) * size], bits[-2], count),
+            )
+            for i in range(pieces)
+        ]
+
+    def grad_end(halves, at):
+        kept, sent = halves[min(at, len(halves) - 1)]
         if sent is not None:
-            kept = add_bf(kept, sent)
-        kept = line.wait(reduce_rest(kept, bits[:-2][::-1], count))
+            kept = line.wait(add_bf(kept, line.wait(sent)))
+        elif at:
+            return None
         return kept, flip(kept)
 
-    def both(pair):
-        return pair[0].astype(F32) + pair[1].astype(F32)
+    def both(pairs):
+        return jnp.concatenate([p[0].astype(F32) + p[1].astype(F32) for p in pairs if p], axis=0)
 
     down_pair = grad_start(cot_all, hidden)
-    down_half = grad_next(*down_pair)
+    ffn_terms = mm(hidden, w_down, ((1,), (1,)), BF)
+    down_half = grad_next(*down_pair, 2)
+    ffn_terms = line.wait(ffn_terms)
+    ffn_far = sum_rows_start(ffn_terms)
     grad_hidden = mm(line.after(cot_all), w_down, ((1,), (0,)))
     grad_gate = (grad_hidden * up * sig * (1.0 + gate * (1.0 - sig))).astype(BF)
     grad_up = (grad_hidden * silu).astype(BF)
     grad_gate, grad_up = line.wait((grad_gate, grad_up))
-    mid_terms = (mm(grad_gate, w_gate, ((1,), (1,))) + mm(grad_up, w_up, ((1,), (1,)))).astype(BF)
-    mid_terms = line.wait(mid_terms)
+    ffn_far = line.wait(ffn_far)
+    ffn_near = sum_rows_next(ffn_terms, ffn_far)
+    mid_terms = line.wait(mm(grad_gate, w_gate, ((1,), (1,))))
+    down_a = grad_end(down_half, 0)
+    mid_terms = line.wait((mid_terms + mm(grad_up, w_up, ((1,), (1,)))).astype(BF))
     far = sum_rows_start(mid_terms)
     normed_left, grad_gate = line.after((normed_two_all, grad_gate))
     gate_pair = grad_start(normed_left, grad_gate)
+    down_b = grad_end(down_half, 1)
+    gate_half = grad_next(*gate_pair, 2)
     far = line.wait(far)
     near = sum_rows_next(mid_terms, far)
-    down_half = line.wait(down_half)
-    down_full = grad_end(*down_half)
-    gate_half = grad_next(*gate_pair)
     normed_left, grad_up = line.after((normed_two_all, grad_up))
     up_pair = grad_start(normed_left, grad_up)
+    ffn_near = line.wait(ffn_near)
+    layer_output = (hidden_one + sum_rows_end(ffn_terms, ffn_near)).astype(BF)
+    down_a = line.wait(down_a)
+    gate_a = grad_end(gate_half, 0)
     near = line.wait(near)
     normed_two_grad = sum_rows_end(mid_terms, near)
 
@@ -497,60 +509,53 @@
 
     resid_low = line.wait(resid.astype(BF))
     near = gather_rows_start(resid_low)
-    ffn_terms = mm(line.after(hidden), w_down, ((1,), (1,)), BF)
-    near, ffn_terms = line.wait((near, ffn_terms))
+    up_half = grad_next(*up_pair, 2)
+    gate_b = grad_end(gate_half, 1)
+    down_b = line.wait(down_b)
+    near = line.wait(near)
     far = gather_rows_next(near)
+    gate_a = line.wait(gate_a)
     far = line.wait(far)
     resid_all = gather_rows_end(resid_low, near, far)
-    grad_context = line.wait(mm(resid_all, w_out, ((1,), (0,)), BF))
+    gate_b, grad_context = line.wait((gate_b, mm(resid_all, w_out, ((1,), (0,)), BF)))
     g_own = grad_context[:, :QW]
     g_oth = flip(grad_context[:, QW:])
-    ffn_far = sum_rows_start(line.after(ffn_terms))
-    gate_half = line.wait(gate_half)
-    gate_full = grad_end(*gate_half)
-    up_half = grad_next(*up_pair)
     resid_left, context = line.after((resid_all, context))
     out_pair = grad_start(resid_left, context)
     g_oth = line.wait(g_oth)
+    up_a = grad_end(up_half, 0)
     d_own, d_oth = attn_backward(
         meta, rot, lse, g_own.astype(F32), g_oth.astype(F32), start_col, cos, sin
     )
-    d_oth = flip(line.wait(d_oth.astype(BF)))
-    ffn_far = line.wait(ffn_far)
-    ffn_near = sum_rows_next(ffn_terms, ffn_far)
-    down_full = line.wait(down_full)
-    down_total = both(down_full)
-    out_half = grad_next(*out_pair)
+    up_a, d_oth = line.wait((up_a, d_oth.astype(BF)))
+    d_oth = flip(d_oth)
+    out_half = grad_next(*out_pair, 1)
     d_oth = line.wait(d_oth)
+    up_b = grad_end(up_half, 1)
     d_pack = jnp.concatenate([d_own.astype(BF), d_oth], axis=1)
     one_terms = mm(d_pack, w_pack, ((1,), (1,)))
-    ffn_near = line.wait(ffn_near)
     one_low = line.wait(one_terms.astype(BF))
     far = sum_rows_start(one_low)
-    up_half = line.wait(up_half)
-    up_full = grad_end(*up_half)
     normed_left, d_pack = line.after((normed_all, d_pack))
     pack_pair = grad_start(normed_left, d_pack)
-    layer_output = (hidden_one + sum_rows_end(ffn_terms, ffn_near)).astype(BF)
-    gain_one_part = jnp.sum(one_terms * hat_all, axis=0)
+    out_full = grad_end(out_half, 0)
+    pack_half = grad_next(*pack_pair, 1)
     far = line.wait(far)
     near = sum_rows_next(one_low, far)
-    out_half = line.wait(out_half)
-    out_full = grad_end(*out_half)
-    pack_half = grad_next(*pack_pair)
-    gate_total = both(line.wait(gate_full))
-
-    part = jnp.stack([gain_one_part, gain_two_part])
-    for step in (1, 2):
-        part = part + lax.ppermute(part, "tensor", [(i, i ^ step) for i in range(4)])
+    gain_one_part = jnp.sum(one_terms * hat_all, axis=0)
+    part = line.wait(jnp.stack([gain_one_part, gain_two_part]))
+
+    part = line.wait(part + lax.ppermute(part, "tensor", [(i, i ^ 1) for i in range(4)]))
+    down_total = both(line.wait([down_a, down_b]))
+    part = line.wait(part + lax.ppermute(part, "tensor", [(i, i ^ 2) for i in range(4)]))
+    pack_full = grad_end(pack_half, 0)
     size = width
     for bit in bits[::-1]:
         size = size // 2
-        part = part[:, :size] + xor_send(part[:, size:], bit, count)
+        part = line.wait(part[:, :size] + xor_send(part[:, size:], bit, count))
     gain_total = part + flip(part)
-
-    pack_half = line.wait(pack_half)
-    pack_full = grad_end(*pack_half)
+    gate_total = both(line.wait([gate_a, gate_b]))
+
     near = line.wait(near)
     normed_one_grad = sum_rows_end(one_low, near)
     back = norm_backward(normed_one_grad, rows_f * scale_one, scale_one, gain_one)
@@ -559,7 +564,7 @@
     def both_swapped(pair):
         return own_first(pair[0].astype(F32) + swap(pair[1]).astype(F32))
 
-    up_total = both(line.wait(up_full))
+    up_total = both(line.wait([up_a, up_b]))
     out_total = both_swapped(line.wait(out_full))
     pack_total = both_swapped(pack_full)
     query_parts, key_parts, value_parts = (
@@ -569,7 +574,7 @@
     return (
         from_xor(layer_output)[None],
         from_xor(tokens_grad)[None],
-        gain_total[0],
+        gain_total[0] + line.mark,
         gain_total[1],
         query_parts,
         key_parts,

time: 719 us -> 596 us (0.83)
  waiting for transfers between devices: 419 us -> 260 us
  starting transfers between devices: 76.8 us -> 94.9 us
  local copies, waits for them, and re-layouts: 37.9 us -> 45.2 us
    ppermute x30 -> x33, waiting for transfers between devices: 181 us -> 109 us  [xor_send(): return lax.ppermute(values, 'shard', [(i, i ^ bit) for i in range(count)])]
    ppermute x10 -> x13, waiting for transfers between devices: 103 us -> 33.2 us  [flip(): return lax.ppermute(values, 'context', [(0, 1), (1, 0)])]
    ppermute x32, waiting for transfers between devices: 127 us -> 101 us  [shift(): lax.ppermute(values, 'tensor', [(i, (i + step) % 4) for i in range(4)])]
    unnamed x146 -> x194, local copies, waits for them, and re-layouts: 19.2 us -> 29.6 us
    ppermute x30 -> x33, starting transfers between devices: 11.1 us -> 21.2 us  [xor_send(): return lax.ppermute(values, 'shard', [(i, i ^ bit) for i in range(count)])]
    ppermute x2, waiting for transfers between devices: 8.03 us -> 16.5 us  [the longest x1 12.8 us: shards(): lax.ppermute(part, 'tensor', [(i, i ^ 1) for i in range(4)])]
    concatenate x0 -> x3, other arithmetic: none -> 7.54 us  [both(): jnp.concatenate([p[0].astype(F32) + p[1].astype(F32) for p in pairs if p]...]
    ppermute x10 -> x13, starting transfers between devices: 11 us -> 16.4 us  [flip(): return lax.ppermute(values, 'context', [(0, 1), (1, 0)])]
  transfers between devices with their start and end apart: 74 -> 80, of which waited for: 37 -> 32; matrix products, arithmetic and copies ran while one was open for 14% -> 23% of each run, Pallas kernels for 5% -> 6%
where the time goes in v2:
time: 596 us; the launch traced here: 588 us
  waiting for transfers between devices  260 us (44%)
  matrix products  103 us (17%)
  starting transfers between devices  94.9 us (16%)
  local copies, waits for them, and re-layouts  45.2 us (8%)
  other arithmetic  41.8 us (7%)
  Pallas kernels  37.4 us (6%)
    ppermute x33, waiting for transfers between devices, xor_send(): return lax.ppermute(values, 'shard', [(i, i ^ bit) for i in range(count)])  109 us
    dot_general x20, matrix products, mm(): lax.dot_general(a, b, (dims, ((), ())), preferred_element_type=F32)  103 us
    ppermute x32, waiting for transfers between devices, shift(): lax.ppermute(values, 'tensor', [(i, (i + step) % 4) for i in range(4)])  101 us
    ppermute x32, starting transfers between devices, shift(): lax.ppermute(values, 'tensor', [(i, (i + step) % 4) for i in range(4)])  55.8 us
    ppermute x13, waiting for transfers between devices, flip(): return lax.ppermute(values, 'context', [(0, 1), (1, 0)])  33.2 us
    unnamed x194, local copies, waits for them, and re-layouts  29.6 us
    pallas_call x1, Pallas kernels, attn_backward(): pl.pallas_call(attn_backward_kernel, out_shape=(jax.ShapeDtypeStruct((hal...  22.3 us
    ppermute x33, starting transfers between devices, xor_send(): return lax.ppermute(values, 'shard', [(i, i ^ bit) for i in range(count)])  21.2 us
  transfers between devices with their start and end apart: 80, of which 32 were waited for; matrix products, arithmetic and copies ran while one was open for 23% of the time, Pallas kernels for 6%

profile of v2, /device:TPU:0, one launch (start us, length us, event | category | flops | bytes accessed | tf_op | source)
XLA Modules:
  0.0 588.3 jit_solution(11591912258008753582)
XLA Ops:
  21.8 12.8 %collective-permute-done.2 = bf16[512,768]{1,0:T(8,128)(2,1)} collective-permute-done((bf16[512,768]{1,0:T(8,128)(2,1)S(1)}, bf16[512,768]{1,0:T(8,128)(2,1)}, u32[]{:S(2)}, u32[]{:S(2)}) %collective-permute-start.2) | collective-permute-done | bytes 786464 | tf_op jit(solution)/shard_map/ppermute | solution.py:37
  40.0 8.5 %collective-permute-done.5 = bf16[512,512]{1,0:T(8,128)(2,1)} collective-permute-done((bf16[512,512]{1,0:T(8,128)(2,1)}, bf16[512,512]{1,0:T(8,128)(2,1)}, u32[]{:S(2)}, u32[]{:S(2)}) %collective-permute-start.5) | collective-permute-done | bytes 524320 | tf_op jit(solution)/shard_map/ppermute | solution.py:37
  72.0 15.1 %attend_forward.1 = (f32[576,256]{1,0:T(8,128)S(1)}, f32[576,256]{1,0:T(8,128)S(1)}, f32[1152,384]{1,0:T(8,128)S(1)}, f32[1152,4]{1,0:T(8,128)S(1)}) custom-call(s32[2]{0:T(128)S(1)} %pad_add_fusion.meta, f32[576,384]{1,0:T(8,128)S(1)} %get-tuple-element.485.own, f32[576,384]{1,0:T(8,128)S(1)} %convert_element_type.392.oth, s32[1152,1]{1,0:T(8,128)S(1)} %bitcast.75, ...), custom_call_target="tpu_custom_call" | custom-call | flops 84934656 | bytes 221184 | tf_op jit(solution)/shard_map/attend_forward/pallas_call | solution.py:231
  106.3 10.0 %collective-permute-done.19 = bf16[64,2048]{1,0:T(8,128)(2,1)S(1)} collective-permute-done((bf16[64,2048]{1,0:T(8,128)(2,1)S(1)}, bf16[64,2048]{1,0:T(8,128)(2,1)S(1)}, u32[]{:S(2)}, u32[]{:S(2)}) %collective-permute-start.19) | collective-permute-done | bytes 262176 | tf_op jit(solution)/shard_map/ppermute | solution.py:29
  127.6 22.6 %collective-permute-done.22 = bf16[512,2048]{1,0:T(8,128)(2,1)S(1)} collective-permute-done((bf16[512,2048]{1,0:T(8,128)(2,1)S(1)}, bf16[512,2048]{1,0:T(8,128)(2,1)S(1)}, u32[]{:S(2)}, u32[]{:S(2)}) %collective-permute-start.22) | collective-permute-done | bytes 2097184 | tf_op jit(solution)/shard_map/ppermute | solution.py:37
  169.0 8.6 %collective-permute-done.25 = bf16[144,2048]{1,0:T(8,128)(2,1)S(1)} collective-permute-done((bf16[144,2048]{1,0:T(8,128)(2,1)S(1)}, bf16[144,2048]{1,0:T(8,128)(2,1)S(1)}, u32[]{:S(2)}, u32[]{:S(2)}) %collective-permute-start.25) | collective-permute-done | bytes 589856 | tf_op jit(solution)/shard_map/ppermute | solution.py:29
  180.7 11.4 %collective-permute-done.27 = bf16[64,2048]{1,0:T(8,128)(2,1)S(1)} collective-permute-done((bf16[64,2048]{1,0:T(8,128)(2,1)S(1)}, bf16[64,2048]{1,0:T(8,128)(2,1)S(1)}, u32[]{:S(2)}, u32[]{:S(2)}) %collective-permute-start.27) | collective-permute-done | bytes 262176 | tf_op jit(solution)/shard_map/ppermute | solution.py:29
  195.2 8.4 %fusion.54 = f32[576,2048]{1,0:T(8,128)S(1)} fusion(bf16[576,2048]{1,0:T(8,128)(2,1)S(1)} %constant_dynamic-update-slice_fusion.13, bf16[2048,2048]{1,0:T(8,128)(2,1)} %constant_dynamic-update-slice_fusion.18), kind=kOutput, calls=%fused_computation.218 | convolution fusion | flops 4831838208 | bytes 15466496 | tf_op jit(solution)/shard_map/dot_general | solution.py:25
  211.2 10.7 %multiply_convert_fusion.2 = (bf16[576,2048]{1,0:T(8,128)(2,1)S(1)}, f32[576,2048]{1,0:T(8,128)}) fusion(f32[576,2048]{1,0:T(8,128)S(1)} %fusion.54, bf16[576,2048]{1,0:T(8,128)(2,1)S(1)} %constant_dynamic-update-slice_fusion.13, bf16[2048,2048]{1,0:T(8,128)(2,1)} %constant_dynamic-update-slice_fusion.22), kind=kOutput, calls=%fused_computation.13 | convolution fusion | flops 4838916096 | bytes 22544384 | tf_op jit(solution)/shard_map/dot_general | solution.py:25
  234.9 9.3 %convolution_convert_fusion.3 = bf16[576,2048]{1,0:T(8,128)(2,1)S(1)} fusion(bf16[576,2048]{1,0:T(8,128)(2,1)} %copy-done.78, bf16[2048,2048]{1,0:T(8,128)(2,1)S(1)} %constant_dynamic-update-slice_fusion.26), kind=kOutput, calls=%fused_computation.23 | convolution fusion | flops 4833017856 | bytes 13107200 | tf_op jit(solution)/shard_map/dot_general | solution.py:25
  248.1 12.1 %multiply_convert_fusion = (bf16[576,2048]{1,0:T(8,128)(2,1)}, bf16[576,2048]{1,0:T(8,128)(2,1)S(1)}) fusion(f32[576,2048]{1,0:T(8,128)} %copy-done.80, f32[576,2048]{1,0:T(8,128)} %get-tuple-element.530, bf16[576,2048]{1,0:T(8,128)(2,1)S(1)} %copy-done.57, bf16[2048,2048]{1,0:T(8,128)(2,1)} %copy-done.46), kind=kOutput, calls=%fused_computation.11 | convolution fusion | flops 4847173632 | bytes 24903680 | tf_op jit(solution)/shard_map/dot_general | solution.py:25
  260.2 8.3 %fusion.55 = f32[576,2048]{1,0:T(8,128)S(1)} fusion(bf16[576,2048]{1,0:T(8,128)(2,1)S(1)} %get-tuple-element.313, bf16[2048,2048]{1,0:T(8,128)(2,1)} %constant_dynamic-update-slice_fusion.18), kind=kOutput, calls=%fused_computation.219 | convolution fusion | flops 4831838208 | bytes 15466496 | tf_op jit(solution)/shard_map/dot_general | solution.py:25
  285.6 12.0 %collective-permute-done.41 = bf16[256,2048]{1,0:T(8,128)(2,1)S(1)} collective-permute-done((bf16[256,2048]{1,0:T(8,128)(2,1)S(1)}, bf16[256,2048]{1,0:T(8,128)(2,1)S(1)}, u32[]{:S(2)}, u32[]{:S(2)}) %collective-permute-start.41) | collective-permute-done | bytes 1048608 | tf_op jit(solution)/shard_map/ppermute | solution.py:37
  310.9 19.8 %collective-permute-done.45 = bf16[256,2048]{1,0:T(8,128)(2,1)S(1)} collective-permute-done((bf16[256,2048]{1,0:T(8,128)(2,1)S(1)}, bf16[256,2048]{1,0:T(8,128)(2,1)S(1)}, u32[]{:S(2)}, u32[]{:S(2)}) %collective-permute-start.45) | collective-permute-done | bytes 1048608 | tf_op jit(solution)/shard_map/ppermute | solution.py:37
  347.9 22.6 %collective-permute-done.40 = bf16[144,2048]{1,0:T(8,128)(2,1)S(1)} collective-permute-done((bf16[144,2048]{1,0:T(8,128)(2,1)S(1)}, bf16[144,2048]{1,0:T(8,128)(2,1)S(1)}, u32[]{:S(2)}, u32[]{:S(2)}) %collective-permute-start.40) | collective-permute-done | bytes 589856 | tf_op jit(solution)/shard_map/ppermute | solution.py:29
  374.2 9.1 %collective-permute-done.47 = bf16[144,2048]{1,0:T(8,128)(2,1)S(1)} collective-permute-done((bf16[144,2048]{1,0:T(8,128)(2,1)S(1)}, bf16[144,2048]{1,0:T(8,128)(2,1)S(1)}, u32[]{:S(2)}, u32[]{:S(2)}) %collective-permute-start.47) | collective-permute-done | bytes 589856 | tf_op jit(solution)/shard_map/ppermute | solution.py:29
  404.1 8.3 %collective-permute-done.54 = bf16[144,2048]{1,0:T(8,128)(2,1)S(1)} collective-permute-done((bf16[144,2048]{1,0:T(8,128)(2,1)S(1)}, bf16[144,2048]{1,0:T(8,128)(2,1)S(1)}, u32[]{:S(2)}, u32[]{:S(2)}) %collective-permute-start.54) | collective-permute-done | bytes 589856 | tf_op jit(solution)/shard_map/ppermute | solution.py:29
  430.4 13.5 %collective-permute-done.52 = bf16[256,2048]{1,0:T(8,128)(2,1)S(1)} collective-permute-done((bf16[256,2048]{1,0:T(8,128)(2,1)S(1)}, bf16[256,2048]{1,0:T(8,128)(2,1)S(1)}, u32[]{:S(2)}, u32[]{:S(2)}) %collective-permute-start.52) | collective-permute-done | bytes 1048608 | tf_op jit(solution)/shard_map/ppermute | solution.py:33
  460.6 22.3 %attend_backward.1 = (f32[576,384]{1,0:T(8,128)S(1)}, f32[576,384]{1,0:T(8,128)S(1)}) custom-call(s32[2]{0:T(128)S(1)} %copy-done.3, f32[1152,384]{1,0:T(8,128)S(1)} %copy-done.1, f32[1152,4]{1,0:T(8,128)S(1)} %get-tuple-element.335.lse, f32[576,256]{1,0:T(8,128)S(1)} %get-tuple-element.492.own, f32[576,256]{1,0:T(8,128)S(1)} %convert_element_type.462.oth, ...), custom_call_target="tpu_custom_call" | custom-call | flops 84934656 | bytes 221184 | tf_op jit(solution)/shard_map/attend_backward/pallas_call | solution.py:252
  486.7 8.9 %collective-permute-done.62 = bf16[576,384]{1,0:T(8,128)(2,1)S(1)} collective-permute-done((bf16[576,384]{1,0:T(8,128)(2,1)S(1)}, bf16[576,384]{1,0:T(8,128)(2,1)S(1)}, u32[]{:S(2)}, u32[]{:S(2)}) %collective-permute-start.62) | collective-permute-done | bytes 442400 | tf_op jit(solution)/shard_map/ppermute | solution.py:33
  498.1 11.6 %collective-permute-done.64 = bf16[256,2048]{1,0:T(8,128)(2,1)S(1)} collective-permute-done((bf16[256,2048]{1,0:T(8,128)(2,1)S(1)}, bf16[256,2048]{1,0:T(8,128)(2,1)S(1)}, u32[]{:S(2)}, u32[]{:S(2)}) %collective-permute-start.64) | collective-permute-done | bytes 1048608 | tf_op jit(solution)/shard_map/ppermute | solution.py:37
  519.5 8.6 %collective-permute-done.68 = bf16[512,512]{1,0:T(8,128)(2,1)S(1)} collective-permute-done((bf16[512,512]{1,0:T(8,128)(2,1)S(1)}, bf16[512,512]{1,0:T(8,128)(2,1)S(1)}, u32[]{:S(2)}, u32[]{:S(2)}) %collective-permute-start.68) | collective-permute-done | bytes 524320 | tf_op jit(solution)/shard_map/ppermute | solution.py:37
  535.8 12.8 %collective-permute-done.71 = f32[2,2048]{1,0:T(2,128)S(1)} collective-permute-done((f32[2,2048]{1,0:T(2,128)S(1)}, f32[2,2048]{1,0:T(2,128)S(1)}, u32[]{:S(2)}, u32[]{:S(2)}) %collective-permute-start.71) | collective-permute-done | bytes 16416 | tf_op jit(solution)/shard_map/ppermute | solution.py:548
  561.4 8.5 %collective-permute-done.70 = bf16[144,2048]{1,0:T(8,128)(2,1)S(1)} collective-permute-done((bf16[144,2048]{1,0:T(8,128)(2,1)S(1)}, bf16[144,2048]{1,0:T(8,128)(2,1)S(1)}, u32[]{:S(2)}, u32[]{:S(2)}) %collective-permute-start.70) | collective-permute-done | bytes 589856 | tf_op jit(solution)/shard_map/ppermute | solution.py:29
  (494 shorter events, 287.2 us)
Async XLA Ops:
  3.7 31.2 %collective-permute-start = (bf16[144,2048]{1,0:T(8,128)(2,1)S(1)}, bf16[144,2048]{1,0:T(8,128)(2,1)}, u32[]{:S(2)}, u32[]{:S(2)}) collective-permute-start(bf16[144,2048]{1,0:T(8,128)(2,1)S(1)} %get-tuple-element.442), channel_id=1, source_target_pairs={{0,1},{1,2},{2,3},{3,0},{4,5},{5,6},{6,7},{7,4},{8,9},{9,10},{10,1... | collective-permute-start | bytes 1769480 | tf_op jit(solution)/shard_map/ppermute | solution.py:29
  48.5 38.7 %collective-permute-start.16 = (bf16[512,512]{1,0:T(8,128)(2,1)}, bf16[512,512]{1,0:T(8,128)(2,1)}, u32[]{:S(2)}, u32[]{:S(2)}) collective-permute-start(bf16[512,512]{1,0:T(8,128)(2,1)} %maximum_select_fusion.2), channel_id=1, source_target_pairs={{0,8},{8,0},{16,24},{24,16},{1,9},{9,1},{17,25},{25,17},{2,10},{10... | collective-permute-start | bytes 1572872 | tf_op jit(solution)/shard_map/ppermute | solution.py:37
  51.9 46.7 %collective-permute-start.13 = (bf16[512,2048]{1,0:T(8,128)(2,1)}, bf16[512,2048]{1,0:T(8,128)(2,1)}, u32[]{:S(2)}, u32[]{:S(2)}) collective-permute-start(bf16[512,2048]{1,0:T(8,128)(2,1)} %param.23), channel_id=1, source_target_pairs={{0,16},{8,24},{16,0},{24,8},{1,17},{9,25},{17,1},{25,9},{2,18},{10... | collective-permute-start | bytes 6291464 | tf_op jit(solution)/shard_map/ppermute | solution.py:37
  59.4 31.5 %collective-permute-start.17 = (bf16[512,512]{1,0:T(8,128)(2,1)}, bf16[512,512]{1,0:T(8,128)(2,1)}, u32[]{:S(2)}, u32[]{:S(2)}) collective-permute-start(bf16[512,512]{1,0:T(8,128)(2,1)} %collective-permute-done.5), channel_id=1, source_target_pairs={{0,8},{8,0},{16,24},{24,16},{1,9},{9,1},{17,25},{25,17},{2,10},{10... | collective-permute-start | bytes 1572872 | tf_op jit(solution)/shard_map/ppermute | solution.py:37
  59.8 32.3 %collective-permute-start.14 = (bf16[144,2048]{1,0:T(8,128)(2,1)}, bf16[144,2048]{1,0:T(8,128)(2,1)S(1)}, u32[]{:S(2)}, u32[]{:S(2)}) collective-permute-start(bf16[144,2048]{1,0:T(8,128)(2,1)} %get-tuple-element.247), channel_id=1, source_target_pairs={{0,1},{1,2},{2,3},{3,0},{4,5},{5,6},{6,7},{7,4},{8,9},{9,10},{10,1... | collective-permute-start | bytes 1769480 | tf_op jit(solution)/shard_map/ppermute | solution.py:29
  105.1 45.1 %collective-permute-start.22 = (bf16[512,2048]{1,0:T(8,128)(2,1)S(1)}, bf16[512,2048]{1,0:T(8,128)(2,1)S(1)}, u32[]{:S(2)}, u32[]{:S(2)}) collective-permute-start(bf16[512,2048]{1,0:T(8,128)(2,1)S(1)} %copy-done.22), channel_id=1, source_target_pairs={{0,16},{8,24},{16,0},{24,8},{1,17},{9,25},{17,1},{25,9},{2,18},{10... | collective-permute-start | bytes 6291464 | tf_op jit(solution)/shard_map/ppermute | solution.py:37
  116.4 33.7 %collective-permute-start.20 = (bf16[144,2048]{1,0:T(8,128)(2,1)S(1)}, bf16[144,2048]{1,0:T(8,128)(2,1)S(1)}, u32[]{:S(2)}, u32[]{:S(2)}) collective-permute-start(bf16[144,2048]{1,0:T(8,128)(2,1)S(1)} %pad_maximum_fusion.10), channel_id=1, source_target_pairs={{0,1},{1,2},{2,3},{3,0},{4,5},{5,6},{6,7},{7,4},{8,9},{9,10},{10,1... | collective-permute-start | bytes 1769480 | tf_op jit(solution)/shard_map/ppermute | solution.py:29
  117.7 32.5 %collective-permute-start.21 = (bf16[144,2048]{1,0:T(8,128)(2,1)S(1)}, bf16[144,2048]{1,0:T(8,128)(2,1)S(1)}, u32[]{:S(2)}, u32[]{:S(2)}) collective-permute-start(bf16[144,2048]{1,0:T(8,128)(2,1)S(1)} %pad_maximum_fusion.11), channel_id=1, source_target_pairs={{0,3},{1,0},{2,1},{3,2},{4,7},{5,4},{6,5},{7,6},{8,11},{9,8},{10,9... | collective-permute-start | bytes 1769480 | tf_op jit(solution)/shard_map/ppermute | solution.py:29
  120.5 37.2 %collective-permute-start.28 = (bf16[512,2048]{1,0:T(8,128)(2,1)}, bf16[512,2048]{1,0:T(8,128)(2,1)S(1)}, u32[]{:S(2)}, u32[]{:S(2)}) collective-permute-start(bf16[512,2048]{1,0:T(8,128)(2,1)} %param.23), channel_id=1, source_target_pairs={{0,8},{8,0},{16,24},{24,16},{1,9},{9,1},{17,25},{25,17},{2,10},{10... | collective-permute-start | bytes 6291464 | tf_op jit(solution)/shard_map/ppermute | solution.py:37
  120.6 39.1 %collective-permute-start.29 = (bf16[512,2048]{1,0:T(8,128)(2,1)}, bf16[512,2048]{1,0:T(8,128)(2,1)S(1)}, u32[]{:S(2)}, u32[]{:S(2)}) collective-permute-start(bf16[512,2048]{1,0:T(8,128)(2,1)} %collective-permute-done.13), channel_id=1, source_target_pairs={{0,8},{8,0},{16,24},{24,16},{1,9},{9,1},{17,25},{25,17},{2,10},{10... | collective-permute-start | bytes 6291464 | tf_op jit(solution)/shard_map/ppermute | solution.py:37
  154.8 53.4 %collective-permute-start.30 = (bf16[512,2048]{1,0:T(8,128)(2,1)S(1)}, bf16[512,2048]{1,0:T(8,128)(2,1)S(1)}, u32[]{:S(2)}, u32[]{:S(2)}) collective-permute-start(bf16[512,2048]{1,0:T(8,128)(2,1)S(1)} %copy-done.22), channel_id=1, source_target_pairs={{0,8},{8,0},{16,24},{24,16},{1,9},{9,1},{17,25},{25,17},{2,10},{10... | collective-permute-start | bytes 6291464 | tf_op jit(solution)/shard_map/ppermute | solution.py:37
  157.8 51.9 %collective-permute-start.31 = (bf16[512,2048]{1,0:T(8,128)(2,1)S(1)}, bf16[512,2048]{1,0:T(8,128)(2,1)S(1)}, u32[]{:S(2)}, u32[]{:S(2)}) collective-permute-start(bf16[512,2048]{1,0:T(8,128)(2,1)S(1)} %collective-permute-done.22), channel_id=1, source_target_pairs={{0,8},{8,0},{16,24},{24,16},{1,9},{9,1},{17,25},{25,17},{2,10},{10... | collective-permute-start | bytes 6291464 | tf_op jit(solution)/shard_map/ppermute | solution.py:37
  159.7 48.4 %collective-permute-start.23 = (bf16[512,2048]{1,0:T(8,128)(2,1)S(1)}, bf16[512,2048]{1,0:T(8,128)(2,1)S(1)}, u32[]{:S(2)}, u32[]{:S(2)}) collective-permute-start(bf16[512,2048]{1,0:T(8,128)(2,1)S(1)} %copy-done.23), channel_id=1, source_target_pairs={{0,16},{8,24},{16,0},{24,8},{1,17},{9,25},{17,1},{25,9},{2,18},{10... | collective-permute-start | bytes 6291464 | tf_op jit(solution)/shard_map/ppermute | solution.py:37
  192.9 29.0 %collective-permute-start.32 = (bf16[80,2048]{1,0:T(8,128)(2,1)S(1)}, bf16[80,2048]{1,0:T(8,128)(2,1)S(1)}, u32[]{:S(2)}, u32[]{:S(2)}) collective-permute-start(bf16[80,2048]{1,0:T(8,128)(2,1)S(1)} %slice.370), channel_id=1, source_target_pairs={{0,3},{1,0},{2,1},{3,2},{4,7},{5,4},{6,5},{7,6},{8,11},{9,8},{10,9... | collective-permute-start | bytes 983048 | tf_op jit(solution)/shard_map/ppermute | solution.py:29
  306.8 39.3 %collective-permute-start.39 = (bf16[144,2048]{1,0:T(8,128)(2,1)S(1)}, bf16[144,2048]{1,0:T(8,128)(2,1)S(1)}, u32[]{:S(2)}, u32[]{:S(2)}) collective-permute-start(bf16[144,2048]{1,0:T(8,128)(2,1)S(1)} %pad_maximum_fusion.12), channel_id=1, source_target_pairs={{0,1},{1,2},{2,3},{3,0},{4,5},{5,6},{6,7},{7,4},{8,9},{9,10},{10,1... | collective-permute-start | bytes 1769480 | tf_op jit(solution)/shard_map/ppermute | solution.py:29
  306.9 30.0 %collective-permute-start.42 = (bf16[80,2048]{1,0:T(8,128)(2,1)S(1)}, bf16[80,2048]{1,0:T(8,128)(2,1)S(1)}, u32[]{:S(2)}, u32[]{:S(2)}) collective-permute-start(bf16[80,2048]{1,0:T(8,128)(2,1)S(1)} %get-tuple-element.462), channel_id=1, source_target_pairs={{0,1},{1,2},{2,3},{3,0},{4,5},{5,6},{6,7},{7,4},{8,9},{9,10},{10,1... | collective-permute-start | bytes 983048 | tf_op jit(solution)/shard_map/ppermute | solution.py:29
  307.0 29.9 %collective-permute-start.43 = (bf16[64,2048]{1,0:T(8,128)(2,1)S(1)}, bf16[64,2048]{1,0:T(8,128)(2,1)S(1)}, u32[]{:S(2)}, u32[]{:S(2)}) collective-permute-start(bf16[64,2048]{1,0:T(8,128)(2,1)S(1)} %get-tuple-element.464), channel_id=1, source_target_pairs={{0,3},{1,0},{2,1},{3,2},{4,7},{5,4},{6,5},{7,6},{8,11},{9,8},{10,9... | collective-permute-start | bytes 786440 | tf_op jit(solution)/shard_map/ppermute | solution.py:29
  342.1 47.9 %collective-permute-start.51 = (bf16[1024,2048]{1,0:T(8,128)(2,1)}, bf16[1024,2048]{1,0:T(8,128)(2,1)S(1)}, u32[]{:S(2)}, u32[]{:S(2)}) collective-permute-start(bf16[1024,2048]{1,0:T(8,128)(2,1)} %convolution_convert_fusion), channel_id=1, source_target_pairs={{0,8},{8,0},{16,24},{24,16},{1,9},{9,1},{17,25},{25,17},{2,10},{10... | collective-permute-start | bytes 12582920 | tf_op jit(solution)/shard_map/ppermute | solution.py:37
  392.0 30.3 %collective-permute-start.58 = (bf16[256,2048]{1,0:T(8,128)(2,1)S(1)}, bf16[256,2048]{1,0:T(8,128)(2,1)S(1)}, u32[]{:S(2)}, u32[]{:S(2)}) collective-permute-start(bf16[256,2048]{1,0:T(8,128)(2,1)S(1)} %add_convert_fusion.9), channel_id=1, source_target_pairs={{0,4},{4,0},{1,5},{5,1},{2,6},{6,2},{3,7},{7,3},{8,12},{12,8},{9,1... | collective-permute-start | bytes 3145736 | tf_op jit(solution)/shard_map/ppermute | solution.py:33
  417.9 32.9 %collective-permute-start.60 = (bf16[256,2048]{1,0:T(8,128)(2,1)S(1)}, bf16[256,2048]{1,0:T(8,128)(2,1)S(1)}, u32[]{:S(2)}, u32[]{:S(2)}) collective-permute-start(bf16[256,2048]{1,0:T(8,128)(2,1)S(1)} %get-tuple-element.452), channel_id=1, source_target_pairs={{0,16},{8,24},{16,0},{24,8},{1,17},{9,25},{17,1},{25,9},{2,18},{10... | collective-permute-start | bytes 3145736 | tf_op jit(solution)/shard_map/ppermute | solution.py:37
  452.3 30.7 %collective-permute-start.61 = (bf16[256,2048]{1,0:T(8,128)(2,1)}, bf16[256,2048]{1,0:T(8,128)(2,1)}, u32[]{:S(2)}, u32[]{:S(2)}) collective-permute-start(bf16[256,2048]{1,0:T(8,128)(2,1)} %add_convert_fusion.7), channel_id=1, source_target_pairs={{0,4},{4,0},{1,5},{5,1},{2,6},{6,2},{3,7},{7,3},{8,12},{12,8},{9,1... | collective-permute-start | bytes 3145736 | tf_op jit(solution)/shard_map/ppermute | solution.py:33
  518.7 52.2 %collective-permute-start.78 = (bf16[256,2048]{1,0:T(8,128)(2,1)S(1)}, bf16[256,2048]{1,0:T(8,128)(2,1)S(1)}, u32[]{:S(2)}, u32[]{:S(2)}) collective-permute-start(bf16[256,2048]{1,0:T(8,128)(2,1)S(1)} %add_convert_fusion.5), channel_id=1, source_target_pairs={{0,4},{4,0},{1,5},{5,1},{2,6},{6,2},{3,7},{7,3},{8,12},{12,8},{9,1... | collective-permute-start | bytes 3145736 | tf_op jit(solution)/shard_map/ppermute | solution.py:33
  528.3 43.3 %collective-permute-start.77 = (bf16[512,512]{1,0:T(8,128)(2,1)S(1)}, bf16[512,512]{1,0:T(8,128)(2,1)S(1)}, u32[]{:S(2)}, u32[]{:S(2)}) collective-permute-start(bf16[512,512]{1,0:T(8,128)(2,1)S(1)} %add_convert_fusion.14), channel_id=1, source_target_pairs={{0,4},{4,0},{1,5},{5,1},{2,6},{6,2},{3,7},{7,3},{8,12},{12,8},{9,1... | collective-permute-start | bytes 1572872 | tf_op jit(solution)/shard_map/ppermute | solution.py:33
  531.0 30.5 %collective-permute-start.69 = (bf16[144,2048]{1,0:T(8,128)(2,1)S(1)}, bf16[144,2048]{1,0:T(8,128)(2,1)S(1)}, u32[]{:S(2)}, u32[]{:S(2)}) collective-permute-start(bf16[144,2048]{1,0:T(8,128)(2,1)S(1)} %pad_maximum_fusion.16), channel_id=1, source_target_pairs={{0,1},{1,2},{2,3},{3,0},{4,5},{5,6},{6,7},{7,4},{8,9},{9,10},{10,1... | collective-permute-start | bytes 1769480 | tf_op jit(solution)/shard_map/ppermute | solution.py:29
  (137 other events, 1865.6 us)

commit v3 on v2

--- a/solution.py
+++ b/solution.py
@@ -475,86 +475,78 @@
         return jnp.concatenate([p[0].astype(F32) + p[1].astype(F32) for p in pairs if p], axis=0)
 
     down_pair = grad_start(cot_all, hidden)
-    ffn_terms = mm(hidden, w_down, ((1,), (1,)), BF)
     down_half = grad_next(*down_pair, 2)
-    ffn_terms = line.wait(ffn_terms)
-    ffn_far = sum_rows_start(ffn_terms)
     grad_hidden = mm(line.after(cot_all), w_down, ((1,), (0,)))
     grad_gate = (grad_hidden * up * sig * (1.0 + gate * (1.0 - sig))).astype(BF)
     grad_up = (grad_hidden * silu).astype(BF)
     grad_gate, grad_up = line.wait((grad_gate, grad_up))
+    mid_terms = mm(grad_gate, w_gate, ((1,), (1,))) + mm(grad_up, w_up, ((1,), (1,)))
+    mid_terms = line.wait(mid_terms.astype(BF))
+    far = sum_rows_start(mid_terms)
+    far = line.wait(far)
+    near = sum_rows_next(mid_terms, far)
+    normed_left, grad_gate = line.after((normed_two_all, grad_gate))
+    gate_pair = grad_start(normed_left, grad_gate)
+    down_a = grad_end(down_half, 0)
+    gate_half = grad_next(*gate_pair, 2)
+    near = line.wait(near)
+    normed_two_grad = sum_rows_end(mid_terms, near)
+
+    resid = cot.astype(F32) + norm_backward(normed_two_grad, hat_two, scale_two, gain_two)
+    gain_two_part = jnp.sum(normed_two_grad * hat_two, axis=0)
+
+    resid_low = line.wait(resid.astype(BF))
+    near = gather_rows_start(resid_low)
+    normed_left, grad_up = line.after((normed_two_all, grad_up))
+    up_pair = grad_start(normed_left, grad_up)
+    down_b = grad_end(down_half, 1)
+    near = line.wait(near)
+    far = gather_rows_next(near)
+    gate_a = grad_end(gate_half, 0)
+    far = line.wait(far)
+    resid_all = gather_rows_end(resid_low, near, far)
+    grad_context = line.wait(mm(resid_all, w_out, ((1,), (0,)), BF))
+    g_own = grad_context[:, :QW]
+    g_oth = flip(grad_context[:, QW:])
+    ffn_terms = line.wait(mm(line.after(hidden), w_down, ((1,), (1,)), BF))
+    ffn_far = sum_rows_start(ffn_terms)
+    up_half = grad_next(*up_pair, 2)
+    g_oth = line.wait(g_oth)
+    gate_b = grad_end(gate_half, 1)
     ffn_far = line.wait(ffn_far)
     ffn_near = sum_rows_next(ffn_terms, ffn_far)
-    mid_terms = line.wait(mm(grad_gate, w_gate, ((1,), (1,))))
-    down_a = grad_end(down_half, 0)
-    mid_terms = line.wait((mid_terms + mm(grad_up, w_up, ((1,), (1,)))).astype(BF))
-    far = sum_rows_start(mid_terms)
-    normed_left, grad_gate = line.after((normed_two_all, grad_gate))
-    gate_pair = grad_start(normed_left, grad_gate)
-    down_b = grad_end(down_half, 1)
-    gate_half = grad_next(*gate_pair, 2)
-    far = line.wait(far)
-    near = sum_rows_next(mid_terms, far)
-    normed_left, grad_up = line.after((normed_two_all, grad_up))
-    up_pair = grad_start(normed_left, grad_up)
-    ffn_near = line.wait(ffn_near)
-    layer_output = (hidden_one + sum_rows_end(ffn_terms, ffn_near)).astype(BF)
-    down_a = line.wait(down_a)
-    gate_a = grad_end(gate_half, 0)
-    near = line.wait(near)
-    normed_two_grad = sum_rows_end(mid_terms, near)
-
-    resid = cot.astype(F32) + norm_backward(normed_two_grad, hat_two, scale_two, gain_two)
-    gain_two_part = jnp.sum(normed_two_grad * hat_two, axis=0)
-
-    resid_low = line.wait(resid.astype(BF))
-    near = gather_rows_start(resid_low)
-    up_half = grad_next(*up_pair, 2)
-    gate_b = grad_end(gate_half, 1)
-    down_b = line.wait(down_b)
-    near = line.wait(near)
-    far = gather_rows_next(near)
-    gate_a = line.wait(gate_a)
-    far = line.wait(far)
-    resid_all = gather_rows_end(resid_low, near, far)
-    gate_b, grad_context = line.wait((gate_b, mm(resid_all, w_out, ((1,), (0,)), BF)))
-    g_own = grad_context[:, :QW]
-    g_oth = flip(grad_context[:, QW:])
+    d_own, d_oth = attn_backward(
+        meta, rot, lse, g_own.astype(F32), g_oth.astype(F32), start_col, cos, sin
+    )
+    down_a, down_b, gate_a, gate_b, ffn_near, d_oth = line.wait(
+        (down_a, down_b, gate_a, gate_b, ffn_near, d_oth.astype(BF))
+    )
+    d_oth = flip(d_oth)
     resid_left, context = line.after((resid_all, context))
     out_pair = grad_start(resid_left, context)
-    g_oth = line.wait(g_oth)
+    up_half[0] = line.wait(up_half[0])
+    out_half = grad_next(*out_pair, 1)
+    layer_output = (hidden_one + sum_rows_end(ffn_terms, ffn_near)).astype(BF)
+    layer_output = line.wait(layer_output)
+    d_oth = line.wait(d_oth)
     up_a = grad_end(up_half, 0)
-    d_own, d_oth = attn_backward(
-        meta, rot, lse, g_own.astype(F32), g_oth.astype(F32), start_col, cos, sin
-    )
-    up_a, d_oth = line.wait((up_a, d_oth.astype(BF)))
-    d_oth = flip(d_oth)
-    out_half = grad_next(*out_pair, 1)
-    d_oth = line.wait(d_oth)
-    up_b = grad_end(up_half, 1)
     d_pack = jnp.concatenate([d_own.astype(BF), d_oth], axis=1)
     one_terms = mm(d_pack, w_pack, ((1,), (1,)))
-    one_low = line.wait(one_terms.astype(BF))
+    gain_one_part = jnp.sum(one_terms * hat_all, axis=0)
+    one_low, part = line.wait((one_terms.astype(BF), jnp.stack([gain_one_part, gain_two_part])))
     far = sum_rows_start(one_low)
+    part_terms = [part] + [shift(part, -step) for step in (1, 2, 3)]
     normed_left, d_pack = line.after((normed_all, d_pack))
     pack_pair = grad_start(normed_left, d_pack)
+    far = line.wait(far)
+    near = sum_rows_next(one_low, far)
+    up_b = grad_end(up_half, 1)
     out_full = grad_end(out_half, 0)
     pack_half = grad_next(*pack_pair, 1)
-    far = line.wait(far)
-    near = sum_rows_next(one_low, far)
-    gain_one_part = jnp.sum(one_terms * hat_all, axis=0)
-    part = line.wait(jnp.stack([gain_one_part, gain_two_part]))
-
-    part = line.wait(part + lax.ppermute(part, "tensor", [(i, i ^ 1) for i in range(4)]))
-    down_total = both(line.wait([down_a, down_b]))
-    part = line.wait(part + lax.ppermute(part, "tensor", [(i, i ^ 2) for i in range(4)]))
+
+    down_total = both([down_a, down_b])
     pack_full = grad_end(pack_half, 0)
-    size = width
-    for bit in bits[::-1]:
-        size = size // 2
-        part = line.wait(part[:, :size] + xor_send(part[:, size:], bit, count))
-    gain_total = part + flip(part)
-    gate_total = both(line.wait([gate_a, gate_b]))
+    gate_total = both([gate_a, gate_b])
 
     near = line.wait(near)
     normed_one_grad = sum_rows_end(one_low, near)
@@ -565,6 +557,14 @@
         return own_first(pair[0].astype(F32) + swap(pair[1]).astype(F32))
 
     up_total = both(line.wait([up_a, up_b]))
+
+    part_terms = jnp.stack(part_terms + part_terms)
+    part = jnp.sum(lax.dynamic_slice_in_dim(part_terms, (4 - z) % 4, 4, axis=0), axis=0)
+    size = width
+    for bit in bits[::-1]:
+        size = size // 2
+        part = part[:, :size] + xor_send(part[:, size:], bit, count)
+    gain_total = part + flip(part)
     out_total = both_swapped(line.wait(out_full))
     pack_total = both_swapped(pack_full)
     query_parts, key_parts, value_parts = (

time: 596 us -> 595 us (level)
  matrix products: 103 us -> 112 us
    ppermute x13, waiting for transfers between devices: 33.2 us -> 57.3 us  [flip(): return lax.ppermute(values, 'context', [(0, 1), (1, 0)])]
    ppermute x32 -> x35, waiting for transfers between devices: 101 us -> 83.9 us  [shift(): lax.ppermute(values, 'tensor', [(i, (i + step) % 4) for i in range(4)])]
    ppermute x2 -> x0, waiting for transfers between devices: 16.5 us -> none  [the longest x1 12.8 us: shards(): lax.ppermute(part, 'tensor', [(i, i ^ 1) for i in range(4)])]
    dot_general x20, matrix products: 103 us -> 112 us  [mm(): lax.dot_general(a, b, (dims, ((), ())), preferred_element_type=F32)]
    unnamed x194 -> x166, local copies, waits for them, and re-layouts: 29.6 us -> 26.7 us
    ppermute x32 -> x35, starting transfers between devices: 55.8 us -> 57.3 us  [shift(): lax.ppermute(values, 'tensor', [(i, (i + step) % 4) for i in range(4)])]
  transfers between devices with their start and end apart: 80 -> 81, of which waited for: 32 -> 33; matrix products, arithmetic and copies ran while one was open for 23% -> 23% of each run, Pallas kernels for 6% -> 6%
where the time goes in v3:
time: 595 us; the launch traced here: 592 us
  waiting for transfers between devices  255 us (43%)
  matrix products  112 us (19%)
  starting transfers between devices  92.9 us (16%)
  other arithmetic  44.9 us (8%)
  local copies, waits for them, and re-layouts  44.3 us (7%)
  Pallas kernels  37.4 us (6%)
    ppermute x33, waiting for transfers between devices, xor_send(): return lax.ppermute(values, 'shard', [(i, i ^ bit) for i in range(count)])  113 us
    dot_general x20, matrix products, mm(): lax.dot_general(a, b, (dims, ((), ())), preferred_element_type=F32)  112 us
    ppermute x35, waiting for transfers between devices, shift(): lax.ppermute(values, 'tensor', [(i, (i + step) % 4) for i in range(4)])  83.9 us
    ppermute x13, waiting for transfers between devices, flip(): return lax.ppermute(values, 'context', [(0, 1), (1, 0)])  57.3 us
    ppermute x35, starting transfers between devices, shift(): lax.ppermute(values, 'tensor', [(i, (i + step) % 4) for i in range(4)])  57.3 us
    unnamed x166, local copies, waits for them, and re-layouts  26.7 us
    pallas_call x1, Pallas kernels, attn_backward(): pl.pallas_call(attn_backward_kernel, out_shape=(jax.ShapeDtypeStruct((hal...  22.3 us
    ppermute x33, starting transfers between devices, xor_send(): return lax.ppermute(values, 'shard', [(i, i ^ bit) for i in range(count)])  20.5 us
  transfers between devices with their start and end apart: 81, of which 33 were waited for; matrix products, arithmetic and copies ran while one was open for 23% of the time, Pallas kernels for 6%

profile of v3, /device:TPU:0, one launch (start us, length us, event | category | flops | bytes accessed | tf_op | source)
XLA Modules:
  0.0 591.7 jit_solution(6371688393767113958)
XLA Ops:
  17.7 13.6 %collective-permute-done.2 = bf16[512,768]{1,0:T(8,128)(2,1)} collective-permute-done((bf16[512,768]{1,0:T(8,128)(2,1)S(1)}, bf16[512,768]{1,0:T(8,128)(2,1)}, u32[]{:S(2)}, u32[]{:S(2)}) %collective-permute-start.2) | collective-permute-done | bytes 786464 | tf_op jit(solution)/shard_map/ppermute | solution.py:37
  61.7 8.1 %collective-permute-done.11 = bf16[576,384]{1,0:T(8,128)(2,1)S(1)} collective-permute-done((bf16[576,384]{1,0:T(8,128)(2,1)}, bf16[576,384]{1,0:T(8,128)(2,1)S(1)}, u32[]{:S(2)}, u32[]{:S(2)}) %collective-permute-start.11) | collective-permute-done | bytes 442400 | tf_op jit(solution)/shard_map/ppermute | solution.py:33
  74.4 15.1 %attend_forward.1 = (f32[576,256]{1,0:T(8,128)S(1)}, f32[576,256]{1,0:T(8,128)S(1)}, f32[1152,384]{1,0:T(8,128)S(1)}, f32[1152,4]{1,0:T(8,128)S(1)}) custom-call(s32[2]{0:T(128)S(1)} %pad_add_fusion.meta, f32[576,384]{1,0:T(8,128)S(1)} %get-tuple-element.445.own, f32[576,384]{1,0:T(8,128)S(1)} %convert_element_type.392.oth, s32[1152,1]{1,0:T(8,128)S(1)} %bitcast.78, ...), custom_call_target="tpu_custom_call" | custom-call | flops 84934656 | bytes 221184 | tf_op jit(solution)/shard_map/attend_forward/pallas_call | solution.py:231
  98.1 11.9 %convolution_convert_fusion.4 = bf16[576,2048]{1,0:T(8,128)(2,1)S(1)} fusion(bf16[2048,512]{1,0:T(8,128)(2,1)S(1)} %constant_dynamic-update-slice_fusion.9, bf16[576,256]{1,0:T(8,128)(2,1)S(1)} %collective-permute-done.12, bf16[576,256]{1,0:T(8,128)(2,1)S(1)} %convert_element_type.394), kind=kOutput, calls=%fused_computation.24 | convolution fusion | flops 1210318848 | bytes 5046272 | tf_op jit(solution)/shard_map/dot_general | solution.py:25
  116.3 10.5 %collective-permute-done.19 = bf16[64,2048]{1,0:T(8,128)(2,1)S(1)} collective-permute-done((bf16[64,2048]{1,0:T(8,128)(2,1)S(1)}, bf16[64,2048]{1,0:T(8,128)(2,1)S(1)}, u32[]{:S(2)}, u32[]{:S(2)}) %collective-permute-start.19) | collective-permute-done | bytes 262176 | tf_op jit(solution)/shard_map/ppermute | solution.py:29
  134.3 26.9 %collective-permute-done.22 = bf16[512,2048]{1,0:T(8,128)(2,1)S(1)} collective-permute-done((bf16[512,2048]{1,0:T(8,128)(2,1)S(1)}, bf16[512,2048]{1,0:T(8,128)(2,1)S(1)}, u32[]{:S(2)}, u32[]{:S(2)}) %collective-permute-start.22) | collective-permute-done | bytes 2097184 | tf_op jit(solution)/shard_map/ppermute | solution.py:37
  170.3 10.7 %collective-permute-done.24 = bf16[144,2048]{1,0:T(8,128)(2,1)S(1)} collective-permute-done((bf16[144,2048]{1,0:T(8,128)(2,1)S(1)}, bf16[144,2048]{1,0:T(8,128)(2,1)S(1)}, u32[]{:S(2)}, u32[]{:S(2)}) %collective-permute-start.24) | collective-permute-done | bytes 589856 | tf_op jit(solution)/shard_map/ppermute | solution.py:29
  181.0 7.8 %collective-permute-done.25 = bf16[144,2048]{1,0:T(8,128)(2,1)S(1)} collective-permute-done((bf16[144,2048]{1,0:T(8,128)(2,1)S(1)}, bf16[144,2048]{1,0:T(8,128)(2,1)S(1)}, u32[]{:S(2)}, u32[]{:S(2)}) %collective-permute-start.25) | collective-permute-done | bytes 589856 | tf_op jit(solution)/shard_map/ppermute | solution.py:29
  192.7 10.5 %collective-permute-done.27 = bf16[64,2048]{1,0:T(8,128)(2,1)S(1)} collective-permute-done((bf16[64,2048]{1,0:T(8,128)(2,1)S(1)}, bf16[64,2048]{1,0:T(8,128)(2,1)S(1)}, u32[]{:S(2)}, u32[]{:S(2)}) %collective-permute-start.27) | collective-permute-done | bytes 262176 | tf_op jit(solution)/shard_map/ppermute | solution.py:29
  207.8 8.5 %fusion.54 = f32[576,2048]{1,0:T(8,128)} fusion(bf16[576,2048]{1,0:T(8,128)(2,1)} %constant_dynamic-update-slice_fusion.13, bf16[2048,2048]{1,0:T(8,128)(2,1)S(1)} %constant_dynamic-update-slice_fusion.18), kind=kOutput, calls=%fused_computation.219 | convolution fusion | flops 4831838208 | bytes 15466496 | tf_op jit(solution)/shard_map/dot_general | solution.py:25
  217.1 12.8 %multiply_convert_fusion.2 = (bf16[576,2048]{1,0:T(8,128)(2,1)}, f32[576,2048]{1,0:T(8,128)}) fusion(f32[576,2048]{1,0:T(8,128)} %fusion.54, bf16[576,2048]{1,0:T(8,128)(2,1)} %constant_dynamic-update-slice_fusion.13, bf16[2048,2048]{1,0:T(8,128)(2,1)S(1)} %constant_dynamic-update-slice_fusion.22), kind=kOutput, calls=%fused_computation.13 | convolution fusion | flops 4838916096 | bytes 22544384 | tf_op jit(solution)/shard_map/dot_general | solution.py:25
  255.3 11.8 %multiply_convert_fusion = (bf16[576,2048]{1,0:T(8,128)(2,1)S(1)}, bf16[576,2048]{1,0:T(8,128)(2,1)S(1)}) fusion(f32[576,2048]{1,0:T(8,128)} %fusion.54, f32[576,2048]{1,0:T(8,128)} %get-tuple-element.490, bf16[576,2048]{1,0:T(8,128)(2,1)} %copy-done.50, bf16[2048,2048]{1,0:T(8,128)(2,1)} %constant_dynamic-update-slice_fusion.31), kind=kOutput, calls=%fused_computation.11 | convolution fusion | flops 4847173632 | bytes 24903680 | tf_op jit(solution)/shard_map/dot_general | solution.py:25
  268.5 7.7 %fusion.55 = f32[576,2048]{1,0:T(8,128)S(1)} fusion(bf16[576,2048]{1,0:T(8,128)(2,1)S(1)} %get-tuple-element.320, bf16[2048,2048]{1,0:T(8,128)(2,1)} %copy-done.37), kind=kOutput, calls=%fused_computation.220 | convolution fusion | flops 4831838208 | bytes 15466496 | tf_op jit(solution)/shard_map/dot_general | solution.py:25
  285.8 11.6 %collective-permute-done.38 = bf16[64,2048]{1,0:T(8,128)(2,1)S(1)} collective-permute-done((bf16[64,2048]{1,0:T(8,128)(2,1)S(1)}, bf16[64,2048]{1,0:T(8,128)(2,1)S(1)}, u32[]{:S(2)}, u32[]{:S(2)}) %collective-permute-start.38) | collective-permute-done | bytes 262176 | tf_op jit(solution)/shard_map/ppermute | solution.py:29
  314.2 20.8 %collective-permute-done.42 = bf16[256,2048]{1,0:T(8,128)(2,1)S(1)} collective-permute-done((bf16[256,2048]{1,0:T(8,128)(2,1)S(1)}, bf16[256,2048]{1,0:T(8,128)(2,1)S(1)}, u32[]{:S(2)}, u32[]{:S(2)}) %collective-permute-start.42) | collective-permute-done | bytes 1048608 | tf_op jit(solution)/shard_map/ppermute | solution.py:37
  349.3 7.7 %collective-permute-done.45 = bf16[256,2048]{1,0:T(8,128)(2,1)S(1)} collective-permute-done((bf16[256,2048]{1,0:T(8,128)(2,1)S(1)}, bf16[256,2048]{1,0:T(8,128)(2,1)S(1)}, u32[]{:S(2)}, u32[]{:S(2)}) %collective-permute-start.45) | collective-permute-done | bytes 1048608 | tf_op jit(solution)/shard_map/ppermute | solution.py:37
  395.0 8.3 %convolution_convert_fusion.3 = bf16[576,2048]{1,0:T(8,128)(2,1)S(1)} fusion(bf16[576,2048]{1,0:T(8,128)(2,1)} %get-tuple-element.312, bf16[2048,2048]{1,0:T(8,128)(2,1)} %constant_dynamic-update-slice_fusion.31), kind=kOutput, calls=%fused_computation.23 | convolution fusion | flops 4833017856 | bytes 13107200 | tf_op jit(solution)/shard_map/dot_general | solution.py:25
  410.0 10.4 %collective-permute-done.53 = bf16[576,256]{1,0:T(8,128)(2,1)S(1)} collective-permute-done((bf16[576,256]{1,0:T(8,128)(2,1)S(1)}, bf16[576,256]{1,0:T(8,128)(2,1)S(1)}, u32[]{:S(2)}, u32[]{:S(2)}) %collective-permute-start.53) | collective-permute-done | bytes 294944 | tf_op jit(solution)/shard_map/ppermute | solution.py:33
  434.6 22.3 %attend_backward.1 = (f32[576,384]{1,0:T(8,128)S(1)}, f32[576,384]{1,0:T(8,128)S(1)}) custom-call(s32[2]{0:T(128)S(1)} %copy-done.3, f32[1152,384]{1,0:T(8,128)S(1)} %copy-done.1, f32[1152,4]{1,0:T(8,128)S(1)} %get-tuple-element.331.lse, f32[576,256]{1,0:T(8,128)S(1)} %get-tuple-element.456.own, f32[576,256]{1,0:T(8,128)S(1)} %convert_element_type.459.oth, ...), custom_call_target="tpu_custom_call" | custom-call | flops 84934656 | bytes 221184 | tf_op jit(solution)/shard_map/attend_backward/pallas_call | solution.py:252
  473.7 10.8 %collective-permute-done.61 = bf16[256,2048]{1,0:T(8,128)(2,1)S(1)} collective-permute-done((bf16[256,2048]{1,0:T(8,128)(2,1)S(1)}, bf16[256,2048]{1,0:T(8,128)(2,1)S(1)}, u32[]{:S(2)}, u32[]{:S(2)}) %collective-permute-start.61) | collective-permute-done | bytes 1048608 | tf_op jit(solution)/shard_map/ppermute | solution.py:37
  516.5 7.5 %collective-permute-done.68 = bf16[512,512]{1,0:T(8,128)(2,1)S(1)} collective-permute-done((bf16[512,512]{1,0:T(8,128)(2,1)S(1)}, bf16[512,512]{1,0:T(8,128)(2,1)S(1)}, u32[]{:S(2)}, u32[]{:S(2)}) %collective-permute-start.68) | collective-permute-done | bytes 524320 | tf_op jit(solution)/shard_map/ppermute | solution.py:37
  528.6 9.3 %collective-permute-done.76 = f32[2,512]{1,0:T(2,128)S(1)} collective-permute-done((f32[2,512]{1,0:T(2,128)S(1)}, f32[2,512]{1,0:T(2,128)S(1)}, u32[]{:S(2)}, u32[]{:S(2)}) %collective-permute-start.76) | collective-permute-done | bytes 4128 | tf_op jit(solution)/shard_map/ppermute | solution.py:33
  560.4 9.3 %collective-permute-done.77 = bf16[512,512]{1,0:T(8,128)(2,1)S(1)} collective-permute-done((bf16[512,512]{1,0:T(8,128)(2,1)S(1)}, bf16[512,512]{1,0:T(8,128)(2,1)S(1)}, u32[]{:S(2)}, u32[]{:S(2)}) %collective-permute-start.77) | collective-permute-done | bytes 524320 | tf_op jit(solution)/shard_map/ppermute | solution.py:33
  579.0 8.7 %collective-permute-done.80 = bf16[512,768]{1,0:T(8,128)(2,1)S(1)} collective-permute-done((bf16[512,768]{1,0:T(8,128)(2,1)S(1)}, bf16[512,768]{1,0:T(8,128)(2,1)S(1)}, u32[]{:S(2)}, u32[]{:S(2)}) %collective-permute-start.80) | collective-permute-done | bytes 786464 | tf_op jit(solution)/shard_map/ppermute | solution.py:33
  (472 shorter events, 303.9 us)
Async XLA Ops:
  51.8 46.1 %collective-permute-start.13 = (bf16[512,2048]{1,0:T(8,128)(2,1)}, bf16[512,2048]{1,0:T(8,128)(2,1)}, u32[]{:S(2)}, u32[]{:S(2)}) collective-permute-start(bf16[512,2048]{1,0:T(8,128)(2,1)} %param.23), channel_id=1, source_target_pairs={{0,16},{8,24},{16,0},{24,8},{1,17},{9,25},{17,1},{25,9},{2,18},{10... | collective-permute-start | bytes 6291464 | tf_op jit(solution)/shard_map/ppermute | solution.py:37
  53.1 36.5 %collective-permute-start.16 = (bf16[512,512]{1,0:T(8,128)(2,1)}, bf16[512,512]{1,0:T(8,128)(2,1)}, u32[]{:S(2)}, u32[]{:S(2)}) collective-permute-start(bf16[512,512]{1,0:T(8,128)(2,1)} %maximum_select_fusion.2), channel_id=1, source_target_pairs={{0,8},{8,0},{16,24},{24,16},{1,9},{9,1},{17,25},{25,17},{2,10},{10... | collective-permute-start | bytes 1572872 | tf_op jit(solution)/shard_map/ppermute | solution.py:37
  59.7 33.6 %collective-permute-start.17 = (bf16[512,512]{1,0:T(8,128)(2,1)}, bf16[512,512]{1,0:T(8,128)(2,1)}, u32[]{:S(2)}, u32[]{:S(2)}) collective-permute-start(bf16[512,512]{1,0:T(8,128)(2,1)} %collective-permute-done.5), channel_id=1, source_target_pairs={{0,8},{8,0},{16,24},{24,16},{1,9},{9,1},{17,25},{25,17},{2,10},{10... | collective-permute-start | bytes 1572872 | tf_op jit(solution)/shard_map/ppermute | solution.py:37
  60.3 34.2 %collective-permute-start.14 = (bf16[144,2048]{1,0:T(8,128)(2,1)}, bf16[144,2048]{1,0:T(8,128)(2,1)S(1)}, u32[]{:S(2)}, u32[]{:S(2)}) collective-permute-start(bf16[144,2048]{1,0:T(8,128)(2,1)} %get-tuple-element.227), channel_id=1, source_target_pairs={{0,1},{1,2},{2,3},{3,0},{4,5},{5,6},{6,7},{7,4},{8,9},{9,10},{10,1... | collective-permute-start | bytes 1769480 | tf_op jit(solution)/shard_map/ppermute | solution.py:29
  114.8 46.4 %collective-permute-start.22 = (bf16[512,2048]{1,0:T(8,128)(2,1)S(1)}, bf16[512,2048]{1,0:T(8,128)(2,1)S(1)}, u32[]{:S(2)}, u32[]{:S(2)}) collective-permute-start(bf16[512,2048]{1,0:T(8,128)(2,1)S(1)} %copy-done.22), channel_id=1, source_target_pairs={{0,16},{8,24},{16,0},{24,8},{1,17},{9,25},{17,1},{25,9},{2,18},{10... | collective-permute-start | bytes 6291464 | tf_op jit(solution)/shard_map/ppermute | solution.py:37
  126.9 34.3 %collective-permute-start.21 = (bf16[144,2048]{1,0:T(8,128)(2,1)S(1)}, bf16[144,2048]{1,0:T(8,128)(2,1)S(1)}, u32[]{:S(2)}, u32[]{:S(2)}) collective-permute-start(bf16[144,2048]{1,0:T(8,128)(2,1)S(1)} %pad_maximum_fusion.11), channel_id=1, source_target_pairs={{0,3},{1,0},{2,1},{3,2},{4,7},{5,4},{6,5},{7,6},{8,11},{9,8},{10,9... | collective-permute-start | bytes 1769480 | tf_op jit(solution)/shard_map/ppermute | solution.py:29
  129.4 31.8 %collective-permute-start.20 = (bf16[144,2048]{1,0:T(8,128)(2,1)S(1)}, bf16[144,2048]{1,0:T(8,128)(2,1)S(1)}, u32[]{:S(2)}, u32[]{:S(2)}) collective-permute-start(bf16[144,2048]{1,0:T(8,128)(2,1)S(1)} %pad_maximum_fusion.10), channel_id=1, source_target_pairs={{0,1},{1,2},{2,3},{3,0},{4,5},{5,6},{6,7},{7,4},{8,9},{9,10},{10,1... | collective-permute-start | bytes 1769480 | tf_op jit(solution)/shard_map/ppermute | solution.py:29
  130.3 36.8 %collective-permute-start.28 = (bf16[512,2048]{1,0:T(8,128)(2,1)}, bf16[512,2048]{1,0:T(8,128)(2,1)S(1)}, u32[]{:S(2)}, u32[]{:S(2)}) collective-permute-start(bf16[512,2048]{1,0:T(8,128)(2,1)} %param.23), channel_id=1, source_target_pairs={{0,8},{8,0},{16,24},{24,16},{1,9},{9,1},{17,25},{25,17},{2,10},{10... | collective-permute-start | bytes 6291464 | tf_op jit(solution)/shard_map/ppermute | solution.py:37
  130.3 37.5 %collective-permute-start.29 = (bf16[512,2048]{1,0:T(8,128)(2,1)}, bf16[512,2048]{1,0:T(8,128)(2,1)S(1)}, u32[]{:S(2)}, u32[]{:S(2)}) collective-permute-start(bf16[512,2048]{1,0:T(8,128)(2,1)} %collective-permute-done.13), channel_id=1, source_target_pairs={{0,8},{8,0},{16,24},{24,16},{1,9},{9,1},{17,25},{25,17},{2,10},{10... | collective-permute-start | bytes 6291464 | tf_op jit(solution)/shard_map/ppermute | solution.py:37
  166.8 49.9 %collective-permute-start.30 = (bf16[512,2048]{1,0:T(8,128)(2,1)S(1)}, bf16[512,2048]{1,0:T(8,128)(2,1)S(1)}, u32[]{:S(2)}, u32[]{:S(2)}) collective-permute-start(bf16[512,2048]{1,0:T(8,128)(2,1)S(1)} %copy-done.22), channel_id=1, source_target_pairs={{0,8},{8,0},{16,24},{24,16},{1,9},{9,1},{17,25},{25,17},{2,10},{10... | collective-permute-start | bytes 6291464 | tf_op jit(solution)/shard_map/ppermute | solution.py:37
  167.1 49.8 %collective-permute-start.31 = (bf16[512,2048]{1,0:T(8,128)(2,1)S(1)}, bf16[512,2048]{1,0:T(8,128)(2,1)S(1)}, u32[]{:S(2)}, u32[]{:S(2)}) collective-permute-start(bf16[512,2048]{1,0:T(8,128)(2,1)S(1)} %collective-permute-done.22), channel_id=1, source_target_pairs={{0,8},{8,0},{16,24},{24,16},{1,9},{9,1},{17,25},{25,17},{2,10},{10... | collective-permute-start | bytes 6291464 | tf_op jit(solution)/shard_map/ppermute | solution.py:37
  168.7 48.0 %collective-permute-start.23 = (bf16[512,2048]{1,0:T(8,128)(2,1)S(1)}, bf16[512,2048]{1,0:T(8,128)(2,1)S(1)}, u32[]{:S(2)}, u32[]{:S(2)}) collective-permute-start(bf16[512,2048]{1,0:T(8,128)(2,1)S(1)} %copy-done.23), channel_id=1, source_target_pairs={{0,16},{8,24},{16,0},{24,8},{1,17},{9,25},{17,1},{25,9},{2,18},{10... | collective-permute-start | bytes 6291464 | tf_op jit(solution)/shard_map/ppermute | solution.py:37
  303.9 33.1 %collective-permute-start.41 = (bf16[1024,2048]{1,0:T(8,128)(2,1)}, bf16[1024,2048]{1,0:T(8,128)(2,1)}, u32[]{:S(2)}, u32[]{:S(2)}) collective-permute-start(bf16[1024,2048]{1,0:T(8,128)(2,1)} %convolution_convert_fusion.1), channel_id=1, source_target_pairs={{0,8},{8,0},{16,24},{24,16},{1,9},{9,1},{17,25},{25,17},{2,10},{10... | collective-permute-start | bytes 12582920 | tf_op jit(solution)/shard_map/ppermute | solution.py:37
  310.5 46.5 %collective-permute-start.45 = (bf16[256,2048]{1,0:T(8,128)(2,1)S(1)}, bf16[256,2048]{1,0:T(8,128)(2,1)S(1)}, u32[]{:S(2)}, u32[]{:S(2)}) collective-permute-start(bf16[256,2048]{1,0:T(8,128)(2,1)S(1)} %get-tuple-element.416), channel_id=1, source_target_pairs={{0,16},{8,24},{16,0},{24,8},{1,17},{9,25},{17,1},{25,9},{2,18},{10... | collective-permute-start | bytes 3145736 | tf_op jit(solution)/shard_map/ppermute | solution.py:37
  311.2 31.6 %collective-permute-start.40 = (bf16[144,2048]{1,0:T(8,128)(2,1)S(1)}, bf16[144,2048]{1,0:T(8,128)(2,1)S(1)}, u32[]{:S(2)}, u32[]{:S(2)}) collective-permute-start(bf16[144,2048]{1,0:T(8,128)(2,1)S(1)} %pad_maximum_fusion.13), channel_id=1, source_target_pairs={{0,3},{1,0},{2,1},{3,2},{4,7},{5,4},{6,5},{7,6},{8,11},{9,8},{10,9... | collective-permute-start | bytes 1769480 | tf_op jit(solution)/shard_map/ppermute | solution.py:29
  335.4 98.6 %collective-permute-start.49 = (bf16[256,2048]{1,0:T(8,128)(2,1)S(1)}, bf16[256,2048]{1,0:T(8,128)(2,1)S(1)}, u32[]{:S(2)}, u32[]{:S(2)}) collective-permute-start(bf16[256,2048]{1,0:T(8,128)(2,1)S(1)} %add_convert_fusion.11), channel_id=1, source_target_pairs={{0,4},{4,0},{1,5},{5,1},{2,6},{6,2},{3,7},{7,3},{8,12},{12,8},{9,1... | collective-permute-start | bytes 3145736 | tf_op jit(solution)/shard_map/ppermute | solution.py:33
  365.5 38.5 %collective-permute-start.54 = (bf16[1024,2048]{1,0:T(8,128)(2,1)}, bf16[1024,2048]{1,0:T(8,128)(2,1)S(1)}, u32[]{:S(2)}, u32[]{:S(2)}) collective-permute-start(bf16[1024,2048]{1,0:T(8,128)(2,1)} %convolution_convert_fusion), channel_id=1, source_target_pairs={{0,8},{8,0},{16,24},{24,16},{1,9},{9,1},{17,25},{25,17},{2,10},{10... | collective-permute-start | bytes 12582920 | tf_op jit(solution)/shard_map/ppermute | solution.py:37
  365.6 56.3 %collective-permute-start.52 = (bf16[256,2048]{1,0:T(8,128)(2,1)S(1)}, bf16[256,2048]{1,0:T(8,128)(2,1)S(1)}, u32[]{:S(2)}, u32[]{:S(2)}) collective-permute-start(bf16[256,2048]{1,0:T(8,128)(2,1)S(1)} %get-tuple-element.414), channel_id=1, source_target_pairs={{0,16},{8,24},{16,0},{24,8},{1,17},{9,25},{17,1},{25,9},{2,18},{10... | collective-permute-start | bytes 3145736 | tf_op jit(solution)/shard_map/ppermute | solution.py:37
  392.0 66.3 %collective-permute-start.50 = (bf16[256,2048]{1,0:T(8,128)(2,1)S(1)}, bf16[256,2048]{1,0:T(8,128)(2,1)S(1)}, u32[]{:S(2)}, u32[]{:S(2)}) collective-permute-start(bf16[256,2048]{1,0:T(8,128)(2,1)S(1)} %add_convert_fusion.10), channel_id=1, source_target_pairs={{0,4},{4,0},{1,5},{5,1},{2,6},{6,2},{3,7},{7,3},{8,12},{12,8},{9,1... | collective-permute-start | bytes 3145736 | tf_op jit(solution)/shard_map/ppermute | solution.py:33
  421.9 37.9 %collective-permute-start.51 = (bf16[256,2048]{1,0:T(8,128)(2,1)S(1)}, bf16[256,2048]{1,0:T(8,128)(2,1)S(1)}, u32[]{:S(2)}, u32[]{:S(2)}) collective-permute-start(bf16[256,2048]{1,0:T(8,128)(2,1)S(1)} %add_convert_fusion.9), channel_id=1, source_target_pairs={{0,4},{4,0},{1,5},{5,1},{2,6},{6,2},{3,7},{7,3},{8,12},{12,8},{9,1... | collective-permute-start | bytes 3145736 | tf_op jit(solution)/shard_map/ppermute | solution.py:33
  432.3 32.3 %collective-permute-start.55 = (bf16[256,2048]{1,0:T(8,128)(2,1)S(1)}, bf16[256,2048]{1,0:T(8,128)(2,1)S(1)}, u32[]{:S(2)}, u32[]{:S(2)}) collective-permute-start(bf16[256,2048]{1,0:T(8,128)(2,1)S(1)} %add_convert_fusion.8), channel_id=1, source_target_pairs={{0,4},{4,0},{1,5},{5,1},{2,6},{6,2},{3,7},{7,3},{8,12},{12,8},{9,1... | collective-permute-start | bytes 3145736 | tf_op jit(solution)/shard_map/ppermute | solution.py:33
  459.8 53.8 %collective-permute-start.69 = (bf16[256,2048]{1,0:T(8,128)(2,1)}, bf16[256,2048]{1,0:T(8,128)(2,1)}, u32[]{:S(2)}, u32[]{:S(2)}) collective-permute-start(bf16[256,2048]{1,0:T(8,128)(2,1)} %get-tuple-element.411), channel_id=1, source_target_pairs={{0,16},{8,24},{16,0},{24,8},{1,17},{9,25},{17,1},{25,9},{2,18},{10... | collective-permute-start | bytes 3145736 | tf_op jit(solution)/shard_map/ppermute | solution.py:37
  511.4 41.9 %collective-permute-start.78 = (bf16[256,2048]{1,0:T(8,128)(2,1)}, bf16[256,2048]{1,0:T(8,128)(2,1)S(1)}, u32[]{:S(2)}, u32[]{:S(2)}) collective-permute-start(bf16[256,2048]{1,0:T(8,128)(2,1)} %add_convert_fusion.6), channel_id=1, source_target_pairs={{0,4},{4,0},{1,5},{5,1},{2,6},{6,2},{3,7},{7,3},{8,12},{12,8},{9,1... | collective-permute-start | bytes 3145736 | tf_op jit(solution)/shard_map/ppermute | solution.py:33
  527.0 33.3 %collective-permute-start.79 = (bf16[256,2048]{1,0:T(8,128)(2,1)S(1)}, bf16[256,2048]{1,0:T(8,128)(2,1)S(1)}, u32[]{:S(2)}, u32[]{:S(2)}) collective-permute-start(bf16[256,2048]{1,0:T(8,128)(2,1)S(1)} %add_convert_fusion.5), channel_id=1, source_target_pairs={{0,4},{4,0},{1,5},{5,1},{2,6},{6,2},{3,7},{7,3},{8,12},{12,8},{9,1... | collective-permute-start | bytes 3145736 | tf_op jit(solution)/shard_map/ppermute | solution.py:33
  (124 other events, 1531.8 us)

commit v4 on v3

--- a/solution.py
+++ b/solution.py
@@ -501,15 +501,14 @@
     up_pair = grad_start(normed_left, grad_up)
     down_b = grad_end(down_half, 1)
     near = line.wait(near)
-    far = gather_rows_next(near)
-    gate_a = grad_end(gate_half, 0)
-    far = line.wait(far)
+    far = line.wait(gather_rows_next(near))
     resid_all = gather_rows_end(resid_low, near, far)
     grad_context = line.wait(mm(resid_all, w_out, ((1,), (0,)), BF))
     g_own = grad_context[:, :QW]
     g_oth = flip(grad_context[:, QW:])
     ffn_terms = line.wait(mm(line.after(hidden), w_down, ((1,), (1,)), BF))
     ffn_far = sum_rows_start(ffn_terms)
+    gate_a = grad_end(gate_half, 0)
     up_half = grad_next(*up_pair, 2)
     g_oth = line.wait(g_oth)
     gate_b = grad_end(gate_half, 1)
@@ -518,33 +517,30 @@
     d_own, d_oth = attn_backward(
         meta, rot, lse, g_own.astype(F32), g_oth.astype(F32), start_col, cos, sin
     )
-    down_a, down_b, gate_a, gate_b, ffn_near, d_oth = line.wait(
-        (down_a, down_b, gate_a, gate_b, ffn_near, d_oth.astype(BF))
+    down_a, down_b, gate_a, gate_b, ffn_near, up_half[0], d_oth = line.wait(
+        (down_a, down_b, gate_a, gate_b, ffn_near, up_half[0], d_oth.astype(BF))
     )
     d_oth = flip(d_oth)
-    resid_left, context = line.after((resid_all, context))
-    out_pair = grad_start(resid_left, context)
-    up_half[0] = line.wait(up_half[0])
-    out_half = grad_next(*out_pair, 1)
+    up_a = grad_end(up_half, 0)
     layer_output = (hidden_one + sum_rows_end(ffn_terms, ffn_near)).astype(BF)
     layer_output = line.wait(layer_output)
     d_oth = line.wait(d_oth)
-    up_a = grad_end(up_half, 0)
     d_pack = jnp.concatenate([d_own.astype(BF), d_oth], axis=1)
     one_terms = mm(d_pack, w_pack, ((1,), (1,)))
     gain_one_part = jnp.sum(one_terms * hat_all, axis=0)
     one_low, part = line.wait((one_terms.astype(BF), jnp.stack([gain_one_part, gain_two_part])))
     far = sum_rows_start(one_low)
     part_terms = [part] + [shift(part, -step) for step in (1, 2, 3)]
-    normed_left, d_pack = line.after((normed_all, d_pack))
+    normed_left, d_pack, resid_left, context = line.after((normed_all, d_pack, resid_all, context))
     pack_pair = grad_start(normed_left, d_pack)
     far = line.wait(far)
     near = sum_rows_next(one_low, far)
+    out_half = grad_next(*grad_start(resid_left, context), 1)
     up_b = grad_end(up_half, 1)
     out_full = grad_end(out_half, 0)
     pack_half = grad_next(*pack_pair, 1)
 
-    down_total = both([down_a, down_b])
+    down_total = both(line.wait([down_a, down_b]))
     pack_full = grad_end(pack_half, 0)
     gate_total = both([gate_a, gate_b])
 

time: 595 us -> 589 us (0.990)
  waiting for transfers between devices: 255 us -> 239 us
  other arithmetic: 44.9 us -> 52.7 us
    ppermute x13, waiting for transfers between devices: 57.3 us -> 40.2 us  [flip(): return lax.ppermute(values, 'context', [(0, 1), (1, 0)])]
    ppermute x35, waiting for transfers between devices: 83.9 us -> 94.1 us  [shift(): lax.ppermute(values, 'tensor', [(i, (i + step) % 4) for i in range(4)])]
    ppermute x33, waiting for transfers between devices: 113 us -> 105 us  [xor_send(): return lax.ppermute(values, 'shard', [(i, i ^ bit) for i in range(count)])]
    unnamed x166 -> x176, local copies, waits for them, and re-layouts: 26.7 us -> 26.1 us
  transfers between devices with their start and end apart: 81 -> 81, of which waited for: 33 -> 36; matrix products, arithmetic and copies ran while one was open for 23% -> 24% of each run, Pallas kernels for 6% -> 6%
where the time goes in v4:
time: 589 us; the launch traced here: 586 us
  waiting for transfers between devices  239 us (41%)
  matrix products  111 us (19%)
  starting transfers between devices  95.1 us (16%)
  other arithmetic  52.7 us (9%)
  local copies, waits for them, and re-layouts  44.8 us (8%)
  Pallas kernels  37.4 us (6%)
    dot_general x20, matrix products, mm(): lax.dot_general(a, b, (dims, ((), ())), preferred_element_type=F32)  111 us
    ppermute x33, waiting for transfers between devices, xor_send(): return lax.ppermute(values, 'shard', [(i, i ^ bit) for i in range(count)])  105 us
    ppermute x35, waiting for transfers between devices, shift(): lax.ppermute(values, 'tensor', [(i, (i + step) % 4) for i in range(4)])  94.1 us
    ppermute x35, starting transfers between devices, shift(): lax.ppermute(values, 'tensor', [(i, (i + step) % 4) for i in range(4)])  59.6 us
    ppermute x13, waiting for transfers between devices, flip(): return lax.ppermute(values, 'context', [(0, 1), (1, 0)])  40.2 us
    unnamed x176, local copies, waits for them, and re-layouts  26.1 us
    pallas_call x1, Pallas kernels, attn_backward(): pl.pallas_call(attn_backward_kernel, out_shape=(jax.ShapeDtypeStruct((hal...  22.3 us
    ppermute x33, starting transfers between devices, xor_send(): return lax.ppermute(values, 'shard', [(i, i ^ bit) for i in range(count)])  20.7 us
  transfers between devices with their start and end apart: 81, of which 36 were waited for; matrix products, arithmetic and copies ran while one was open for 24% of the time, Pallas kernels for 6%

profile of v4, /device:TPU:0, one launch (start us, length us, event | category | flops | bytes accessed | tf_op | source)
XLA Modules:
  0.0 586.0 jit_solution(5176975409039077187)
XLA Ops:
  18.1 13.7 %collective-permute-done.2 = bf16[512,768]{1,0:T(8,128)(2,1)} collective-permute-done((bf16[512,768]{1,0:T(8,128)(2,1)S(1)}, bf16[512,768]{1,0:T(8,128)(2,1)}, u32[]{:S(2)}, u32[]{:S(2)}) %collective-permute-start.2) | collective-permute-done | bytes 786464 | tf_op jit(solution)/shard_map/ppermute | solution.py:37
  62.2 8.1 %collective-permute-done.11 = bf16[576,384]{1,0:T(8,128)(2,1)S(1)} collective-permute-done((bf16[576,384]{1,0:T(8,128)(2,1)}, bf16[576,384]{1,0:T(8,128)(2,1)S(1)}, u32[]{:S(2)}, u32[]{:S(2)}) %collective-permute-start.11) | collective-permute-done | bytes 442400 | tf_op jit(solution)/shard_map/ppermute | solution.py:33
  74.9 15.1 %attend_forward.1 = (f32[576,256]{1,0:T(8,128)S(1)}, f32[576,256]{1,0:T(8,128)S(1)}, f32[1152,384]{1,0:T(8,128)S(1)}, f32[1152,4]{1,0:T(8,128)S(1)}) custom-call(s32[2]{0:T(128)S(1)} %pad_add_fusion.meta, f32[576,384]{1,0:T(8,128)S(1)} %get-tuple-element.451.own, f32[576,384]{1,0:T(8,128)S(1)} %convert_element_type.392.oth, s32[1152,1]{1,0:T(8,128)S(1)} %bitcast.78, ...), custom_call_target="tpu_custom_call" | custom-call | flops 84934656 | bytes 221184 | tf_op jit(solution)/shard_map/attend_forward/pallas_call | solution.py:231
  98.6 11.9 %convolution_convert_fusion.4 = bf16[576,2048]{1,0:T(8,128)(2,1)S(1)} fusion(bf16[2048,512]{1,0:T(8,128)(2,1)S(1)} %constant_dynamic-update-slice_fusion.9, bf16[576,256]{1,0:T(8,128)(2,1)S(1)} %collective-permute-done.12, bf16[576,256]{1,0:T(8,128)(2,1)S(1)} %convert_element_type.394), kind=kOutput, calls=%fused_computation.24 | convolution fusion | flops 1210318848 | bytes 5046272 | tf_op jit(solution)/shard_map/dot_general | solution.py:25
  116.8 10.5 %collective-permute-done.19 = bf16[64,2048]{1,0:T(8,128)(2,1)S(1)} collective-permute-done((bf16[64,2048]{1,0:T(8,128)(2,1)S(1)}, bf16[64,2048]{1,0:T(8,128)(2,1)S(1)}, u32[]{:S(2)}, u32[]{:S(2)}) %collective-permute-start.19) | collective-permute-done | bytes 262176 | tf_op jit(solution)/shard_map/ppermute | solution.py:29
  134.8 26.9 %collective-permute-done.22 = bf16[512,2048]{1,0:T(8,128)(2,1)S(1)} collective-permute-done((bf16[512,2048]{1,0:T(8,128)(2,1)S(1)}, bf16[512,2048]{1,0:T(8,128)(2,1)S(1)}, u32[]{:S(2)}, u32[]{:S(2)}) %collective-permute-start.22) | collective-permute-done | bytes 2097184 | tf_op jit(solution)/shard_map/ppermute | solution.py:37
  170.0 10.5 %collective-permute-done.24 = bf16[144,2048]{1,0:T(8,128)(2,1)S(1)} collective-permute-done((bf16[144,2048]{1,0:T(8,128)(2,1)S(1)}, bf16[144,2048]{1,0:T(8,128)(2,1)S(1)}, u32[]{:S(2)}, u32[]{:S(2)}) %collective-permute-start.24) | collective-permute-done | bytes 589856 | tf_op jit(solution)/shard_map/ppermute | solution.py:29
  180.5 7.8 %collective-permute-done.25 = bf16[144,2048]{1,0:T(8,128)(2,1)S(1)} collective-permute-done((bf16[144,2048]{1,0:T(8,128)(2,1)S(1)}, bf16[144,2048]{1,0:T(8,128)(2,1)S(1)}, u32[]{:S(2)}, u32[]{:S(2)}) %collective-permute-start.25) | collective-permute-done | bytes 589856 | tf_op jit(solution)/shard_map/ppermute | solution.py:29
  192.3 10.5 %collective-permute-done.27 = bf16[64,2048]{1,0:T(8,128)(2,1)S(1)} collective-permute-done((bf16[64,2048]{1,0:T(8,128)(2,1)S(1)}, bf16[64,2048]{1,0:T(8,128)(2,1)S(1)}, u32[]{:S(2)}, u32[]{:S(2)}) %collective-permute-start.27) | collective-permute-done | bytes 262176 | tf_op jit(solution)/shard_map/ppermute | solution.py:29
  207.3 8.4 %fusion.54 = f32[576,2048]{1,0:T(8,128)} fusion(bf16[576,2048]{1,0:T(8,128)(2,1)} %constant_dynamic-update-slice_fusion.13, bf16[2048,2048]{1,0:T(8,128)(2,1)S(1)} %constant_dynamic-update-slice_fusion.18), kind=kOutput, calls=%fused_computation.219 | convolution fusion | flops 4831838208 | bytes 15466496 | tf_op jit(solution)/shard_map/dot_general | solution.py:25
  218.8 10.7 %multiply_convert_fusion.2 = (bf16[576,2048]{1,0:T(8,128)(2,1)S(1)}, f32[576,2048]{1,0:T(8,128)}) fusion(f32[576,2048]{1,0:T(8,128)S(1)} %copy-done.69, bf16[576,2048]{1,0:T(8,128)(2,1)} %constant_dynamic-update-slice_fusion.13, bf16[2048,2048]{1,0:T(8,128)(2,1)S(1)} %constant_dynamic-update-slice_fusion.22), kind=kOutput, calls=%fused_computation.13 | convolution fusion | flops 4838916096 | bytes 22544384 | tf_op jit(solution)/shard_map/dot_general | solution.py:25
  250.5 13.0 %multiply_convert_fusion = (bf16[576,2048]{1,0:T(8,128)(2,1)S(1)}, bf16[576,2048]{1,0:T(8,128)(2,1)}) fusion(f32[576,2048]{1,0:T(8,128)} %fusion.54, f32[576,2048]{1,0:T(8,128)} %get-tuple-element.496, bf16[576,2048]{1,0:T(8,128)(2,1)} %copy-done.50, bf16[2048,2048]{1,0:T(8,128)(2,1)} %constant_dynamic-update-slice_fusion.31), kind=kOutput, calls=%fused_computation.11 | convolution fusion | flops 4847173632 | bytes 24903680 | tf_op jit(solution)/shard_map/dot_general | solution.py:25
  263.5 10.9 %fusion.55 = f32[576,2048]{1,0:T(8,128)} fusion(bf16[576,2048]{1,0:T(8,128)(2,1)S(1)} %get-tuple-element.323, bf16[2048,2048]{1,0:T(8,128)(2,1)} %copy-done.41), kind=kOutput, calls=%fused_computation.220 | convolution fusion | flops 4831838208 | bytes 15466496 | tf_op jit(solution)/shard_map/dot_general | solution.py:25
  274.4 8.0 %add_convert_fusion.3 = bf16[576,2048]{1,0:T(8,128)(2,1)S(1)} fusion(f32[576,2048]{1,0:T(8,128)} %fusion.55, bf16[576,2048]{1,0:T(8,128)(2,1)} %get-tuple-element.288, bf16[2048,2048]{1,0:T(8,128)(2,1)S(1)} %bitcast.81), kind=kOutput, calls=%fused_computation.10 | convolution fusion | flops 4834197504 | bytes 17825792 | tf_op jit(solution)/shard_map/dot_general | solution.py:25
  286.4 11.6 %collective-permute-done.38 = bf16[64,2048]{1,0:T(8,128)(2,1)S(1)} collective-permute-done((bf16[64,2048]{1,0:T(8,128)(2,1)S(1)}, bf16[64,2048]{1,0:T(8,128)(2,1)S(1)}, u32[]{:S(2)}, u32[]{:S(2)}) %collective-permute-start.38) | collective-permute-done | bytes 262176 | tf_op jit(solution)/shard_map/ppermute | solution.py:29
  308.2 21.0 %collective-permute-done.42 = bf16[256,2048]{1,0:T(8,128)(2,1)S(1)} collective-permute-done((bf16[256,2048]{1,0:T(8,128)(2,1)S(1)}, bf16[256,2048]{1,0:T(8,128)(2,1)S(1)}, u32[]{:S(2)}, u32[]{:S(2)}) %collective-permute-start.42) | collective-permute-done | bytes 1048608 | tf_op jit(solution)/shard_map/ppermute | solution.py:37
  357.3 10.2 %collective-permute-done.44 = bf16[144,2048]{1,0:T(8,128)(2,1)S(1)} collective-permute-done((bf16[144,2048]{1,0:T(8,128)(2,1)S(1)}, bf16[144,2048]{1,0:T(8,128)(2,1)S(1)}, u32[]{:S(2)}, u32[]{:S(2)}) %collective-permute-start.44) | collective-permute-done | bytes 589856 | tf_op jit(solution)/shard_map/ppermute | solution.py:29
  371.6 10.8 %collective-permute-done.47 = bf16[64,2048]{1,0:T(8,128)(2,1)S(1)} collective-permute-done((bf16[64,2048]{1,0:T(8,128)(2,1)S(1)}, bf16[64,2048]{1,0:T(8,128)(2,1)S(1)}, u32[]{:S(2)}, u32[]{:S(2)}) %collective-permute-start.47) | collective-permute-done | bytes 262176 | tf_op jit(solution)/shard_map/ppermute | solution.py:29
  387.4 8.3 %convolution_convert_fusion.3 = bf16[576,2048]{1,0:T(8,128)(2,1)S(1)} fusion(bf16[576,2048]{1,0:T(8,128)(2,1)} %copy-done.64, bf16[2048,2048]{1,0:T(8,128)(2,1)} %constant_dynamic-update-slice_fusion.31), kind=kOutput, calls=%fused_computation.23 | convolution fusion | flops 4833017856 | bytes 13107200 | tf_op jit(solution)/shard_map/dot_general | solution.py:25
  438.8 22.3 %attend_backward.1 = (f32[576,384]{1,0:T(8,128)S(1)}, f32[576,384]{1,0:T(8,128)S(1)}) custom-call(s32[2]{0:T(128)S(1)} %copy-done.3, f32[1152,384]{1,0:T(8,128)S(1)} %copy-done.1, f32[1152,4]{1,0:T(8,128)S(1)} %get-tuple-element.335.lse, f32[576,256]{1,0:T(8,128)S(1)} %get-tuple-element.462.own, f32[576,256]{1,0:T(8,128)S(1)} %convert_element_type.459.oth, ...), custom_call_target="tpu_custom_call" | custom-call | flops 84934656 | bytes 221184 | tf_op jit(solution)/shard_map/attend_backward/pallas_call | solution.py:252
  517.4 10.9 %collective-permute-done.68 = bf16[512,512]{1,0:T(8,128)(2,1)S(1)} collective-permute-done((bf16[512,512]{1,0:T(8,128)(2,1)S(1)}, bf16[512,512]{1,0:T(8,128)(2,1)S(1)}, u32[]{:S(2)}, u32[]{:S(2)}) %collective-permute-start.68) | collective-permute-done | bytes 524320 | tf_op jit(solution)/shard_map/ppermute | solution.py:37
  533.4 16.6 %collective-permute-done.70 = bf16[512,768]{1,0:T(8,128)(2,1)S(1)} collective-permute-done((bf16[512,768]{1,0:T(8,128)(2,1)S(1)}, bf16[512,768]{1,0:T(8,128)(2,1)S(1)}, u32[]{:S(2)}, u32[]{:S(2)}) %collective-permute-start.70) | collective-permute-done | bytes 786464 | tf_op jit(solution)/shard_map/ppermute | solution.py:37
  554.3 9.5 %collective-permute-done.77 = bf16[512,512]{1,0:T(8,128)(2,1)S(1)} collective-permute-done((bf16[512,512]{1,0:T(8,128)(2,1)S(1)}, bf16[512,512]{1,0:T(8,128)(2,1)S(1)}, u32[]{:S(2)}, u32[]{:S(2)}) %collective-permute-start.77) | collective-permute-done | bytes 524320 | tf_op jit(solution)/shard_map/ppermute | solution.py:33
  574.0 8.0 %collective-permute-done.80 = bf16[512,768]{1,0:T(8,128)(2,1)S(1)} collective-permute-done((bf16[512,768]{1,0:T(8,128)(2,1)S(1)}, bf16[512,768]{1,0:T(8,128)(2,1)S(1)}, u32[]{:S(2)}, u32[]{:S(2)}) %collective-permute-start.80) | collective-permute-done | bytes 786464 | tf_op jit(solution)/shard_map/ppermute | solution.py:33
  (483 shorter events, 285.5 us)
Async XLA Ops:
  52.3 46.1 %collective-permute-start.13 = (bf16[512,2048]{1,0:T(8,128)(2,1)}, bf16[512,2048]{1,0:T(8,128)(2,1)}, u32[]{:S(2)}, u32[]{:S(2)}) collective-permute-start(bf16[512,2048]{1,0:T(8,128)(2,1)} %param.23), channel_id=1, source_target_pairs={{0,16},{8,24},{16,0},{24,8},{1,17},{9,25},{17,1},{25,9},{2,18},{10... | collective-permute-start | bytes 6291464 | tf_op jit(solution)/shard_map/ppermute | solution.py:37
  53.6 36.5 %collective-permute-start.16 = (bf16[512,512]{1,0:T(8,128)(2,1)}, bf16[512,512]{1,0:T(8,128)(2,1)}, u32[]{:S(2)}, u32[]{:S(2)}) collective-permute-start(bf16[512,512]{1,0:T(8,128)(2,1)} %maximum_select_fusion.2), channel_id=1, source_target_pairs={{0,8},{8,0},{16,24},{24,16},{1,9},{9,1},{17,25},{25,17},{2,10},{10... | collective-permute-start | bytes 1572872 | tf_op jit(solution)/shard_map/ppermute | solution.py:37
  60.2 33.6 %collective-permute-start.17 = (bf16[512,512]{1,0:T(8,128)(2,1)}, bf16[512,512]{1,0:T(8,128)(2,1)}, u32[]{:S(2)}, u32[]{:S(2)}) collective-permute-start(bf16[512,512]{1,0:T(8,128)(2,1)} %collective-permute-done.5), channel_id=1, source_target_pairs={{0,8},{8,0},{16,24},{24,16},{1,9},{9,1},{17,25},{25,17},{2,10},{10... | collective-permute-start | bytes 1572872 | tf_op jit(solution)/shard_map/ppermute | solution.py:37
  60.8 34.2 %collective-permute-start.14 = (bf16[144,2048]{1,0:T(8,128)(2,1)}, bf16[144,2048]{1,0:T(8,128)(2,1)S(1)}, u32[]{:S(2)}, u32[]{:S(2)}) collective-permute-start(bf16[144,2048]{1,0:T(8,128)(2,1)} %get-tuple-element.230), channel_id=1, source_target_pairs={{0,1},{1,2},{2,3},{3,0},{4,5},{5,6},{6,7},{7,4},{8,9},{9,10},{10,1... | collective-permute-start | bytes 1769480 | tf_op jit(solution)/shard_map/ppermute | solution.py:29
  115.3 46.4 %collective-permute-start.22 = (bf16[512,2048]{1,0:T(8,128)(2,1)S(1)}, bf16[512,2048]{1,0:T(8,128)(2,1)S(1)}, u32[]{:S(2)}, u32[]{:S(2)}) collective-permute-start(bf16[512,2048]{1,0:T(8,128)(2,1)S(1)} %copy-done.21), channel_id=1, source_target_pairs={{0,16},{8,24},{16,0},{24,8},{1,17},{9,25},{17,1},{25,9},{2,18},{10... | collective-permute-start | bytes 6291464 | tf_op jit(solution)/shard_map/ppermute | solution.py:37
  127.4 34.3 %collective-permute-start.21 = (bf16[144,2048]{1,0:T(8,128)(2,1)S(1)}, bf16[144,2048]{1,0:T(8,128)(2,1)S(1)}, u32[]{:S(2)}, u32[]{:S(2)}) collective-permute-start(bf16[144,2048]{1,0:T(8,128)(2,1)S(1)} %pad_maximum_fusion.11), channel_id=1, source_target_pairs={{0,3},{1,0},{2,1},{3,2},{4,7},{5,4},{6,5},{7,6},{8,11},{9,8},{10,9... | collective-permute-start | bytes 1769480 | tf_op jit(solution)/shard_map/ppermute | solution.py:29
  130.8 36.0 %collective-permute-start.28 = (bf16[512,2048]{1,0:T(8,128)(2,1)}, bf16[512,2048]{1,0:T(8,128)(2,1)S(1)}, u32[]{:S(2)}, u32[]{:S(2)}) collective-permute-start(bf16[512,2048]{1,0:T(8,128)(2,1)} %param.23), channel_id=1, source_target_pairs={{0,8},{8,0},{16,24},{24,16},{1,9},{9,1},{17,25},{25,17},{2,10},{10... | collective-permute-start | bytes 6291464 | tf_op jit(solution)/shard_map/ppermute | solution.py:37
  130.8 36.7 %collective-permute-start.29 = (bf16[512,2048]{1,0:T(8,128)(2,1)}, bf16[512,2048]{1,0:T(8,128)(2,1)S(1)}, u32[]{:S(2)}, u32[]{:S(2)}) collective-permute-start(bf16[512,2048]{1,0:T(8,128)(2,1)} %collective-permute-done.13), channel_id=1, source_target_pairs={{0,8},{8,0},{16,24},{24,16},{1,9},{9,1},{17,25},{25,17},{2,10},{10... | collective-permute-start | bytes 6291464 | tf_op jit(solution)/shard_map/ppermute | solution.py:37
  166.3 50.1 %collective-permute-start.30 = (bf16[512,2048]{1,0:T(8,128)(2,1)S(1)}, bf16[512,2048]{1,0:T(8,128)(2,1)S(1)}, u32[]{:S(2)}, u32[]{:S(2)}) collective-permute-start(bf16[512,2048]{1,0:T(8,128)(2,1)S(1)} %copy-done.21), channel_id=1, source_target_pairs={{0,8},{8,0},{16,24},{24,16},{1,9},{9,1},{17,25},{25,17},{2,10},{10... | collective-permute-start | bytes 6291464 | tf_op jit(solution)/shard_map/ppermute | solution.py:37
  166.8 49.9 %collective-permute-start.31 = (bf16[512,2048]{1,0:T(8,128)(2,1)S(1)}, bf16[512,2048]{1,0:T(8,128)(2,1)S(1)}, u32[]{:S(2)}, u32[]{:S(2)}) collective-permute-start(bf16[512,2048]{1,0:T(8,128)(2,1)S(1)} %collective-permute-done.22), channel_id=1, source_target_pairs={{0,8},{8,0},{16,24},{24,16},{1,9},{9,1},{17,25},{25,17},{2,10},{10... | collective-permute-start | bytes 6291464 | tf_op jit(solution)/shard_map/ppermute | solution.py:37
  168.4 48.0 %collective-permute-start.23 = (bf16[512,2048]{1,0:T(8,128)(2,1)S(1)}, bf16[512,2048]{1,0:T(8,128)(2,1)S(1)}, u32[]{:S(2)}, u32[]{:S(2)}) collective-permute-start(bf16[512,2048]{1,0:T(8,128)(2,1)S(1)} %copy-done.22), channel_id=1, source_target_pairs={{0,16},{8,24},{16,0},{24,8},{1,17},{9,25},{17,1},{25,9},{2,18},{10... | collective-permute-start | bytes 6291464 | tf_op jit(solution)/shard_map/ppermute | solution.py:37
  304.8 46.5 %collective-permute-start.45 = (bf16[256,2048]{1,0:T(8,128)(2,1)S(1)}, bf16[256,2048]{1,0:T(8,128)(2,1)S(1)}, u32[]{:S(2)}, u32[]{:S(2)}) collective-permute-start(bf16[256,2048]{1,0:T(8,128)(2,1)S(1)} %get-tuple-element.422), channel_id=1, source_target_pairs={{0,16},{8,24},{16,0},{24,8},{1,17},{9,25},{17,1},{25,9},{2,18},{10... | collective-permute-start | bytes 3145736 | tf_op jit(solution)/shard_map/ppermute | solution.py:37
  329.7 96.8 %collective-permute-start.48 = (bf16[256,2048]{1,0:T(8,128)(2,1)S(1)}, bf16[256,2048]{1,0:T(8,128)(2,1)S(1)}, u32[]{:S(2)}, u32[]{:S(2)}) collective-permute-start(bf16[256,2048]{1,0:T(8,128)(2,1)S(1)} %add_convert_fusion.11), channel_id=1, source_target_pairs={{0,4},{4,0},{1,5},{5,1},{2,6},{6,2},{3,7},{7,3},{8,12},{12,8},{9,1... | collective-permute-start | bytes 3145736 | tf_op jit(solution)/shard_map/ppermute | solution.py:33
  348.0 50.8 %collective-permute-start.54 = (bf16[1024,2048]{1,0:T(8,128)(2,1)S(1)}, bf16[1024,2048]{1,0:T(8,128)(2,1)S(1)}, u32[]{:S(2)}, u32[]{:S(2)}) collective-permute-start(bf16[1024,2048]{1,0:T(8,128)(2,1)S(1)} %convolution_convert_fusion), channel_id=1, source_target_pairs={{0,8},{8,0},{16,24},{24,16},{1,9},{9,1},{17,25},{25,17},{2,10},{10... | collective-permute-start | bytes 12582920 | tf_op jit(solution)/shard_map/ppermute | solution.py:37
  382.4 34.9 %collective-permute-start.52 = (bf16[256,2048]{1,0:T(8,128)(2,1)S(1)}, bf16[256,2048]{1,0:T(8,128)(2,1)S(1)}, u32[]{:S(2)}, u32[]{:S(2)}) collective-permute-start(bf16[256,2048]{1,0:T(8,128)(2,1)S(1)} %get-tuple-element.420), channel_id=1, source_target_pairs={{0,16},{8,24},{16,0},{24,8},{1,17},{9,25},{17,1},{25,9},{2,18},{10... | collective-permute-start | bytes 3145736 | tf_op jit(solution)/shard_map/ppermute | solution.py:37
  383.9 46.9 %collective-permute-start.49 = (bf16[256,2048]{1,0:T(8,128)(2,1)S(1)}, bf16[256,2048]{1,0:T(8,128)(2,1)S(1)}, u32[]{:S(2)}, u32[]{:S(2)}) collective-permute-start(bf16[256,2048]{1,0:T(8,128)(2,1)S(1)} %add_convert_fusion.10), channel_id=1, source_target_pairs={{0,4},{4,0},{1,5},{5,1},{2,6},{6,2},{3,7},{7,3},{8,12},{12,8},{9,1... | collective-permute-start | bytes 3145736 | tf_op jit(solution)/shard_map/ppermute | solution.py:33
  417.3 43.9 %collective-permute-start.51 = (bf16[256,2048]{1,0:T(8,128)(2,1)}, bf16[256,2048]{1,0:T(8,128)(2,1)}, u32[]{:S(2)}, u32[]{:S(2)}) collective-permute-start(bf16[256,2048]{1,0:T(8,128)(2,1)} %add_convert_fusion.9), channel_id=1, source_target_pairs={{0,4},{4,0},{1,5},{5,1},{2,6},{6,2},{3,7},{7,3},{8,12},{12,8},{9,1... | collective-permute-start | bytes 3145736 | tf_op jit(solution)/shard_map/ppermute | solution.py:33
  423.6 39.2 %collective-permute-start.60 = (bf16[256,2048]{1,0:T(8,128)(2,1)}, bf16[256,2048]{1,0:T(8,128)(2,1)}, u32[]{:S(2)}, u32[]{:S(2)}) collective-permute-start(bf16[256,2048]{1,0:T(8,128)(2,1)} %get-tuple-element.418), channel_id=1, source_target_pairs={{0,16},{8,24},{16,0},{24,8},{1,17},{9,25},{17,1},{25,9},{2,18},{10... | collective-permute-start | bytes 3145736 | tf_op jit(solution)/shard_map/ppermute | solution.py:37
  424.2 39.4 %collective-permute-start.55 = (bf16[256,2048]{1,0:T(8,128)(2,1)}, bf16[256,2048]{1,0:T(8,128)(2,1)}, u32[]{:S(2)}, u32[]{:S(2)}) collective-permute-start(bf16[256,2048]{1,0:T(8,128)(2,1)} %add_convert_fusion.8), channel_id=1, source_target_pairs={{0,4},{4,0},{1,5},{5,1},{2,6},{6,2},{3,7},{7,3},{8,12},{12,8},{9,1... | collective-permute-start | bytes 3145736 | tf_op jit(solution)/shard_map/ppermute | solution.py:33
  426.5 36.3 %collective-permute-start.59 = (bf16[144,2048]{1,0:T(8,128)(2,1)}, bf16[144,2048]{1,0:T(8,128)(2,1)}, u32[]{:S(2)}, u32[]{:S(2)}) collective-permute-start(bf16[144,2048]{1,0:T(8,128)(2,1)} %pad_maximum_fusion.15), channel_id=1, source_target_pairs={{0,3},{1,0},{2,1},{3,2},{4,7},{5,4},{6,5},{7,6},{8,11},{9,8},{10,9... | collective-permute-start | bytes 1769480 | tf_op jit(solution)/shard_map/ppermute | solution.py:29
  461.2 52.9 %collective-permute-start.69 = (bf16[256,2048]{1,0:T(8,128)(2,1)}, bf16[256,2048]{1,0:T(8,128)(2,1)}, u32[]{:S(2)}, u32[]{:S(2)}) collective-permute-start(bf16[256,2048]{1,0:T(8,128)(2,1)} %get-tuple-element.417), channel_id=1, source_target_pairs={{0,16},{8,24},{16,0},{24,8},{1,17},{9,25},{17,1},{25,9},{2,18},{10... | collective-permute-start | bytes 3145736 | tf_op jit(solution)/shard_map/ppermute | solution.py:37
  467.8 85.4 %collective-permute-start.78 = (bf16[256,2048]{1,0:T(8,128)(2,1)S(1)}, bf16[256,2048]{1,0:T(8,128)(2,1)}, u32[]{:S(2)}, u32[]{:S(2)}) collective-permute-start(bf16[256,2048]{1,0:T(8,128)(2,1)S(1)} %add_convert_fusion.7), channel_id=1, source_target_pairs={{0,4},{4,0},{1,5},{5,1},{2,6},{6,2},{3,7},{7,3},{8,12},{12,8},{9,1... | collective-permute-start | bytes 3145736 | tf_op jit(solution)/shard_map/ppermute | solution.py:33
  510.9 42.3 %collective-permute-start.65 = (bf16[144,2048]{1,0:T(8,128)(2,1)S(1)}, bf16[144,2048]{1,0:T(8,128)(2,1)S(1)}, u32[]{:S(2)}, u32[]{:S(2)}) collective-permute-start(bf16[144,2048]{1,0:T(8,128)(2,1)S(1)} %pad_maximum_fusion.17), channel_id=1, source_target_pairs={{0,3},{1,0},{2,1},{3,2},{4,7},{5,4},{6,5},{7,6},{8,11},{9,8},{10,9... | collective-permute-start | bytes 1769480 | tf_op jit(solution)/shard_map/ppermute | solution.py:29
  513.0 40.3 %collective-permute-start.64 = (bf16[144,2048]{1,0:T(8,128)(2,1)S(1)}, bf16[144,2048]{1,0:T(8,128)(2,1)S(1)}, u32[]{:S(2)}, u32[]{:S(2)}) collective-permute-start(bf16[144,2048]{1,0:T(8,128)(2,1)S(1)} %pad_maximum_fusion.16), channel_id=1, source_target_pairs={{0,1},{1,2},{2,3},{3,0},{4,5},{5,6},{6,7},{7,4},{8,9},{9,10},{10,1... | collective-permute-start | bytes 1769480 | tf_op jit(solution)/shard_map/ppermute | solution.py:29
  (129 other events, 1731.6 us)
